TPU v7x, 32 devices: a whole 2x2x4 slice. The times are simulated.
32 devices in a mesh: dp: 2 (over x), tensor: 16 (over z, y, core).
Axes of the slice: x: 2, y: 2, z: 4, core: 2. Of those that a mesh axis runs over, the one named last changes fastest.
Arguments:
- tokens: bfloat16 [8192, 1536], P(('dp', 'tensor')), may hold values from -6 to 6
- lengths: int32 [2], P('dp'), may hold values from 256 to 4096
- routes: int32 [8192, 8], P(('dp', 'tensor')), may hold values from 0 to 15, all different within a row; in each aligned block of 256 rows (0 to 255, 256 to 511, ...) at most 160 rows name the same one
- norm_gain: float32 [1536], replicated, may hold values from 0.1 to 1.9
- router: bfloat16 [1536, 16], replicated, may hold values from -0.15625 to 0.15625
- w_gate: bfloat16 [16, 1536, 512], P('tensor', 'dp'), may hold values from -0.15625 to 0.15625
- w_up: bfloat16 [16, 1536, 512], P('tensor', 'dp'), may hold values from -0.15625 to 0.15625
- w_down: bfloat16 [16, 512, 1536], P('tensor', None, 'dp'), may hold values from -0.25 to 0.25
Outputs:
- mixed: bfloat16 [8192, 1536], P(('dp', 'tensor'))
Inputs may be any that keep to these rules, and one draw needn't show every extreme that they name: `routes`: each row names 8 different experts; among the 256 rows of one device (aligned blocks) no expert is named more than 160 times, and in some device one expert is named exactly 160 times.
All inputs are finite; a program needn't handle non-finite values.
Results may differ from a plain program's by a relative error of at most 0.0048.
Values may be sent and summed in bfloat16 or wider, within the bound.
No kernel may reach another device: no remote copies, remote signals or barrier semaphores. Data moves between devices by JAX's collectives and lax.ppermute only.
A program may use at most 64 MiB of HBM per device.

v0:
```python
import jax
import jax.numpy as jnp
from jax import lax
from jax.sharding import PartitionSpec as P

LMAX = 4096


def shards(tokens, lengths, routes, norm_gain, router, w_gate, w_up, w_down):
    row_count = tokens.shape[0]
    width = tokens.shape[1]
    experts = router.shape[1]
    local_experts = w_gate.shape[0]
    n_tensor = lax.axis_size("tensor")
    top_count = routes.shape[1]
    slot_total = min(row_count, row_count * top_count * 5 // (4 * experts))
    tokens_f32 = tokens.astype(jnp.float32)
    scale_rows = lax.rsqrt(jnp.mean(tokens_f32 * tokens_f32, axis=-1, keepdims=True) + 1e-06)
    normed = (tokens_f32 * scale_rows * norm_gain).astype(jnp.bfloat16)
    logits = jnp.dot(normed, router, preferred_element_type=jnp.float32)
    position = lax.axis_index("tensor") * row_count + jnp.arange(row_count, dtype=jnp.int32)
    living = position % LMAX < lengths[position // LMAX]
    gate_weights = jax.nn.sigmoid(jnp.take_along_axis(logits, routes, axis=1)) * living[
        :, None
    ].astype(jnp.float32)
    expert_index = routes.reshape(row_count * top_count)
    pair_living = jnp.repeat(living, top_count)
    pair_hits = (
        (expert_index[:, None] == jnp.arange(experts, dtype=jnp.int32)[None, :])
        & pair_living[:, None]
    ).astype(jnp.int32)
    slot_rank = jnp.cumsum(pair_hits, axis=0) - pair_hits
    slot_index = jnp.sum(slot_rank * pair_hits, axis=1)
    slot_index = jnp.where(pair_living, slot_index, slot_total)
    pair_rows = jnp.repeat(normed, top_count, axis=0)
    buffer = jnp.zeros((experts, slot_total, width), jnp.bfloat16)
    buffer = buffer.at[expert_index, slot_index].set(pair_rows, mode="drop")
    gate_all, up_all = (
        lax.all_gather(w_gate, "dp", axis=1, tiled=True),
        lax.all_gather(w_up, "dp", axis=1, tiled=True),
    )
    down_all = lax.all_gather(w_down, "dp", axis=2, tiled=True)
    received = lax.all_to_all(buffer, "tensor", split_axis=0, concat_axis=0, tiled=True)
    slot_count = received.shape[1]
    grouped = received.reshape(n_tensor, local_experts, slot_count, width)
    gate_proj = jnp.einsum("sxcd,xdh->sxch", grouped, gate_all, preferred_element_type=jnp.float32)
    up_proj = jnp.einsum("sxcd,xdh->sxch", grouped, up_all, preferred_element_type=jnp.float32)
    hidden = (jax.nn.silu(gate_proj) * up_proj).astype(jnp.bfloat16)
    result = jnp.einsum(
        "sxch,xhd->sxcd", hidden, down_all, preferred_element_type=jnp.float32
    ).astype(jnp.bfloat16)
    outputs = result.reshape(n_tensor * local_experts, slot_count, width)
    returned = lax.all_to_all(outputs, "tensor", split_axis=0, concat_axis=0, tiled=True)
    picked = returned[expert_index, jnp.minimum(slot_index, slot_total - 1)]
    picked = picked.reshape(row_count, top_count, width)
    combined = jnp.sum(gate_weights[:, :, None] * picked.astype(jnp.float32), axis=1)
    return (tokens_f32 + combined).astype(jnp.bfloat16)


def solution(mesh):
    placed = (
        P(("dp", "tensor"), None),
        P("dp"),
        P(("dp", "tensor"), None),
        P(),
        P(),
        P("tensor", "dp", None),
        P("tensor", "dp", None),
        P("tensor", None, "dp"),
    )
    return jax.shard_map(
        shards, mesh=mesh, in_specs=placed, out_specs=P(("dp", "tensor"), None), check_vma=False
    )
```

profile of v0, /device:TPU:29, one launch (start us, length us, event | category | flops | bytes accessed | tf_op | source)
XLA Modules:
  0.0 477.4 jit_solution(10666003150021628220)
XLA Ops:
  6.5 0.0 copy-start
  7.2 0.1 broadcast_in_dim.33
  7.3 0.1 and.44
  7.4 0.1 reshape.183
  7.6 0.8 copy.22
  8.4 0.1 eq.31
  8.5 0.1 eq.27
  8.6 0.1 reshape.182
  8.7 1.4 fusion.10
  10.2 0.1 copy.25
  10.3 4.5 reduce-window.6
  14.8 0.4 slice_reduce_fusion
  15.3 0.2 reduce-window.9
  15.4 0.1 broadcast_add_fusion
  15.5 0.1 fusion.24
  15.6 0.1 fusion.32
  15.7 0.8 and_reduce_fusion
  16.4 0.7 multiply_reduce_fusion
  17.2 1.4 fusion.12
  18.6 14.7 %scatter_custom_fusion = bf16[2560,1536]{1,0:T(8,128)(2,1)} fusion(s32[2048]{0:T(1024)S(1)} %broadcast_select_fusion, bf16[]{:T(256)} %constant.71.clone.1, bf16[256,1536]{1,0:T(8,128)(2,1)S(1)} %fusion.12), kind=kCustom, calls=%fused_computation.5 | custom fusion | bytes 8650754
  33.3 6.3 %all-to-all-start = ((bf16[16,160,1536]{2,1,0:T(8,128)(2,1)}), bf16[16,160,1536]{2,1,0:T(8,128)(2,1)}, u32[]{:S(2)}, u32[]{:S(2)}) async-start(bf16[16,160,1536]{2,1,0:T(8,128)(2,1)} %bitcast.94), calls=%async_computation | async-start | bytes 15728640 | tf_op jit(solution)/shard_map/all_to_all | solution.py:43
  39.6 0.0 all-gather.6.cloned.1.call-start
  39.6 0.7 all-gather.6.cloned.1.call-update
  40.3 0.0 all-gather.4.cloned.1.call-start
  40.4 0.7 all-gather.4.cloned.1.call-update
  41.1 0.2 all-gather.8.cloned.1.call-start
  41.3 0.5 all-gather.8.cloned.1.call-update
  41.8 28.0 %all-gather.6.cloned.1.call-done = bf16[1,1536,512]{2,1,0:T(8,128)(2,1)} async-done(((bf16[1,768,512]{2,1,0:T(8,128)(2,1)}), bf16[1,1536,512]{2,1,0:T(8,128)(2,1)}) %all-gather.6.cloned.1.call-update) | async-done | bytes 1572880 | tf_op jit(solution)/shard_map/all_gather | solution.py:40
  69.8 139.9 %all-to-all-done = bf16[16,160,1536]{2,1,0:T(8,128)(2,1)} async-done(((bf16[16,160,1536]{2,1,0:T(8,128)(2,1)}), bf16[16,160,1536]{2,1,0:T(8,128)(2,1)}, u32[]{:S(2)}, u32[]{:S(2)}) %all-to-all-start) | async-done | bytes 7864352 | tf_op jit(solution)/shard_map/all_to_all | solution.py:43
  209.8 10.1 %fusion.15 = f32[16,160,512]{2,1,0:T(8,128)} fusion(bf16[16,160,1536]{2,1,0:T(8,128)(2,1)} %all-to-all-done, bf16[1,1536,512]{2,1,0:T(8,128)(2,1)} %all-gather.6.cloned.1.call-done), kind=kOutput, calls=%fused_computation.26 | convolution fusion | flops 4026531840 | bytes 14680064 | tf_op jit(solution)/shard_map/sxcd,xdh->sxch/dot_general | solution.py:47
  219.9 0.0 all-gather.4.cloned.1.call-done
  219.9 0.0 all-gather.8.cloned.1.call-done
  219.9 14.7 %convolution_convert_fusion = bf16[16,160,1536]{2,1,0:T(8,128)(2,1)} fusion(bf16[1,512,1536]{2,1,0:T(8,128)(2,1)} %all-gather.8.cloned.1.call-done, f32[16,160,512]{2,1,0:T(8,128)} %fusion.15, bf16[16,160,1536]{2,1,0:T(8,128)(2,1)} %all-to-all-done, bf16[1,1536,512]{2,1,0:T(8,128)(2,1)} %all-gather.4.cloned.1.call-done), kind=kOutput, calls=%fused_computation.7 | convolution fusion | flops 8064860160 | bytes 24117248 | tf_op jit(solution)/shard_map/sxch,xhd->sxcd/dot_general | solution.py:49
  234.6 6.0 %all-to-all-start.1 = ((bf16[16,160,1536]{2,1,0:T(8,128)(2,1)}), bf16[16,160,1536]{2,1,0:T(8,128)(2,1)}, u32[]{:S(2)}, u32[]{:S(2)}) async-start(bf16[16,160,1536]{2,1,0:T(8,128)(2,1)} %convolution_convert_fusion), calls=%async_computation.1 | async-start | bytes 15728640 | tf_op jit(solution)/shard_map/all_to_all | solution.py:53
  240.6 0.0 copy-done.2
  240.6 0.1 copy.19
  240.8 0.1 reshape.201
  240.9 0.0 copy-done
  240.9 0.3 fusion.38
  241.2 16.8 %gather_fusion.1 = f32[2048]{0:T(1024)S(1)} fusion(f32[256,16]{0,1:T(8,128)S(1)} %fusion.38, s32[2048]{0:T(1024)S(1)} %reshape.201), kind=kCustom, calls=%fused_computation.1 | custom fusion | bytes 32768 | tf_op jit(solution)/shard_map/jit(take_along_axis)/gather | solution.py:23
  258.0 0.1 reshape.204
  258.1 0.1 copy.20
  258.2 0.1 copy.21
  258.3 152.4 %all-to-all-done.1 = bf16[16,160,1536]{2,1,0:T(8,128)(2,1)} async-done(((bf16[16,160,1536]{2,1,0:T(8,128)(2,1)}), bf16[16,160,1536]{2,1,0:T(8,128)(2,1)}, u32[]{:S(2)}, u32[]{:S(2)}) %all-to-all-start.1) | async-done | bytes 7864352 | tf_op jit(solution)/shard_map/all_to_all | solution.py:53
  410.8 50.1 %gather_fusion = bf16[2048,1536]{1,0:T(8,128)(2,1)} fusion(bf16[16,160,1536]{2,1,0:T(8,128)(2,1)} %all-to-all-done.1, s32[2048]{0:T(1024)S(1)} %bitcast.93), kind=kCustom, calls=%fused_computation | custom fusion | bytes 12599296 | tf_op jit(solution)/shard_map/gather | solution.py:54
  460.9 8.9 %fusion = f32[256,1536]{1,0:T(8,128)S(1)} fusion(bf16[2048,1536]{1,0:T(8,128)(2,1)} %gather_fusion, f32[256,8]{1,0:T(8,128)S(1)} %copy.21), kind=kLoop, calls=%fused_computation.4 | loop fusion | flops 9043968 | bytes 7872512 | tf_op jit(solution)/shard_map/reduce_sum | solution.py:56
  469.8 0.0 copy-done.1
  469.8 1.1 fusion.13
  (10 shorter events, 0.1 us)
Async XLA Ops:
  6.5 234.4 %copy-start = (bf16[1536,16]{0,1:T(8,128)(2,1)S(1)}, bf16[1536,16]{0,1:T(8,128)(2,1)}, u32[]{:S(2)}) copy-start(bf16[1536,16]{0,1:T(8,128)(2,1)} %param.12) | copy-start | bytes 147460
  33.3 176.5 %all-to-all-start = ((bf16[16,160,1536]{2,1,0:T(8,128)(2,1)}), bf16[16,160,1536]{2,1,0:T(8,128)(2,1)}, u32[]{:S(2)}, u32[]{:S(2)}) async-start(bf16[16,160,1536]{2,1,0:T(8,128)(2,1)} %bitcast.94), calls=%async_computation | async-start | bytes 15728640 | tf_op jit(solution)/shard_map/all_to_all | solution.py:43
  39.6 30.2 %all-gather.6.cloned.1.call-start = ((), (), s32[]{:S(2)}) async-start(), calls=%async_computation.3 | async-start | bytes 2359296 | tf_op jit(solution)/shard_map/all_gather | solution.py:40
  40.3 179.6 %all-gather.4.cloned.1.call-start = ((), (), s32[]{:S(2)}) async-start(), calls=%async_computation.2 | async-start | bytes 2359296 | tf_op jit(solution)/shard_map/all_gather | solution.py:39
  41.1 178.8 %all-gather.8.cloned.1.call-start = ((), (), s32[]{:S(2)}) async-start(), calls=%async_computation.4 | async-start | bytes 2359296 | tf_op jit(solution)/shard_map/all_gather | solution.py:42
  234.6 6.0 %copy-start.2 = (s32[256,8]{0,1:T(8,128)S(1)}, s32[256,8]{0,1:T(8,128)}, u32[]{:S(2)}) copy-start(s32[256,8]{0,1:T(8,128)} %param.10) | copy-start | bytes 24580
  234.6 176.2 %all-to-all-start.1 = ((bf16[16,160,1536]{2,1,0:T(8,128)(2,1)}), bf16[16,160,1536]{2,1,0:T(8,128)(2,1)}, u32[]{:S(2)}, u32[]{:S(2)}) async-start(bf16[16,160,1536]{2,1,0:T(8,128)(2,1)} %convolution_convert_fusion), calls=%async_computation.1 | async-start | bytes 15728640 | tf_op jit(solution)/shard_map/all_to_all | solution.py:53
  460.9 8.9 %copy-start.1 = (bf16[256,1536]{1,0:T(8,128)(2,1)S(1)}, bf16[256,1536]{1,0:T(8,128)(2,1)}, u32[]{:S(2)}) copy-start(bf16[256,1536]{1,0:T(8,128)(2,1)} %param.8) | copy-start | bytes 2359300
Sparse Core Ops, SparseCore 0:
  42.0 27.8 all-gather.5
  71.4 27.2 all-gather.3
  100.2 27.1 all-gather.7
where the time goes:
time: 479 us; the launch traced here: 477 us
  waiting for transfers between devices  322 us (67%)
  local copies, waits for them, and re-layouts  84.1 us (18%)
  matrix products  25.1 us (5%)
  other arithmetic  19.3 us (4%)
  between operations  14 us (3%)
  starting transfers between devices  12.6 us (3%)
    all_to_all x1, waiting for transfers between devices, shards(): lax.all_to_all(outputs, 'tensor', split_axis=0, concat_axis=0, tiled=True)  152 us
    all_to_all x1, waiting for transfers between devices, shards(): lax.all_to_all(buffer, 'tensor', split_axis=0, concat_axis=0, tiled=True)  140 us
    gather x1, local copies, waits for them, and re-layouts, shards(): picked = returned[expert_index, jnp.minimum(slot_index, slot_total - 1)]  50.1 us
    all_gather x1, waiting for transfers between devices, shards(): lax.all_gather(w_up, 'dp', axis=1, tiled=True)  28 us
    gather x5, local copies, waits for them, and re-layouts, shards(): jnp.take_along_axis(logits, routes, axis=1)  17.2 us
    unnamed x8, local copies, waits for them, and re-layouts  15.5 us
    dot_general x1, matrix products, shards(): jnp.einsum('sxch,xhd->sxcd', hidden, down_all, preferred_element_type=jnp...  14.7 us
    dot_general x1, matrix products, shards(): jnp.einsum('sxcd,xdh->sxch', grouped, up_all, preferred_element_type=jnp....  10.1 us
  transfers between devices with their start and end apart: 5, of which 3 were waited for; matrix products, arithmetic and copies ran while one was open for 6% of the time, Pallas kernels for 0%

commit v1 on v0

v1 whole, which is shorter than its diff:
```python
import jax
import jax.numpy as jnp
from jax import lax
from jax.sharding import PartitionSpec as P

LMAX = 4096
F32 = jnp.float32
BF16 = jnp.bfloat16


def gate_of(logits, routes, lengths, experts):
    rows = logits.shape[0]
    position = lax.axis_index("tensor") * rows + jnp.arange(rows, dtype=jnp.int32)
    living = position % LMAX < lengths[position // LMAX]
    ids = jnp.arange(experts, dtype=jnp.int32)
    named = jnp.zeros((rows, experts), jnp.bool_)
    for k in range(routes.shape[1]):
        named = named | (routes[:, k : k + 1] == ids[None, :])
    return jnp.where(named & living[:, None], jax.nn.sigmoid(logits), 0.0)


def norm_of(tokens_f32, norm_gain):
    scale_rows = lax.rsqrt(jnp.mean(tokens_f32 * tokens_f32, axis=-1, keepdims=True) + 1e-06)
    return (tokens_f32 * scale_rows * norm_gain).astype(BF16)


def dot(a, b):
    return jnp.dot(a, b, preferred_element_type=F32)


def general(tokens, lengths, routes, norm_gain, router, w_gate, w_up, w_down):
    experts = router.shape[1]
    local = w_gate.shape[0]
    tokens_f32 = tokens.astype(F32)
    normed = norm_of(tokens_f32, norm_gain)
    gates = gate_of(dot(normed, router), routes, lengths, experts)
    gate_all = lax.all_gather(w_gate, "dp", axis=1, tiled=True)
    up_all = lax.all_gather(w_up, "dp", axis=1, tiled=True)
    down_all = lax.all_gather(w_down, "dp", axis=2, tiled=True)
    rows_all = lax.all_gather(normed, "tensor", axis=0, tiled=True)
    gates_all = lax.all_gather(gates, "tensor", axis=0, tiled=True)
    first = lax.axis_index("tensor") * local
    total = jnp.zeros(rows_all.shape, F32)
    for x in range(local):
        weight = lax.dynamic_slice_in_dim(gates_all, first + x, 1, axis=1)
        hidden = jax.nn.silu(dot(rows_all, gate_all[x])) * dot(rows_all, up_all[x])
        total = total + dot((hidden * weight).astype(BF16), down_all[x])
    combined = lax.psum_scatter(total.astype(BF16), "tensor", scatter_dimension=0, tiled=True)
    return (tokens_f32 + combined.astype(F32)).astype(BF16)


def lanes(tokens, lengths, routes, norm_gain, router, w_gate, w_up, w_down):
    experts = router.shape[1]
    width = tokens.shape[1]
    half = width // 2
    rows = tokens.shape[0]
    x = lax.axis_index("dp")
    t = lax.axis_index("tensor")
    z, y, c = t // 4, (t // 2) % 2, t % 2
    middle = (z == 1) | (z == 2)

    def swap(v):
        return jnp.where(x == 0, v, jnp.concatenate([v[:, half:], v[:, :half]], axis=1))

    def over(axis_pairs):
        return [(a * 4 + r, b * 4 + r) for a, b in axis_pairs for r in range(4)]

    def send(v, pairs):
        return lax.ppermute(v, "tensor", pairs)

    by_core = [(i, i ^ 1) for i in range(16)]
    by_y = [(i, i ^ 2) for i in range(16)]
    outer = over([(0, 1), (1, 0), (2, 3), (3, 2)])
    inner = over([(1, 2), (2, 1)])
    outward = over([(1, 0), (2, 3)])
    inward = over([(0, 1), (3, 2)])

    tokens_f32 = tokens.astype(F32)
    normed = norm_of(tokens_f32, norm_gain)
    gates = gate_of(dot(normed, router), routes, lengths, experts)
    gates_all = lax.all_gather(gates.T, "tensor", axis=0)

    in_own = jnp.concatenate([w_gate[0], w_up[0]], axis=1)
    down_own = w_down[0]
    in_far = lax.ppermute(in_own, "dp", [(0, 1), (1, 0)])
    down_far = lax.ppermute(down_own, "dp", [(0, 1), (1, 0)])
    in_parts = [[in_own, in_far], [send(in_own, by_core), send(in_far, by_core)]]
    down_parts = [[down_own, down_far], [send(down_own, by_core), send(down_far, by_core)]]
    hid = w_gate.shape[2]
    gate_w = jnp.concatenate([jnp.concatenate([p[:, :hid] for p in e], axis=0) for e in in_parts], axis=1)
    up_w = jnp.concatenate([jnp.concatenate([p[:, hid:] for p in e], axis=0) for e in in_parts], axis=1)
    down_w = jnp.concatenate([jnp.concatenate(e, axis=1) for e in down_parts], axis=0)

    s_0 = swap(normed)
    t_0 = send(s_0, by_y)
    s_a = send(s_0, outer)
    s_m = send(s_0, inner)
    t_a = send(s_a, by_y)
    s_b = jnp.where(middle, s_m, send(s_m, outward))
    s_n = send(s_a, inner)
    t_b = send(s_b, by_y)
    s_c = jnp.where(middle, s_n, send(s_n, outward))
    t_c = send(s_c, by_y)

    low = z < 2
    planes = [z, z ^ 1, jnp.where(low, 2, 1), jnp.where(low, 3, 0)]
    my_experts = gates_all.reshape(4, 2, 2, experts, rows)

    def weights_of(plane, side):
        own = lax.dynamic_slice(my_experts, (plane, side, c, 2 * (t // 2), 0), (1, 1, 1, 2, rows)).reshape(2, rows)
        own = jnp.where(c == 0, own, own[::-1])
        return own.T

    def partial(block, plane, side):
        w = weights_of(plane, side)
        w = jnp.repeat(w, hid, axis=1)
        hidden = jax.nn.silu(dot(block, gate_w)) * dot(block, up_w) * w
        return dot(hidden.astype(BF16), down_w).astype(BF16)

    def add(a, b):
        return (a.astype(F32) + b.astype(F32)).astype(BF16)

    q_c = add(partial(s_c, planes[3], y), send(partial(t_c, planes[3], 1 - y), by_y))
    q_b = add(partial(s_b, planes[2], y), send(partial(t_b, planes[2], 1 - y), by_y))
    q_a = add(partial(s_a, planes[1], y), send(partial(t_a, planes[1], 1 - y), by_y))
    r_0 = send(partial(t_0, planes[0], 1 - y), by_y)
    q_n = add(q_c, send(q_c, inward))
    q_a = add(q_a, send(q_n, inner))
    q_m = add(q_b, send(q_b, inward))
    r_m = send(q_m, inner)
    r_a = send(q_a, outer)
    p_0 = partial(s_0, planes[0], y)
    combined = p_0.astype(F32) + r_0.astype(F32) + r_m.astype(F32) + r_a.astype(F32)
    return (tokens_f32 + swap(combined)).astype(BF16)


def solution(mesh):
    placed = (
        P(("dp", "tensor"), None),
        P("dp"),
        P(("dp", "tensor"), None),
        P(),
        P(),
        P("tensor", "dp", None),
        P("tensor", "dp", None),
        P("tensor", None, "dp"),
    )

    def shards(*args):
        fits = mesh.shape["dp"] == 2 and mesh.shape["tensor"] == 16 and args[5].shape[0] == 1
        return (lanes if fits else general)(*args)

    return jax.shard_map(
        shards, mesh=mesh, in_specs=placed, out_specs=P(("dp", "tensor"), None), check_vma=False
    )
```

time: 479 us -> 267 us (0.56)
  the two profiles are of different devices: /device:TPU:29 before, /device:TPU:0 now
where the time goes in v1:
time: 267 us
  matrix products  78.4 us (29%)
  waiting for transfers between devices  78 us (29%)
  blocking collectives  30.9 us (12%)
  starting transfers between devices  28.1 us (11%)
  local copies, waits for them, and re-layouts  26 us (10%)
  other arithmetic  24.2 us (9%)
    dot_general x17, matrix products, dot(): return jnp.dot(a, b, preferred_element_type=F32)  78.4 us
    ppermute x22, waiting for transfers between devices, send(): return lax.ppermute(v, 'tensor', pairs)  78 us
    all_gather x1, blocking collectives, lanes(): gates_all = lax.all_gather(gates.T, 'tensor', axis=0)  30.9 us
    ppermute x22, starting transfers between devices, send(): return lax.ppermute(v, 'tensor', pairs)  24.6 us
    concatenate x1, other arithmetic, lanes(): jnp.concatenate([jnp.concatenate([p[:, :hid] for p in e], axis=0) for e i...  12.7 us
    unnamed x54, local copies, waits for them, and re-layouts  11.5 us
    broadcast_in_dim x8, local copies, waits for them, and re-layouts, partial(): w = jnp.repeat(w, hid, axis=1)  5.4 us
  transfers between devices with their start and end apart: 24, of which 8 were waited for; matrix products, arithmetic and copies ran while one was open for 43% of the time, Pallas kernels for 0%

profile of v1, /device:TPU:0, one launch (start us, length us, event | category | flops | bytes accessed | tf_op | source)
XLA Modules:
  0.0 266.8 jit_solution(11737837544929951845)
XLA Ops:
  0.0 2.8 %pad_maximum_fusion = bf16[768,1024]{1,0:T(8,128)(2,1)} fusion(bf16[768,512]{1,0:T(8,128)(2,1)} %bitcast.118, bf16[768,512]{1,0:T(8,128)(2,1)} %bitcast.108), kind=kLoop, calls=%fused_computation.34 | loop fusion | flops 3145728 | bytes 3145728 | tf_op jit(solution)/shard_map/concatenate | solution.py:83
  2.8 2.9 %collective-permute-start = (bf16[768,1024]{1,0:T(8,128)(2,1)}, bf16[768,1024]{1,0:T(8,128)(2,1)S(1)}, u32[]{:S(2)}, u32[]{:S(2)}) collective-permute-start(bf16[768,1024]{1,0:T(8,128)(2,1)} %pad_maximum_fusion), channel_id=1, source_target_pairs={{0,16},{16,0},{1,17},{17,1},{2,18},{18,2},{3,19},{19,3},{4,20},{20... | collective-permute-start | bytes 4718600 | tf_op jit(solution)/shard_map/ppermute | solution.py:85
  7.2 2.3 maximum_select_fusion.1
  9.6 1.6 collective-permute-start.14
  11.1 1.5 collective-permute-start.8
  14.3 30.9 %all-gather = f32[256,256]{1,0:T(8,128)S(1)} all-gather(f32[16,256]{1,0:T(8,128)S(1)} %fusion.24), channel_id=2, replica_groups=mesh['dp'=2,'tensor'=16] {'tensor'}, dimensions={0}, use_global_device_ids=true | all-gather | bytes 278528 | tf_op jit(solution)/shard_map/all_gather | solution.py:81
  45.4 1.6 collective-permute-start.17
  47.1 1.3 collective-permute-start.9
  49.1 1.2 copy.24
  55.1 1.2 broadcast_in_dim.44
  58.3 1.2 broadcast_in_dim.43
  61.7 1.2 broadcast_in_dim.42
  63.0 1.2 copy.18
  64.1 1.6 collective-permute-start.18
  67.2 2.0 collective-permute-done.9
  69.1 2.1 broadcast_select_fusion.1
  71.2 15.7 %collective-permute-done.18 = bf16[256,1536]{1,0:T(8,128)(2,1)S(1)} collective-permute-done((bf16[256,1536]{1,0:T(8,128)(2,1)}, bf16[256,1536]{1,0:T(8,128)(2,1)S(1)}, u32[]{:S(2)}, u32[]{:S(2)}) %collective-permute-start.18) | collective-permute-done | bytes 786464 | tf_op jit(solution)/shard_map/ppermute | solution.py:69
  89.2 2.3 fusion.55
  93.5 12.7 %maximum_maximum_fusion = bf16[1536,1024]{1,0:T(8,128)(2,1)S(1)} fusion(bf16[768,512]{1,0:T(8,128)(2,1)S(1)} %get-tuple-element.11, bf16[768,512]{1,0:T(8,128)(2,1)S(1)} %get-tuple-element.9, bf16[768,512]{1,0:T(8,128)(2,1)S(1)} %get-tuple-element.7, bf16[768,512]{1,0:T(8,128)(2,1)S(1)} %bitcast.109), kind=kLoop, calls=%fused_computation | loop fusion | flops 12582912 | bytes 6291456 | tf_op jit(solution)/shard_map/concatenate | solution.py:90
  106.2 18.3 %collective-permute-done.19 = bf16[256,1536]{1,0:T(8,128)(2,1)S(1)} collective-permute-done((bf16[256,1536]{1,0:T(8,128)(2,1)S(1)}, bf16[256,1536]{1,0:T(8,128)(2,1)S(1)}, u32[]{:S(2)}, u32[]{:S(2)}) %collective-permute-start.19) | collective-permute-done | bytes 786464 | tf_op jit(solution)/shard_map/ppermute | solution.py:69
  125.5 2.0 fusion.80
  129.3 6.1 %convolution_convert_fusion = bf16[256,1536]{1,0:T(8,128)(2,1)} fusion(f32[256,1024]{1,0:T(8,128)S(1)} %bitcast.113, f32[256,1024]{1,0:T(8,128)} %fusion.80, bf16[512,768]{1,0:T(8,128)(2,1)} %copy-done.20, bf16[512,768]{1,0:T(8,128)(2,1)} %copy-done.19, bf16[512,768]{1,0:T(8,128)(2,1)} %collective-permute-done.3, bf16[512,768]{1,0:T(8,128)(2,1)} %bitcast.137, ...), kind=kOutput, calls=%fused_computation.3 | convolution fusion | flops 1638006784 | bytes 9961472 | tf_op jit(solution)/shard_map/dot_general | solution.py:28
  136.4 5.1 %collective-permute-done.15 = bf16[256,1536]{1,0:T(8,128)(2,1)} collective-permute-done((bf16[256,1536]{1,0:T(8,128)(2,1)}, bf16[256,1536]{1,0:T(8,128)(2,1)}, u32[]{:S(2)}, u32[]{:S(2)}) %collective-permute-start.15) | collective-permute-done | bytes 786464 | tf_op jit(solution)/shard_map/ppermute | solution.py:69
  141.5 4.1 %fusion.78 = f32[256,1024]{1,0:T(8,128)} fusion(bf16[256,1536]{1,0:T(8,128)(2,1)} %collective-permute-done.15, bf16[1536,1024]{1,0:T(8,128)(2,1)} %copy-done.3), kind=kOutput, calls=%fused_computation.128 | convolution fusion | flops 805306368 | bytes 4980736 | tf_op jit(solution)/shard_map/dot_general | solution.py:28
  145.6 6.1 %convolution_convert_fusion.2 = bf16[256,1536]{1,0:T(8,128)(2,1)} fusion(f32[256,1024]{1,0:T(8,128)S(1)} %bitcast.114, f32[256,1024]{1,0:T(8,128)} %fusion.78, bf16[512,768]{1,0:T(8,128)(2,1)} %copy-done.20, bf16[512,768]{1,0:T(8,128)(2,1)} %copy-done.19, bf16[512,768]{1,0:T(8,128)(2,1)} %collective-permute-done.3, bf16[512,768]{1,0:T(8,128)(2,1)} %bitcast.138, ...), kind=kOutput, calls=%fused_computation.5 | convolution fusion | flops 1638006784 | bytes 9961472 | tf_op jit(solution)/shard_map/dot_general | solution.py:28
  152.6 5.8 %collective-permute-done.10 = bf16[256,1536]{1,0:T(8,128)(2,1)} collective-permute-done((bf16[256,1536]{1,0:T(8,128)(2,1)}, bf16[256,1536]{1,0:T(8,128)(2,1)}, u32[]{:S(2)}, u32[]{:S(2)}) %collective-permute-start.10) | collective-permute-done | bytes 786464 | tf_op jit(solution)/shard_map/ppermute | solution.py:69
  158.3 4.1 %fusion.76 = f32[256,1024]{1,0:T(8,128)} fusion(bf16[256,1536]{1,0:T(8,128)(2,1)} %collective-permute-done.10, bf16[1536,1024]{1,0:T(8,128)(2,1)} %copy-done.3), kind=kOutput, calls=%fused_computation.126 | convolution fusion | flops 805306368 | bytes 4980736 | tf_op jit(solution)/shard_map/dot_general | solution.py:28
  162.4 6.1 %convolution_convert_fusion.4 = bf16[256,1536]{1,0:T(8,128)(2,1)} fusion(f32[256,1024]{1,0:T(8,128)S(1)} %bitcast.115, f32[256,1024]{1,0:T(8,128)} %fusion.76, bf16[512,768]{1,0:T(8,128)(2,1)} %copy-done.20, bf16[512,768]{1,0:T(8,128)(2,1)} %copy-done.19, bf16[512,768]{1,0:T(8,128)(2,1)} %collective-permute-done.3, bf16[512,768]{1,0:T(8,128)(2,1)} %bitcast.139, ...), kind=kOutput, calls=%fused_computation.7 | convolution fusion | flops 1638006784 | bytes 9961472 | tf_op jit(solution)/shard_map/dot_general | solution.py:28
  169.4 4.1 %fusion.74 = f32[256,1024]{1,0:T(8,128)} fusion(bf16[256,1536]{1,0:T(8,128)(2,1)} %collective-permute-done.6, bf16[1536,1024]{1,0:T(8,128)(2,1)} %copy-done.3), kind=kOutput, calls=%fused_computation.124 | convolution fusion | flops 805306368 | bytes 4980736 | tf_op jit(solution)/shard_map/dot_general | solution.py:28
  173.5 6.1 %convolution_convert_fusion.6 = bf16[256,1536]{1,0:T(8,128)(2,1)} fusion(f32[256,1024]{1,0:T(8,128)S(1)} %bitcast.116, f32[256,1024]{1,0:T(8,128)} %fusion.74, bf16[512,768]{1,0:T(8,128)(2,1)} %copy-done.20, bf16[512,768]{1,0:T(8,128)(2,1)} %copy-done.19, bf16[512,768]{1,0:T(8,128)(2,1)} %collective-permute-done.3, bf16[512,768]{1,0:T(8,128)(2,1)} %bitcast.140, ...), kind=kOutput, calls=%fused_computation.9 | convolution fusion | flops 1638006784 | bytes 9961472 | tf_op jit(solution)/shard_map/dot_general | solution.py:28
  180.7 4.1 %fusion.79 = f32[256,1024]{1,0:T(8,128)} fusion(bf16[256,1536]{1,0:T(8,128)(2,1)} %copy-done.12, bf16[1536,1024]{1,0:T(8,128)(2,1)} %copy-done.3), kind=kOutput, calls=%fused_computation.129 | convolution fusion | flops 805306368 | bytes 4980736 | tf_op jit(solution)/shard_map/dot_general | solution.py:28
  184.8 3.2 %fusion.75 = f32[256,1024]{1,0:T(8,128)} fusion(bf16[256,1536]{1,0:T(8,128)(2,1)} %broadcast_select_fusion.1, bf16[1536,1024]{1,0:T(8,128)(2,1)S(1)} %copy-done.4), kind=kOutput, calls=%fused_computation.125 | convolution fusion | flops 805306368 | bytes 4980736 | tf_op jit(solution)/shard_map/dot_general | solution.py:28
  188.0 6.3 %fusion.15 = bf16[256,1536]{1,0:T(8,128)(2,1)} fusion(bf16[256,1536]{1,0:T(8,128)(2,1)} %collective-permute-done.20, f32[256,1024]{1,0:T(8,128)S(1)} %bitcast.111, f32[256,1024]{1,0:T(8,128)} %fusion.79, bf16[512,768]{1,0:T(8,128)(2,1)} %copy-done.20, bf16[512,768]{1,0:T(8,128)(2,1)} %copy-done.19, bf16[512,768]{1,0:T(8,128)(2,1)} %collective-permute-done.3, ...), kind=kOutput, calls=%fused_computation.26 | convolution fusion | flops 1639579648 | bytes 10747904 | tf_op jit(solution)/shard_map/dot_general | solution.py:28
  194.3 1.9 collective-permute-start.21
  196.2 12.7 %collective-permute-done.11 = bf16[256,1536]{1,0:T(8,128)(2,1)} collective-permute-done((bf16[256,1536]{1,0:T(8,128)(2,1)}, bf16[256,1536]{1,0:T(8,128)(2,1)}, u32[]{:S(2)}, u32[]{:S(2)}) %collective-permute-start.11) | collective-permute-done | bytes 786464 | tf_op jit(solution)/shard_map/ppermute | solution.py:69
  208.9 6.7 %fusion.6 = bf16[256,1536]{1,0:T(8,128)(2,1)} fusion(bf16[256,1536]{1,0:T(8,128)(2,1)} %collective-permute-done.11, f32[256,1024]{1,0:T(8,128)} %bitcast.112, f32[256,1024]{1,0:T(8,128)} %fusion.75, bf16[512,768]{1,0:T(8,128)(2,1)} %copy-done.20, bf16[512,768]{1,0:T(8,128)(2,1)} %copy-done.19, bf16[512,768]{1,0:T(8,128)(2,1)} %collective-permute-done.3, ...), kind=kOutput, calls=%fused_computation.17 | convolution fusion | flops 1639579648 | bytes 10747904 | tf_op jit(solution)/shard_map/dot_general | solution.py:28
  215.6 1.6 collective-permute-start.12
  218.3 4.1 %fusion.77 = f32[256,1024]{1,0:T(8,128)} fusion(bf16[256,1536]{1,0:T(8,128)(2,1)} %collective-permute-done.14, bf16[1536,1024]{1,0:T(8,128)(2,1)} %copy-done.3), kind=kOutput, calls=%fused_computation.127 | convolution fusion | flops 805306368 | bytes 4980736 | tf_op jit(solution)/shard_map/dot_general | solution.py:28
  222.4 9.2 %collective-permute-done.12 = bf16[256,1536]{1,0:T(8,128)(2,1)S(1)} collective-permute-done((bf16[256,1536]{1,0:T(8,128)(2,1)}, bf16[256,1536]{1,0:T(8,128)(2,1)S(1)}, u32[]{:S(2)}, u32[]{:S(2)}) %collective-permute-start.12) | collective-permute-done | bytes 786464 | tf_op jit(solution)/shard_map/ppermute | solution.py:69
  231.6 2.2 add_convert_fusion.1
  233.8 1.5 collective-permute-start.13
  236.3 6.1 %fusion.12 = bf16[256,1536]{1,0:T(8,128)(2,1)} fusion(bf16[256,1536]{1,0:T(8,128)(2,1)} %copy-done.22, bf16[256,1536]{1,0:T(8,128)(2,1)} %collective-permute-done.16, f32[256,1024]{1,0:T(8,128)S(1)} %bitcast.110, f32[256,1024]{1,0:T(8,128)} %fusion.77, bf16[512,768]{1,0:T(8,128)(2,1)} %copy-done.20, bf16[512,768]{1,0:T(8,128)(2,1)} %copy-done.19, ...), kind=kOutput, calls=%fused_computation.23 | convolution fusion | flops 1641152512 | bytes 11534336 | tf_op jit(solution)/shard_map/dot_general | solution.py:28
  242.4 2.8 %collective-permute-start.23 = (bf16[256,1536]{1,0:T(8,128)(2,1)}, bf16[256,1536]{1,0:T(8,128)(2,1)}, u32[]{:S(2)}, u32[]{:S(2)}) collective-permute-start(bf16[256,1536]{1,0:T(8,128)(2,1)} %fusion.12), channel_id=1, source_target_pairs={{0,4},{1,5},{2,6},{3,7},{4,0},{5,1},{6,2},{7,3},{8,12},{9,13},{10,... | collective-permute-start | bytes 2359304 | tf_op jit(solution)/shard_map/ppermute | solution.py:69
  245.8 1.3 copy-done.5
  247.2 3.1 %fusion.73 = f32[256,1024]{1,0:T(8,128)} fusion(bf16[256,1536]{1,0:T(8,128)(2,1)} %maximum_select_fusion.1, bf16[1536,1024]{1,0:T(8,128)(2,1)S(1)} %copy-done.5), kind=kOutput, calls=%fused_computation.123 | convolution fusion | flops 805306368 | bytes 4980736 | tf_op jit(solution)/shard_map/dot_general | solution.py:28
  250.3 9.1 %collective-permute-done.23 = bf16[256,1536]{1,0:T(8,128)(2,1)} collective-permute-done((bf16[256,1536]{1,0:T(8,128)(2,1)}, bf16[256,1536]{1,0:T(8,128)(2,1)}, u32[]{:S(2)}, u32[]{:S(2)}) %collective-permute-start.23) | collective-permute-done | bytes 786464 | tf_op jit(solution)/shard_map/ppermute | solution.py:69
  259.4 6.0 %fusion.3 = f32[256,1536]{1,0:T(8,128)S(1)} fusion(bf16[256,1536]{1,0:T(8,128)(2,1)} %collective-permute-done.23, bf16[256,1536]{1,0:T(8,128)(2,1)} %collective-permute-done.13, bf16[256,1536]{1,0:T(8,128)(2,1)} %collective-permute-done.7, f32[256,1024]{1,0:T(8,128)S(1)} %bitcast.117, f32[256,1024]{1,0:T(8,128)} %fusion.73, ...), kind=kOutput, calls=%fused_computation.14 | convolution fusion | flops 1640759296 | bytes 13107200 | tf_op jit(solution)/shard_map/dot_general | solution.py:28
  265.5 1.2 fusion.19
  (119 shorter events, 27.2 us)
Async XLA Ops:
  0.0 14.0 %copy-start = (bf16[1536,16]{0,1:T(8,128)(2,1)S(1)}, bf16[1536,16]{0,1:T(8,128)(2,1)}, u32[]{:S(2)}) copy-start(bf16[1536,16]{0,1:T(8,128)(2,1)} %param.12) | copy-start | bytes 147460
  0.0 5.7 %copy-start.2 = (bf16[256,1536]{1,0:T(8,128)(2,1)S(1)}, bf16[256,1536]{1,0:T(8,128)(2,1)}, u32[]{:S(2)}) copy-start(bf16[256,1536]{1,0:T(8,128)(2,1)} %param.8) | copy-start | bytes 2359300
  0.0 6.0 %copy-start.16 = (f32[1536]{0:T(1024)S(1)}, f32[1536]{0:T(1024)}, u32[]{:S(2)}) copy-start(f32[1536]{0:T(1024)} %param.11) | copy-start | bytes 18436
  2.8 63.0 %collective-permute-start = (bf16[768,1024]{1,0:T(8,128)(2,1)}, bf16[768,1024]{1,0:T(8,128)(2,1)S(1)}, u32[]{:S(2)}, u32[]{:S(2)}) collective-permute-start(bf16[768,1024]{1,0:T(8,128)(2,1)} %pad_maximum_fusion), channel_id=1, source_target_pairs={{0,16},{16,0},{1,17},{17,1},{2,18},{18,2},{3,19},{19,3},{4,20},{20... | collective-permute-start | bytes 4718600 | tf_op jit(solution)/shard_map/ppermute | solution.py:85
  5.7 82.3 %collective-permute-start.1 = (bf16[768,1024]{1,0:T(8,128)(2,1)}, bf16[768,1024]{1,0:T(8,128)(2,1)}, u32[]{:S(2)}, u32[]{:S(2)}) collective-permute-start(bf16[768,1024]{1,0:T(8,128)(2,1)} %pad_maximum_fusion), channel_id=1, source_target_pairs={{0,1},{1,0},{2,3},{3,2},{4,5},{5,4},{6,7},{7,6},{8,9},{9,8},{10,11... | collective-permute-start | bytes 4718600 | tf_op jit(solution)/shard_map/ppermute | solution.py:69
  5.7 7.5 %copy-start.17 = (s32[256,8]{0,1:T(8,128)S(1)}, s32[256,8]{0,1:T(8,128)}, u32[]{:S(2)}) copy-start(s32[256,8]{0,1:T(8,128)} %param.10) | copy-start | bytes 24580
  9.6 35.8 %collective-permute-start.14 = (bf16[256,1536]{1,0:T(8,128)(2,1)}, bf16[256,1536]{1,0:T(8,128)(2,1)}, u32[]{:S(2)}, u32[]{:S(2)}) collective-permute-start(bf16[256,1536]{1,0:T(8,128)(2,1)} %maximum_select_fusion.1), channel_id=1, source_target_pairs={{0,4},{1,5},{2,6},{3,7},{4,0},{5,1},{6,2},{7,3},{8,12},{9,13},{10,... | collective-permute-start | bytes 2359304 | tf_op jit(solution)/shard_map/ppermute | solution.py:69
  11.1 36.0 %collective-permute-start.8 = (bf16[256,1536]{1,0:T(8,128)(2,1)}, bf16[256,1536]{1,0:T(8,128)(2,1)}, u32[]{:S(2)}, u32[]{:S(2)}) collective-permute-start(bf16[256,1536]{1,0:T(8,128)(2,1)} %maximum_select_fusion.1), channel_id=1, source_target_pairs={{4,8},{5,9},{6,10},{7,11},{8,4},{9,5},{10,6},{11,7},{20,24},{21,25... | collective-permute-start | bytes 2359304 | tf_op jit(solution)/shard_map/ppermute | solution.py:69
  12.7 78.9 %collective-permute-start.3 = (bf16[512,768]{1,0:T(8,128)(2,1)}, bf16[512,768]{1,0:T(8,128)(2,1)}, u32[]{:S(2)}, u32[]{:S(2)}) collective-permute-start(bf16[512,768]{1,0:T(8,128)(2,1)} %bitcast.136), channel_id=1, source_target_pairs={{0,16},{16,0},{1,17},{17,1},{2,18},{18,2},{3,19},{19,3},{4,20},{20... | collective-permute-start | bytes 2359304 | tf_op jit(solution)/shard_map/ppermute | solution.py:86
  45.4 18.8 %collective-permute-start.17 = (bf16[256,1536]{1,0:T(8,128)(2,1)}, bf16[256,1536]{1,0:T(8,128)(2,1)}, u32[]{:S(2)}, u32[]{:S(2)}) collective-permute-start(bf16[256,1536]{1,0:T(8,128)(2,1)} %collective-permute-done.14), channel_id=1, source_target_pairs={{4,8},{5,9},{6,10},{7,11},{8,4},{9,5},{10,6},{11,7},{20,24},{21,25... | collective-permute-start | bytes 2359304 | tf_op jit(solution)/shard_map/ppermute | solution.py:69
  47.1 22.0 %collective-permute-start.9 = (bf16[256,1536]{1,0:T(8,128)(2,1)}, bf16[256,1536]{1,0:T(8,128)(2,1)}, u32[]{:S(2)}, u32[]{:S(2)}) collective-permute-start(bf16[256,1536]{1,0:T(8,128)(2,1)} %collective-permute-done.8), channel_id=1, source_target_pairs={{4,0},{5,1},{6,2},{7,3},{8,12},{9,13},{10,14},{11,15},{20,16},{21,... | collective-permute-start | bytes 2359304 | tf_op jit(solution)/shard_map/ppermute | solution.py:69
  64.1 5.0 %copy-start.18 = (bf16[1,512,768]{2,1,0:T(8,128)(2,1)S(1)}, bf16[1,512,768]{2,1,0:T(8,128)(2,1)}, u32[]{:S(2)}) copy-start(bf16[1,512,768]{2,1,0:T(8,128)(2,1)} %param.15) | copy-start | bytes 2359300
  64.1 22.8 %collective-permute-start.18 = (bf16[256,1536]{1,0:T(8,128)(2,1)}, bf16[256,1536]{1,0:T(8,128)(2,1)S(1)}, u32[]{:S(2)}, u32[]{:S(2)}) collective-permute-start(bf16[256,1536]{1,0:T(8,128)(2,1)} %collective-permute-done.17), channel_id=1, source_target_pairs={{4,0},{5,1},{6,2},{7,3},{8,12},{9,13},{10,14},{11,15},{20,16},{21,... | collective-permute-start | bytes 2359304 | tf_op jit(solution)/shard_map/ppermute | solution.py:69
  65.8 26.7 %collective-permute-start.2 = (bf16[768,1024]{1,0:T(8,128)(2,1)S(1)}, bf16[768,1024]{1,0:T(8,128)(2,1)S(1)}, u32[]{:S(2)}, u32[]{:S(2)}) collective-permute-start(bf16[768,1024]{1,0:T(8,128)(2,1)S(1)} %collective-permute-done), channel_id=1, source_target_pairs={{0,1},{1,0},{2,3},{3,2},{4,5},{5,4},{6,7},{7,6},{8,9},{9,8},{10,11... | collective-permute-start | bytes 4718600 | tf_op jit(solution)/shard_map/ppermute | solution.py:69
  69.1 58.3 %collective-permute-start.4 = (bf16[512,768]{1,0:T(8,128)(2,1)S(1)}, bf16[512,768]{1,0:T(8,128)(2,1)S(1)}, u32[]{:S(2)}, u32[]{:S(2)}) collective-permute-start(bf16[512,768]{1,0:T(8,128)(2,1)S(1)} %bitcast.145), channel_id=1, source_target_pairs={{0,1},{1,0},{2,3},{3,2},{4,5},{5,4},{6,7},{7,6},{8,9},{9,8},{10,11... | collective-permute-start | bytes 2359304 | tf_op jit(solution)/shard_map/ppermute | solution.py:69
  87.0 82.4 %collective-permute-start.6 = (bf16[256,1536]{1,0:T(8,128)(2,1)}, bf16[256,1536]{1,0:T(8,128)(2,1)}, u32[]{:S(2)}, u32[]{:S(2)}) collective-permute-start(bf16[256,1536]{1,0:T(8,128)(2,1)} %maximum_select_fusion.1), channel_id=1, source_target_pairs={{0,2},{1,3},{2,0},{3,1},{4,6},{5,7},{6,4},{7,5},{8,10},{9,11},{10,... | collective-permute-start | bytes 2359304 | tf_op jit(solution)/shard_map/ppermute | solution.py:69
  88.0 5.5 %copy-start.12 = (bf16[256,1536]{1,0:T(8,128)(2,1)}, bf16[256,1536]{1,0:T(8,128)(2,1)S(1)}, u32[]{:S(2)}) copy-start(bf16[256,1536]{1,0:T(8,128)(2,1)S(1)} %broadcast_select_fusion) | copy-start | bytes 2359300
  88.0 5.5 %copy-start.6 = (bf16[1,768,512]{2,1,0:T(8,128)(2,1)S(1)}, bf16[1,768,512]{2,1,0:T(8,128)(2,1)}, u32[]{:S(2)}) copy-start(bf16[1,768,512]{2,1,0:T(8,128)(2,1)} %param.13) | copy-start | bytes 2359300
  88.1 36.5 %collective-permute-start.19 = (bf16[256,1536]{1,0:T(8,128)(2,1)S(1)}, bf16[256,1536]{1,0:T(8,128)(2,1)S(1)}, u32[]{:S(2)}, u32[]{:S(2)}) collective-permute-start(bf16[256,1536]{1,0:T(8,128)(2,1)S(1)} %broadcast_select_fusion), channel_id=1, source_target_pairs={{0,2},{1,3},{2,0},{3,1},{4,6},{5,7},{6,4},{7,5},{8,10},{9,11},{10,... | collective-permute-start | bytes 2359304 | tf_op jit(solution)/shard_map/ppermute | solution.py:69
  91.6 49.9 %collective-permute-start.15 = (bf16[256,1536]{1,0:T(8,128)(2,1)}, bf16[256,1536]{1,0:T(8,128)(2,1)}, u32[]{:S(2)}, u32[]{:S(2)}) collective-permute-start(bf16[256,1536]{1,0:T(8,128)(2,1)} %collective-permute-done.14), channel_id=1, source_target_pairs={{0,2},{1,3},{2,0},{3,1},{4,6},{5,7},{6,4},{7,5},{8,10},{9,11},{10,... | collective-permute-start | bytes 2359304 | tf_op jit(solution)/shard_map/ppermute | solution.py:69
  92.5 35.9 %collective-permute-start.5 = (bf16[512,768]{1,0:T(8,128)(2,1)}, bf16[512,768]{1,0:T(8,128)(2,1)S(1)}, u32[]{:S(2)}, u32[]{:S(2)}) collective-permute-start(bf16[512,768]{1,0:T(8,128)(2,1)} %collective-permute-done.3), channel_id=1, source_target_pairs={{0,1},{1,0},{2,3},{3,2},{4,5},{5,4},{6,7},{7,6},{8,9},{9,8},{10,11... | collective-permute-start | bytes 2359304 | tf_op jit(solution)/shard_map/ppermute | solution.py:69
  106.2 19.3 %copy-start.3 = (bf16[1536,1024]{1,0:T(8,128)(2,1)}, bf16[1536,1024]{1,0:T(8,128)(2,1)S(1)}, u32[]{:S(2)}) copy-start(bf16[1536,1024]{1,0:T(8,128)(2,1)S(1)} %maximum_maximum_fusion) | copy-start | bytes 9437188
  106.2 23.1 %copy-start.8 = (f32[32,8,2,512]{3,1,2,0:T(8,128)S(1)}, f32[32,8,2,512]{3,1,2,0:T(8,128)}, u32[]{:S(2)}) copy-start(f32[32,8,2,512]{3,1,2,0:T(8,128)} %copy.24) | copy-start | bytes 3145732
  124.5 4.7 %copy-start.21 = (bf16[256,1536]{1,0:T(8,128)(2,1)}, bf16[256,1536]{1,0:T(8,128)(2,1)S(1)}, u32[]{:S(2)}) copy-start(bf16[256,1536]{1,0:T(8,128)(2,1)S(1)} %collective-permute-done.19) | copy-start | bytes 2359300
  124.5 33.8 %collective-permute-start.10 = (bf16[256,1536]{1,0:T(8,128)(2,1)}, bf16[256,1536]{1,0:T(8,128)(2,1)}, u32[]{:S(2)}, u32[]{:S(2)}) collective-permute-start(bf16[256,1536]{1,0:T(8,128)(2,1)} %broadcast_select_fusion.1), channel_id=1, source_target_pairs={{0,2},{1,3},{2,0},{3,1},{4,6},{5,7},{6,4},{7,5},{8,10},{9,11},{10,... | collective-permute-start | bytes 2359304 | tf_op jit(solution)/shard_map/ppermute | solution.py:69
  127.5 0.9 copy-start.19
  128.4 0.9 copy-start.20
  135.3 10.3 %copy-start.9 = (f32[32,8,2,512]{3,1,2,0:T(8,128)S(1)}, f32[32,8,2,512]{3,1,2,0:T(8,128)}, u32[]{:S(2)}) copy-start(f32[32,8,2,512]{3,1,2,0:T(8,128)} %copy.22) | copy-start | bytes 3145732
  135.3 52.7 %collective-permute-start.20 = (bf16[256,1536]{1,0:T(8,128)(2,1)}, bf16[256,1536]{1,0:T(8,128)(2,1)}, u32[]{:S(2)}, u32[]{:S(2)}) collective-permute-start(bf16[256,1536]{1,0:T(8,128)(2,1)} %convolution_convert_fusion), channel_id=1, source_target_pairs={{0,2},{1,3},{2,0},{3,1},{4,6},{5,7},{6,4},{7,5},{8,10},{9,11},{10,... | collective-permute-start | bytes 2359304 | tf_op jit(solution)/shard_map/ppermute | solution.py:69
  151.7 10.8 %copy-start.10 = (f32[32,8,2,512]{3,1,2,0:T(8,128)S(1)}, f32[32,8,2,512]{3,1,2,0:T(8,128)}, u32[]{:S(2)}) copy-start(f32[32,8,2,512]{3,1,2,0:T(8,128)} %copy.20) | copy-start | bytes 3145732
  151.7 83.7 %collective-permute-start.16 = (bf16[256,1536]{1,0:T(8,128)(2,1)}, bf16[256,1536]{1,0:T(8,128)(2,1)}, u32[]{:S(2)}, u32[]{:S(2)}) collective-permute-start(bf16[256,1536]{1,0:T(8,128)(2,1)} %convolution_convert_fusion.2), channel_id=1, source_target_pairs={{0,2},{1,3},{2,0},{3,1},{4,6},{5,7},{6,4},{7,5},{8,10},{9,11},{10,... | collective-permute-start | bytes 2359304 | tf_op jit(solution)/shard_map/ppermute | solution.py:69
  168.5 5.0 %copy-start.11 = (f32[32,8,2,512]{3,1,2,0:T(8,128)S(1)}, f32[32,8,2,512]{3,1,2,0:T(8,128)}, u32[]{:S(2)}) copy-start(f32[32,8,2,512]{3,1,2,0:T(8,128)} %copy.18) | copy-start | bytes 3145732
  168.5 40.4 %collective-permute-start.11 = (bf16[256,1536]{1,0:T(8,128)(2,1)}, bf16[256,1536]{1,0:T(8,128)(2,1)}, u32[]{:S(2)}, u32[]{:S(2)}) collective-permute-start(bf16[256,1536]{1,0:T(8,128)(2,1)} %convolution_convert_fusion.4), channel_id=1, source_target_pairs={{0,2},{1,3},{2,0},{3,1},{4,6},{5,7},{6,4},{7,5},{8,10},{9,11},{10,... | collective-permute-start | bytes 2359304 | tf_op jit(solution)/shard_map/ppermute | solution.py:69
  179.6 5.2 %copy-start.4 = (bf16[1536,1024]{1,0:T(8,128)(2,1)S(1)}, bf16[1536,1024]{1,0:T(8,128)(2,1)}, u32[]{:S(2)}) copy-start(bf16[1536,1024]{1,0:T(8,128)(2,1)} %copy-done.3) | copy-start | bytes 9437188
  179.6 70.7 %collective-permute-start.7 = (bf16[256,1536]{1,0:T(8,128)(2,1)}, bf16[256,1536]{1,0:T(8,128)(2,1)}, u32[]{:S(2)}, u32[]{:S(2)}) collective-permute-start(bf16[256,1536]{1,0:T(8,128)(2,1)} %convolution_convert_fusion.6), channel_id=1, source_target_pairs={{0,2},{1,3},{2,0},{3,1},{4,6},{5,7},{6,4},{7,5},{8,10},{9,11},{10,... | collective-permute-start | bytes 2359304 | tf_op jit(solution)/shard_map/ppermute | solution.py:69
  184.8 3.2 %copy-start.7 = (f32[32,8,2,512]{3,1,2,0:T(8,128)S(1)}, f32[32,8,2,512]{3,1,2,0:T(8,128)}, u32[]{:S(2)}) copy-start(f32[32,8,2,512]{3,1,2,0:T(8,128)} %copy.23) | copy-start | bytes 3145732
  194.3 22.9 %collective-permute-start.21 = (bf16[256,1536]{1,0:T(8,128)(2,1)}, bf16[256,1536]{1,0:T(8,128)(2,1)S(1)}, u32[]{:S(2)}, u32[]{:S(2)}) collective-permute-start(bf16[256,1536]{1,0:T(8,128)(2,1)} %fusion.15), channel_id=1, source_target_pairs={{0,4},{1,5},{2,6},{3,7},{12,8},{13,9},{14,10},{15,11},{16,20},{17,... | collective-permute-start | bytes 2359304 | tf_op jit(solution)/shard_map/ppermute | solution.py:69
  208.9 8.3 %copy-start.15 = (bf16[256,1536]{1,0:T(8,128)(2,1)S(1)}, bf16[256,1536]{1,0:T(8,128)(2,1)}, u32[]{:S(2)}) copy-start(bf16[256,1536]{1,0:T(8,128)(2,1)} %fusion.15) | copy-start | bytes 2359300
  215.6 16.0 %collective-permute-start.12 = (bf16[256,1536]{1,0:T(8,128)(2,1)}, bf16[256,1536]{1,0:T(8,128)(2,1)S(1)}, u32[]{:S(2)}, u32[]{:S(2)}) collective-permute-start(bf16[256,1536]{1,0:T(8,128)(2,1)} %fusion.6), channel_id=1, source_target_pairs={{0,4},{1,5},{2,6},{3,7},{12,8},{13,9},{14,10},{15,11},{16,20},{17,... | collective-permute-start | bytes 2359304 | tf_op jit(solution)/shard_map/ppermute | solution.py:69
  217.4 18.9 %copy-start.13 = (bf16[1,768,512]{2,1,0:T(8,128)(2,1)S(1)}, bf16[1,768,512]{2,1,0:T(8,128)(2,1)}, u32[]{:S(2)}) copy-start(bf16[1,768,512]{2,1,0:T(8,128)(2,1)} %param.14) | copy-start | bytes 2359300
  217.4 18.8 %copy-start.14 = (bf16[768,512]{1,0:T(8,128)(2,1)S(1)}, bf16[768,512]{1,0:T(8,128)(2,1)}, u32[]{:S(2)}) copy-start(bf16[768,512]{1,0:T(8,128)(2,1)} %get-tuple-element.8) | copy-start | bytes 2359300
  217.4 17.9 %collective-permute-start.22 = (bf16[256,1536]{1,0:T(8,128)(2,1)S(1)}, bf16[256,1536]{1,0:T(8,128)(2,1)S(1)}, u32[]{:S(2)}, u32[]{:S(2)}) collective-permute-start(bf16[256,1536]{1,0:T(8,128)(2,1)S(1)} %add_convert_fusion), channel_id=1, source_target_pairs={{4,8},{5,9},{6,10},{7,11},{8,4},{9,5},{10,6},{11,7},{20,24},{21,25... | collective-permute-start | bytes 2359304 | tf_op jit(solution)/shard_map/ppermute | solution.py:69
  233.8 16.5 %collective-permute-start.13 = (bf16[256,1536]{1,0:T(8,128)(2,1)}, bf16[256,1536]{1,0:T(8,128)(2,1)}, u32[]{:S(2)}, u32[]{:S(2)}) collective-permute-start(bf16[256,1536]{1,0:T(8,128)(2,1)} %add_convert_fusion.1), channel_id=1, source_target_pairs={{4,8},{5,9},{6,10},{7,11},{8,4},{9,5},{10,6},{11,7},{20,24},{21,25... | collective-permute-start | bytes 2359304 | tf_op jit(solution)/shard_map/ppermute | solution.py:69
  235.4 0.9 copy-start.22
  242.4 17.0 %collective-permute-start.23 = (bf16[256,1536]{1,0:T(8,128)(2,1)}, bf16[256,1536]{1,0:T(8,128)(2,1)}, u32[]{:S(2)}, u32[]{:S(2)}) collective-permute-start(bf16[256,1536]{1,0:T(8,128)(2,1)} %fusion.12), channel_id=1, source_target_pairs={{0,4},{1,5},{2,6},{3,7},{4,0},{5,1},{6,2},{7,3},{8,12},{9,13},{10,... | collective-permute-start | bytes 2359304 | tf_op jit(solution)/shard_map/ppermute | solution.py:69
  245.3 1.9 copy-start.5
  265.4 1.4 copy-start.1

commit v2 on v1

v2 whole, which is shorter than its diff:
```python
import functools
import jax
import jax.numpy as jnp
from jax import lax
from jax.experimental import pallas as pl
from jax.experimental.pallas import tpu as pltpu
from jax.sharding import PartitionSpec as P

LMAX = 4096
F32 = jnp.float32
BF16 = jnp.bfloat16


def gate_of(logits, routes, lengths, experts):
    rows = logits.shape[0]
    position = lax.axis_index("tensor") * rows + jnp.arange(rows, dtype=jnp.int32)
    living = position % LMAX < lengths[position // LMAX]
    ids = jnp.arange(experts, dtype=jnp.int32)
    named = jnp.zeros((rows, experts), jnp.bool_)
    for k in range(routes.shape[1]):
        named = named | (routes[:, k : k + 1] == ids[None, :])
    return jnp.where(named & living[:, None], jax.nn.sigmoid(logits), 0.0)


def norm_of(tokens_f32, norm_gain):
    scale_rows = lax.rsqrt(jnp.mean(tokens_f32 * tokens_f32, axis=-1, keepdims=True) + 1e-06)
    return (tokens_f32 * scale_rows * norm_gain).astype(BF16)


def dot(a, b):
    return jnp.dot(a, b, preferred_element_type=F32)


def general(tokens, lengths, routes, norm_gain, router, w_gate, w_up, w_down):
    experts = router.shape[1]
    local = w_gate.shape[0]
    tokens_f32 = tokens.astype(F32)
    normed = norm_of(tokens_f32, norm_gain)
    gates = gate_of(dot(normed, router), routes, lengths, experts)
    gate_all = lax.all_gather(w_gate, "dp", axis=1, tiled=True)
    up_all = lax.all_gather(w_up, "dp", axis=1, tiled=True)
    down_all = lax.all_gather(w_down, "dp", axis=2, tiled=True)
    rows_all = lax.all_gather(normed, "tensor", axis=0, tiled=True)
    gates_all = lax.all_gather(gates, "tensor", axis=0, tiled=True)
    first = lax.axis_index("tensor") * local
    total = jnp.zeros(rows_all.shape, F32)
    for x in range(local):
        weight = lax.dynamic_slice_in_dim(gates_all, first + x, 1, axis=1)
        hidden = jax.nn.silu(dot(rows_all, gate_all[x])) * dot(rows_all, up_all[x])
        total = total + dot((hidden * weight).astype(BF16), down_all[x])
    combined = lax.psum_scatter(total.astype(BF16), "tensor", scatter_dimension=0, tiled=True)
    return (tokens_f32 + combined.astype(F32)).astype(BF16)


def prologue_kernel(scalars, tokens, gain, router, routes_t, normed, gates_t):
    v = tokens[...].astype(F32)
    scale_rows = lax.rsqrt(jnp.mean(v * v, axis=-1, keepdims=True) + 1e-06)
    out = (v * scale_rows * gain[...]).astype(BF16)
    normed[...] = out
    logits_t = lax.dot_general(router[...], out, (((1,), (1,)), ((), ())), preferred_element_type=F32)
    experts, rows = logits_t.shape
    ids = lax.broadcasted_iota(jnp.int32, (experts, rows), 0)
    position = scalars[0] + lax.broadcasted_iota(jnp.int32, (experts, rows), 1)
    named = routes_t[0:1, :] == ids
    for k in range(1, routes_t.shape[0]):
        named = named | (routes_t[k : k + 1, :] == ids)
    living = position < scalars[1]
    gates_t[...] = jnp.where(named & living, jax.nn.sigmoid(logits_t), 0.0)


def expert_kernel(gate_at, scalars, *refs):
    count = len(gate_at)
    gates, blocks = refs[:3], refs[3 : 3 + count]
    weights = refs[3 + count : 15 + count]
    outs, total = refs[15 + count : 15 + 2 * count], refs[15 + 2 * count]
    step, last = pl.program_id(0), pl.num_programs(0) - 1
    rows, width = blocks[0].shape
    half = width // 2
    own = pl.ds(pl.multiple_of(scalars[0] * half, half), half)
    far = pl.ds(pl.multiple_of((1 - scalars[0]) * half, half), half)
    eye = lax.broadcasted_iota(jnp.int32, (rows, rows), 0) == lax.broadcasted_iota(jnp.int32, (rows, rows), 1)
    for b in range(count):
        which, entry, side = gate_at[b]
        entry = scalars[-entry] + side if entry < 0 else entry + side
        near, away = blocks[b][:, own], blocks[b][:, far]
        hidden = []
        for e in range(2):
            go, gf, uo, uf = (weights[6 * e + i] for i in range(4))
            line = gates[which][entry, pl.ds(scalars[1 + e], 1), :]
            weight = jnp.sum(jnp.where(eye, line, 0.0), axis=1, keepdims=True)
            gate = dot(near, go[...]) + dot(away, gf[...])
            up = dot(near, uo[...]) + dot(away, uf[...])
            hidden.append((jax.nn.silu(gate) * up * weight).astype(BF16))
        for columns, i in ((own, 4), (far, 5)):
            value = dot(hidden[0], weights[i][...]) + dot(hidden[1], weights[6 + i][...])

            @pl.when(step == 0)
            def _():
                total[b, :, columns] = value

            @pl.when((step > 0) & (step < last))
            def _():
                total[b, :, columns] += value

            @pl.when(step == last)
            def _():
                outs[b][:, columns] = (total[b, :, columns] + value).astype(BF16)


def lanes(tokens, lengths, routes, norm_gain, router, w_gate, w_up, w_down):
    experts = router.shape[1]
    rows, width = tokens.shape
    half = width // 2
    hid = w_gate.shape[2]
    x = lax.axis_index("dp")
    t = lax.axis_index("tensor")
    z, y, c = t // 4, (t // 2) % 2, t % 2
    middle = (z == 1) | (z == 2)

    def over(axis_pairs):
        return [(a * 4 + r, b * 4 + r) for a, b in axis_pairs for r in range(4)]

    def send(v, pairs):
        return lax.ppermute(v, "tensor", pairs)

    by_core = [(i, i ^ 1) for i in range(16)]
    by_y = [(i, i ^ 2) for i in range(16)]
    outer = over([(0, 1), (1, 0), (2, 3), (3, 2)])
    inner = over([(1, 2), (2, 1)])
    skip = over([(0, 2), (2, 0), (1, 3), (3, 1)])
    outward = over([(1, 0), (2, 3)])
    inward = over([(0, 1), (3, 2)])

    smem = pl.BlockSpec(memory_space=pltpu.SMEM)
    vmem = pl.BlockSpec(memory_space=pltpu.VMEM)
    place = jnp.stack([t * rows, lengths[0]]).astype(jnp.int32)
    s_0, gates = pl.pallas_call(
        prologue_kernel,
        out_shape=(jax.ShapeDtypeStruct((rows, width), BF16), jax.ShapeDtypeStruct((experts, rows), F32)),
        in_specs=[smem] + [vmem] * 4,
        out_specs=(vmem, vmem),
        name="prologue",
    )(place, tokens, norm_gain.reshape(1, width), router.T, routes.T)

    def together(*values):
        return lax.optimization_barrier(values)

    own_w = [w_gate[0], w_up[0], w_down[0]]
    far_w = [None] * 3
    pair_far = [None] * 3
    own_w[0], own_w[1], own_w[2], s_0, gates = together(*own_w, s_0, gates)

    t_0 = send(s_0, by_y)
    s_a = send(s_0, outer)
    s_m = send(s_0, inner)
    far_w[0] = lax.ppermute(own_w[0], "dp", [(0, 1), (1, 0)])
    g_y = send(gates, by_y)
    pair_own = [send(w, by_core) for w in own_w]
    s_0, t_0, s_a, s_m, far_w[0], g_y, own_w[1], own_w[2], pair_own[0], pair_own[1], pair_own[2] = together(
        s_0, t_0, s_a, s_m, far_w[0], g_y, own_w[1], own_w[2], *pair_own
    )

    t_a = send(s_a, by_y)
    s_b = send(s_m, outward)
    s_n = send(s_a, inner)
    far_w[1] = lax.ppermute(own_w[1], "dp", [(0, 1), (1, 0)])
    pair_far[0] = send(far_w[0], by_core)
    g_0 = jnp.stack([gates, g_y])
    g_1 = send(g_0, outer)
    t_a, s_b, s_n, far_w[1], pair_far[0], g_0, g_1, own_w[2] = together(
        t_a, s_b, s_n, far_w[1], pair_far[0], g_0, g_1, own_w[2]
    )

    s_b = jnp.where(middle, s_m, s_b)
    t_b = send(s_b, by_y)
    s_c = send(s_n, outward)
    far_w[2] = lax.ppermute(own_w[2], "dp", [(0, 1), (1, 0)])
    pair_far[1] = send(far_w[1], by_core)
    g_2 = send(jnp.concatenate([g_0, g_1]), skip)
    s_b, t_b, s_c, far_w[2], pair_far[1], g_2, t_a, s_n = together(s_b, t_b, s_c, far_w[2], pair_far[1], g_2, t_a, s_n)

    s_c = jnp.where(middle, s_n, s_c)
    t_c = send(s_c, by_y)
    pair_far[2] = send(far_w[2], by_core)
    weights = []
    for near, away in ((own_w, far_w), (pair_own, pair_far)):
        for o, f in zip(near, away):
            weights += [o, f]

    scalars = jnp.stack([x, t, t ^ 1, jnp.where(middle, 2, 0), jnp.where(middle, 0, 2)]).astype(jnp.int32)
    at = {"0": (0, 0), "a": (1, 0), "b": (2, -3), "c": (2, -4)}

    def run(w, g_0, g_1, g_2, *named):
        count = len(named)
        block = pl.BlockSpec((rows, width), lambda h: (0, 0))
        into = pl.BlockSpec((half, 256), lambda h: (0, h))
        outof = pl.BlockSpec((256, half), lambda h: (h, 0))
        gate_spec = [pl.BlockSpec(g.shape, lambda h: (0, 0, 0)) for g in (g_0, g_1, g_2)]
        gate_at = tuple(at[n[1]] + (int(n[0] == "t"),) for n, _ in named)
        flops = 2 * count * rows * 2 * 3 * width * hid
        return pl.pallas_call(
            functools.partial(expert_kernel, gate_at),
            grid=(hid // 256,),
            out_shape=tuple(jax.ShapeDtypeStruct((rows, width), BF16) for _ in named),
            in_specs=[smem] + gate_spec + [block] * count + ([into] * 4 + [outof] * 2) * 2,
            out_specs=tuple([block] * count),
            scratch_shapes=[pltpu.VMEM((count, rows, width), F32)],
            compiler_params=pltpu.CompilerParams(vmem_limit_bytes=40 * 2**20),
            cost_estimate=pl.CostEstimate(flops=flops, bytes_accessed=12 * width * hid, transcendentals=0),
            name="experts_" + "_".join(n for n, _ in named),
        )(scalars, g_0, g_1, g_2, *(v for _, v in named), *w)

    def add(a, b):
        return (a.astype(F32) + b.astype(F32)).astype(BF16)

    g = (g_0, g_1, g_2)
    p_sc, p_tb, p_ta = run(weights, *g, ("sc", s_c), ("tb", t_b), ("ta", t_a))
    t_c, p_sc, p_tb, p_ta = together(t_c, p_sc, p_tb, p_ta)
    (p_tc,) = run(weights, *g, ("tc", t_c))
    p_tc, s_b, t_0, s_a, s_0 = together(p_tc, s_b, t_0, s_a, s_0)

    r_c = send(p_tc, by_y)
    p_sb, p_t0, p_sa = run(weights, *g, ("sb", s_b), ("t0", t_0), ("sa", s_a))
    r_c, p_sb, p_t0, p_sa, p_tb, s_0 = together(r_c, p_sb, p_t0, p_sa, p_tb, s_0)

    q_c = add(p_sc, r_c)
    r_b = send(p_tb, by_y)
    r_n = send(q_c, inward)
    (p_s0,) = run(weights, *g, ("s0", s_0))
    q_c, r_b, r_n, p_s0, p_ta = together(q_c, r_b, r_n, p_s0, p_ta)

    q_n = add(q_c, r_n)
    q_b = add(p_sb, r_b)
    r_a = send(p_ta, by_y)
    r_i = send(q_n, inner)
    r_m = send(q_b, inward)
    r_a, r_i, r_m, q_b, p_t0 = together(r_a, r_i, r_m, q_b, p_t0)

    q_a = p_sa.astype(F32) + r_a.astype(F32) + r_i.astype(F32)
    r_0 = send(p_t0, by_y)
    r_o = send(q_a.astype(BF16), outer)
    r_m = send(add(q_b, r_m), inner)
    combined = p_s0.astype(F32) + r_0.astype(F32) + r_m.astype(F32) + r_o.astype(F32)
    return (tokens.astype(F32) + combined).astype(BF16)


def solution(mesh):
    placed = (
        P(("dp", "tensor"), None),
        P("dp"),
        P(("dp", "tensor"), None),
        P(),
        P(),
        P("tensor", "dp", None),
        P("tensor", "dp", None),
        P("tensor", None, "dp"),
    )

    def shards(*args):
        fits = mesh.shape["dp"] == 2 and mesh.shape["tensor"] == 16 and args[5].shape[0] == 1
        return (lanes if fits else general)(*args)

    return jax.shard_map(
        shards, mesh=mesh, in_specs=placed, out_specs=P(("dp", "tensor"), None), check_vma=False
    )
```

time: 267 us -> 196 us (0.73)
  matrix products: 78.4 us -> 0 us
  Pallas kernels: 0 us -> 40.2 us
  blocking collectives: 30.9 us -> 0 us
  other arithmetic: 24.2 us -> 5.94 us
  waiting for transfers between devices: 78 us -> 94.2 us
  local copies, waits for them, and re-layouts: 26 us -> 10.5 us
  starting transfers between devices: 28.1 us -> 43.3 us
    dot_general x17 -> x0, matrix products: 78.4 us -> none  [dot(): return jnp.dot(a, b, preferred_element_type=F32)]
    pallas_call x0 -> x5, Pallas kernels: none -> 40.2 us  [the longest x4 37.9 us: run(): pl.pallas_call(functools.partial(expert_kernel, gate_at), grid=(hid // 25...]
    all_gather x1 -> x0, blocking collectives: 30.9 us -> none  [lanes(): gates_all = lax.all_gather(gates.T, 'tensor', axis=0)]
    ppermute x22 -> x27, waiting for transfers between devices: 78 us -> 94.2 us  [send(): return lax.ppermute(v, 'tensor', pairs)]
    concatenate x2 -> x1, other arithmetic: 15.4 us -> 0.01 us  [lanes(): g_2 = send(jnp.concatenate([g_0, g_1]), skip)]
    ppermute x22 -> x27, starting transfers between devices: 24.6 us -> 38.6 us  [send(): return lax.ppermute(v, 'tensor', pairs)]
    broadcast_in_dim x8 -> x0, local copies, waits for them, and re-layouts: 5.4 us -> none  [partial(): w = jnp.repeat(w, hid, axis=1)]
    slice x6 -> x0, local copies, waits for them, and re-layouts: 5.4 us -> none  [the longest x3 4.33 us: lanes(): p[:, :hid]]
  transfers between devices with their start and end apart: 24 -> 30, of which waited for: 8 -> 15; matrix products, arithmetic and copies ran while one was open for 43% -> 1% of each run, Pallas kernels for 0% -> 16%
where the time goes in v2:
time: 196 us; the launch traced here: 195 us
  waiting for transfers between devices  94.2 us (48%)
  starting transfers between devices  43.3 us (22%)
  Pallas kernels  40.2 us (21%)
  local copies, waits for them, and re-layouts  10.5 us (5%)
  other arithmetic  5.94 us (3%)
    ppermute x27, waiting for transfers between devices, send(): return lax.ppermute(v, 'tensor', pairs)  94.2 us
    ppermute x27, starting transfers between devices, send(): return lax.ppermute(v, 'tensor', pairs)  38.6 us
    pallas_call x4, Pallas kernels, run(): pl.pallas_call(functools.partial(expert_kernel, gate_at), grid=(hid // 25...  37.9 us
    unnamed x40, local copies, waits for them, and re-layouts  9.1 us
  transfers between devices with their start and end apart: 30, of which 15 were waited for; matrix products, arithmetic and copies ran while one was open for 1% of the time, Pallas kernels for 16%

profile of v2, /device:TPU:0, one launch (start us, length us, event | category | flops | bytes accessed | tf_op | source)
XLA Modules:
  0.0 195.1 jit_solution(862412722786650028)
XLA Ops:
  0.7 1.3 reshape.3.gain
  2.6 2.4 %prologue.1 = (bf16[256,1536]{1,0:T(8,128)(2,1)}, f32[16,256]{1,0:T(8,128)}) custom-call(s32[2]{0:T(128)} %pad_add_fusion.scalars, bf16[256,1536]{1,0:T(8,128)(2,1)} %tokens.1, f32[1,1536]{1,0:T(1,128)} %reshape.3.gain, bf16[16,1536]{1,0:T(8,128)(2,1)} %bitcast.31, s32[8,256]{1,0:T(8,128)} %bitcast.34), custom_call_target="tpu_custom_call" | custom-call | tf_op jit(solution)/shard_map/prologue/pallas_call | solution.py:137
  5.5 3.0 %collective-permute-start.4 = (f32[16,256]{1,0:T(8,128)}, f32[16,256]{1,0:T(8,128)S(1)}, u32[]{:S(2)}, u32[]{:S(2)}) collective-permute-start(f32[16,256]{1,0:T(8,128)} %get-tuple-element.74), channel_id=1, source_target_pairs={{0,2},{1,3},{2,0},{3,1},{4,6},{5,7},{6,4},{7,5},{8,10},{9,11},{10,... | collective-permute-start | bytes 49160 | tf_op jit(solution)/shard_map/ppermute | solution.py:124
  8.5 1.5 collective-permute-start.2
  10.0 3.6 %collective-permute-start.1 = (bf16[256,1536]{1,0:T(8,128)(2,1)}, bf16[256,1536]{1,0:T(8,128)(2,1)}, u32[]{:S(2)}, u32[]{:S(2)}) collective-permute-start(bf16[256,1536]{1,0:T(8,128)(2,1)} %get-tuple-element.120.refs_3_), channel_id=1, source_target_pairs={{0,4},{1,5},{2,6},{3,7},{4,0},{5,1},{6,2},{7,3},{8,12},{9,13},{10,... | collective-permute-start | bytes 2359304 | tf_op jit(solution)/shard_map/ppermute | solution.py:124
  14.1 1.6 collective-permute-start.3
  15.7 15.4 %collective-permute-done.1.refs_5_ = bf16[256,1536]{1,0:T(8,128)(2,1)} collective-permute-done((bf16[256,1536]{1,0:T(8,128)(2,1)}, bf16[256,1536]{1,0:T(8,128)(2,1)}, u32[]{:S(2)}, u32[]{:S(2)}) %collective-permute-start.1) | collective-permute-done | bytes 786464 | tf_op jit(solution)/shard_map/ppermute | solution.py:124
  31.0 1.4 collective-permute-done.refs_4_
  33.3 0.9 copy-done.6
  35.3 1.6 collective-permute-start.10
  36.9 1.2 collective-permute-start.8
  38.1 1.3 collective-permute-start.9
  39.4 1.6 collective-permute-start.11
  40.9 18.1 %collective-permute-done.9 = bf16[256,1536]{1,0:T(8,128)(2,1)} collective-permute-done((bf16[256,1536]{1,0:T(8,128)(2,1)}, bf16[256,1536]{1,0:T(8,128)(2,1)}, u32[]{:S(2)}, u32[]{:S(2)}) %collective-permute-start.9) | collective-permute-done | bytes 786464 | tf_op jit(solution)/shard_map/ppermute | solution.py:124
  59.0 1.2 broadcast_select_fusion.1.refs_3_
  60.3 1.1 collective-permute-start.14
  61.4 1.0 copy-done.13
  62.3 1.3 collective-permute-start.15
  63.6 1.6 collective-permute-start.16
  65.2 3.2 %collective-permute-start.18 = (f32[4,16,256]{2,1,0:T(8,128)S(1)}, f32[4,16,256]{2,1,0:T(8,128)S(1)}, u32[]{:S(2)}, u32[]{:S(2)}) collective-permute-start(f32[4,16,256]{2,1,0:T(8,128)S(1)} %pad_maximum_fusion), channel_id=1, source_target_pairs={{0,8},{1,9},{2,10},{3,11},{8,0},{9,1},{10,2},{11,3},{4,12},{5,13},... | collective-permute-start | bytes 196616 | tf_op jit(solution)/shard_map/ppermute | solution.py:124
  68.4 2.9 %collective-permute-done.18.refs_2_ = f32[4,16,256]{2,1,0:T(8,128)S(1)} collective-permute-done((f32[4,16,256]{2,1,0:T(8,128)S(1)}, f32[4,16,256]{2,1,0:T(8,128)S(1)}, u32[]{:S(2)}, u32[]{:S(2)}) %collective-permute-start.18) | collective-permute-done | bytes 65568 | tf_op jit(solution)/shard_map/ppermute | solution.py:124
  71.3 6.7 %collective-permute-done.14.refs_4_ = bf16[256,1536]{1,0:T(8,128)(2,1)S(1)} collective-permute-done((bf16[256,1536]{1,0:T(8,128)(2,1)S(1)}, bf16[256,1536]{1,0:T(8,128)(2,1)S(1)}, u32[]{:S(2)}, u32[]{:S(2)}) %collective-permute-start.14) | collective-permute-done | bytes 786464 | tf_op jit(solution)/shard_map/ppermute | solution.py:124
  78.9 4.3 %collective-permute-done.15 = bf16[256,1536]{1,0:T(8,128)(2,1)S(1)} collective-permute-done((bf16[256,1536]{1,0:T(8,128)(2,1)}, bf16[256,1536]{1,0:T(8,128)(2,1)S(1)}, u32[]{:S(2)}, u32[]{:S(2)}) %collective-permute-start.15) | collective-permute-done | bytes 786464 | tf_op jit(solution)/shard_map/ppermute | solution.py:124
  84.1 1.0 broadcast_select_fusion.refs_3_
  85.0 1.0 collective-permute-start.19
  86.7 1.1 copy-done.4
  87.8 1.1 copy-done.7
  89.0 1.1 copy-done.10
  90.1 1.1 copy-done.18
  91.2 13.7 %experts_sc_tb_ta.1 = (bf16[256,1536]{1,0:T(8,128)(2,1)S(1)}, bf16[256,1536]{1,0:T(8,128)(2,1)S(1)}, bf16[256,1536]{1,0:T(8,128)(2,1)S(1)}) custom-call(s32[5]{0:T(128)S(1)} %stack.43.scalars, f32[2,16,256]{2,1,0:T(8,128)S(1)} %pad_maximum_fusion.1.refs_0_, f32[2,16,256]{2,1,0:T(8,128)S(1)} %collective-permute-done.13.refs_1_, ...), custom_call_target="tpu_custom_call" | custom-call | flops 7247757312 | bytes 9437184 | tf_op jit(solution)/shard_map/experts_sc_tb_ta/pallas_call | solution.py:201
  105.3 5.7 %experts_tc.1 = bf16[256,1536]{1,0:T(8,128)(2,1)S(1)} custom-call(s32[5]{0:T(128)S(1)} %stack.43.scalars, f32[2,16,256]{2,1,0:T(8,128)S(1)} %pad_maximum_fusion.1.refs_0_, f32[2,16,256]{2,1,0:T(8,128)S(1)} %collective-permute-done.13.refs_1_, f32[4,16,256]{2,1,0:T(8,128)S(1)} %collective-permute-done.18.refs_2_, ...), custom_call_target="tpu_custom_call" | custom-call | flops 2415919104 | bytes 9437184 | tf_op jit(solution)/shard_map/experts_tc/pallas_call | solution.py:201
  111.1 1.1 collective-permute-start.21
  112.2 13.1 %experts_sb_t0_sa.1 = (bf16[256,1536]{1,0:T(8,128)(2,1)S(1)}, bf16[256,1536]{1,0:T(8,128)(2,1)S(1)}, bf16[256,1536]{1,0:T(8,128)(2,1)S(1)}) custom-call(s32[5]{0:T(128)S(1)} %stack.43.scalars, f32[2,16,256]{2,1,0:T(8,128)S(1)} %pad_maximum_fusion.1.refs_0_, f32[2,16,256]{2,1,0:T(8,128)S(1)} %collective-permute-done.13.refs_1_, ...), custom_call_target="tpu_custom_call" | custom-call | flops 7247757312 | bytes 9437184 | tf_op jit(solution)/shard_map/experts_sb_t0_sa/pallas_call | solution.py:201
  125.3 5.0 %collective-permute-done.21 = bf16[256,1536]{1,0:T(8,128)(2,1)S(1)} collective-permute-done((bf16[256,1536]{1,0:T(8,128)(2,1)S(1)}, bf16[256,1536]{1,0:T(8,128)(2,1)S(1)}, u32[]{:S(2)}, u32[]{:S(2)}) %collective-permute-start.21) | collective-permute-done | bytes 786464 | tf_op jit(solution)/shard_map/ppermute | solution.py:124
  130.5 3.8 %collective-permute-start.23 = (bf16[256,1536]{1,0:T(8,128)(2,1)S(1)}, bf16[256,1536]{1,0:T(8,128)(2,1)S(1)}, u32[]{:S(2)}, u32[]{:S(2)}) collective-permute-start(bf16[256,1536]{1,0:T(8,128)(2,1)S(1)} %add_convert_fusion.5), channel_id=1, source_target_pairs={{0,4},{1,5},{2,6},{3,7},{12,8},{13,9},{14,10},{15,11},{16,20},{17,... | collective-permute-start | bytes 2359304 | tf_op jit(solution)/shard_map/ppermute | solution.py:124
  134.3 1.1 collective-permute-start.22
  135.4 5.3 %experts_s0.1 = bf16[256,1536]{1,0:T(8,128)(2,1)S(1)} custom-call(s32[5]{0:T(128)S(1)} %stack.43.scalars, f32[2,16,256]{2,1,0:T(8,128)S(1)} %pad_maximum_fusion.1.refs_0_, f32[2,16,256]{2,1,0:T(8,128)S(1)} %collective-permute-done.13.refs_1_, f32[4,16,256]{2,1,0:T(8,128)S(1)} %collective-permute-done.18.refs_2_, bf16[256,1536]{1,0:T(8,128)(2,1)S(1)} %copy-done.12, ...), custom_call_target="tpu_custom_call" | custom-call | flops 2415919104 | bytes 9437184 | tf_op jit(solution)/shard_map/experts_s0/pallas_call | solution.py:201
  140.8 9.1 %collective-permute-done.23 = bf16[256,1536]{1,0:T(8,128)(2,1)S(1)} collective-permute-done((bf16[256,1536]{1,0:T(8,128)(2,1)S(1)}, bf16[256,1536]{1,0:T(8,128)(2,1)S(1)}, u32[]{:S(2)}, u32[]{:S(2)}) %collective-permute-start.23) | collective-permute-done | bytes 786464 | tf_op jit(solution)/shard_map/ppermute | solution.py:124
  149.9 2.6 %collective-permute-done.22 = bf16[256,1536]{1,0:T(8,128)(2,1)S(1)} collective-permute-done((bf16[256,1536]{1,0:T(8,128)(2,1)S(1)}, bf16[256,1536]{1,0:T(8,128)(2,1)S(1)}, u32[]{:S(2)}, u32[]{:S(2)}) %collective-permute-start.22) | collective-permute-done | bytes 786464 | tf_op jit(solution)/shard_map/ppermute | solution.py:124
  153.3 1.1 collective-permute-start.24
  154.6 4.6 %collective-permute-start.26 = (bf16[256,1536]{1,0:T(8,128)(2,1)S(1)}, bf16[256,1536]{1,0:T(8,128)(2,1)S(1)}, u32[]{:S(2)}, u32[]{:S(2)}) collective-permute-start(bf16[256,1536]{1,0:T(8,128)(2,1)S(1)} %add_convert_fusion.3), channel_id=1, source_target_pairs={{0,4},{1,5},{2,6},{3,7},{12,8},{13,9},{14,10},{15,11},{16,20},{17,... | collective-permute-start | bytes 2359304 | tf_op jit(solution)/shard_map/ppermute | solution.py:124
  159.2 11.3 %collective-permute-done.24 = bf16[256,1536]{1,0:T(8,128)(2,1)S(1)} collective-permute-done((bf16[256,1536]{1,0:T(8,128)(2,1)S(1)}, bf16[256,1536]{1,0:T(8,128)(2,1)S(1)}, u32[]{:S(2)}, u32[]{:S(2)}) %collective-permute-start.24) | collective-permute-done | bytes 786464 | tf_op jit(solution)/shard_map/ppermute | solution.py:124
  170.5 3.0 %collective-permute-done.26 = bf16[256,1536]{1,0:T(8,128)(2,1)S(1)} collective-permute-done((bf16[256,1536]{1,0:T(8,128)(2,1)S(1)}, bf16[256,1536]{1,0:T(8,128)(2,1)S(1)}, u32[]{:S(2)}, u32[]{:S(2)}) %collective-permute-start.26) | collective-permute-done | bytes 786464 | tf_op jit(solution)/shard_map/ppermute | solution.py:124
  174.5 0.9 collective-permute-start.27
  175.7 4.4 %collective-permute-start.29 = (bf16[256,1536]{1,0:T(8,128)(2,1)S(1)}, bf16[256,1536]{1,0:T(8,128)(2,1)S(1)}, u32[]{:S(2)}, u32[]{:S(2)}) collective-permute-start(bf16[256,1536]{1,0:T(8,128)(2,1)S(1)} %add_convert_fusion.1), channel_id=1, source_target_pairs={{0,4},{1,5},{2,6},{3,7},{4,0},{5,1},{6,2},{7,3},{8,12},{9,13},{10,... | collective-permute-start | bytes 2359304 | tf_op jit(solution)/shard_map/ppermute | solution.py:124
  180.2 10.3 %collective-permute-done.27 = bf16[256,1536]{1,0:T(8,128)(2,1)S(1)} collective-permute-done((bf16[256,1536]{1,0:T(8,128)(2,1)S(1)}, bf16[256,1536]{1,0:T(8,128)(2,1)S(1)}, u32[]{:S(2)}, u32[]{:S(2)}) %collective-permute-start.27) | collective-permute-done | bytes 786464 | tf_op jit(solution)/shard_map/ppermute | solution.py:124
  190.5 3.3 %collective-permute-done.29 = bf16[256,1536]{1,0:T(8,128)(2,1)S(1)} collective-permute-done((bf16[256,1536]{1,0:T(8,128)(2,1)S(1)}, bf16[256,1536]{1,0:T(8,128)(2,1)S(1)}, u32[]{:S(2)}, u32[]{:S(2)}) %collective-permute-start.29) | collective-permute-done | bytes 786464 | tf_op jit(solution)/shard_map/ppermute | solution.py:124
  193.7 1.4 add_convert_fusion
  (70 shorter events, 9.1 us)
Async XLA Ops:
  0.0 14.1 %copy-start = (bf16[1,768,512]{2,1,0:T(8,128)(2,1)S(1)}, bf16[1,768,512]{2,1,0:T(8,128)(2,1)}, u32[]{:S(2)}) copy-start(bf16[1,768,512]{2,1,0:T(8,128)(2,1)} %param.13) | copy-start | bytes 2359300
  5.0 9.1 %collective-permute-start.6 = (bf16[768,512]{1,0:T(8,128)(2,1)}, bf16[768,512]{1,0:T(8,128)(2,1)S(1)}, u32[]{:S(2)}, u32[]{:S(2)}) collective-permute-start(bf16[768,512]{1,0:T(8,128)(2,1)} %bitcast.19), channel_id=1, source_target_pairs={{0,1},{1,0},{2,3},{3,2},{4,5},{5,4},{6,7},{7,6},{8,9},{9,8},{10,11... | collective-permute-start | bytes 2359304 | tf_op jit(solution)/shard_map/ppermute | solution.py:124
  5.4 8.7 %collective-permute-start.7 = (bf16[512,768]{1,0:T(8,128)(2,1)}, bf16[512,768]{1,0:T(8,128)(2,1)S(1)}, u32[]{:S(2)}, u32[]{:S(2)}) collective-permute-start(bf16[512,768]{1,0:T(8,128)(2,1)} %bitcast.25), channel_id=1, source_target_pairs={{0,1},{1,0},{2,3},{3,2},{4,5},{5,4},{6,7},{7,6},{8,9},{9,8},{10,11... | collective-permute-start | bytes 2359304 | tf_op jit(solution)/shard_map/ppermute | solution.py:124
  5.5 8.1 %collective-permute-start.4 = (f32[16,256]{1,0:T(8,128)}, f32[16,256]{1,0:T(8,128)S(1)}, u32[]{:S(2)}, u32[]{:S(2)}) collective-permute-start(f32[16,256]{1,0:T(8,128)} %get-tuple-element.74), channel_id=1, source_target_pairs={{0,2},{1,3},{2,0},{3,1},{4,6},{5,7},{6,4},{7,5},{8,10},{9,11},{10,... | collective-permute-start | bytes 49160 | tf_op jit(solution)/shard_map/ppermute | solution.py:124
  8.5 7.2 %collective-permute-start.2 = (bf16[256,1536]{1,0:T(8,128)(2,1)}, bf16[256,1536]{1,0:T(8,128)(2,1)}, u32[]{:S(2)}, u32[]{:S(2)}) collective-permute-start(bf16[256,1536]{1,0:T(8,128)(2,1)} %get-tuple-element.120.refs_3_), channel_id=1, source_target_pairs={{4,8},{5,9},{6,10},{7,11},{8,4},{9,5},{10,6},{11,7},{20,24},{21,25... | collective-permute-start | bytes 2359304 | tf_op jit(solution)/shard_map/ppermute | solution.py:124
  10.0 21.1 %collective-permute-start.1 = (bf16[256,1536]{1,0:T(8,128)(2,1)}, bf16[256,1536]{1,0:T(8,128)(2,1)}, u32[]{:S(2)}, u32[]{:S(2)}) collective-permute-start(bf16[256,1536]{1,0:T(8,128)(2,1)} %get-tuple-element.120.refs_3_), channel_id=1, source_target_pairs={{0,4},{1,5},{2,6},{3,7},{4,0},{5,1},{6,2},{7,3},{8,12},{9,13},{10,... | collective-permute-start | bytes 2359304 | tf_op jit(solution)/shard_map/ppermute | solution.py:124
  13.6 18.8 %collective-permute-start = (bf16[256,1536]{1,0:T(8,128)(2,1)}, bf16[256,1536]{1,0:T(8,128)(2,1)S(1)}, u32[]{:S(2)}, u32[]{:S(2)}) collective-permute-start(bf16[256,1536]{1,0:T(8,128)(2,1)} %get-tuple-element.120.refs_3_), channel_id=1, source_target_pairs={{0,2},{1,3},{2,0},{3,1},{4,6},{5,7},{6,4},{7,5},{8,10},{9,11},{10,... | collective-permute-start | bytes 2359304 | tf_op jit(solution)/shard_map/ppermute | solution.py:124
  14.1 19.2 %collective-permute-start.5 = (bf16[768,512]{1,0:T(8,128)(2,1)S(1)}, bf16[768,512]{1,0:T(8,128)(2,1)S(1)}, u32[]{:S(2)}, u32[]{:S(2)}) collective-permute-start(bf16[768,512]{1,0:T(8,128)(2,1)S(1)} %bitcast.13), channel_id=1, source_target_pairs={{0,1},{1,0},{2,3},{3,2},{4,5},{5,4},{6,7},{7,6},{8,9},{9,8},{10,11... | collective-permute-start | bytes 2359304 | tf_op jit(solution)/shard_map/ppermute | solution.py:124
  14.1 46.1 %copy-start.3 = (bf16[512,768]{1,0:T(8,128)(2,1)}, bf16[512,768]{1,0:T(8,128)(2,1)S(1)}, u32[]{:S(2)}) copy-start(bf16[512,768]{1,0:T(8,128)(2,1)S(1)} %collective-permute-done.7.refs_16_.refs_14_) | copy-start | bytes 2359300
  14.1 20.1 %collective-permute-start.3 = (bf16[768,512]{1,0:T(8,128)(2,1)S(1)}, bf16[768,512]{1,0:T(8,128)(2,1)}, u32[]{:S(2)}, u32[]{:S(2)}) collective-permute-start(bf16[768,512]{1,0:T(8,128)(2,1)S(1)} %bitcast.14), channel_id=1, source_target_pairs={{0,16},{16,0},{1,17},{17,1},{2,18},{18,2},{3,19},{19,3},{4,20},{20... | collective-permute-start | bytes 2359304 | tf_op jit(solution)/shard_map/ppermute | solution.py:156
  33.3 0.9 copy-start.6
  34.9 6.0 %collective-permute-start.13 = (f32[2,16,256]{2,1,0:T(8,128)S(1)}, f32[2,16,256]{2,1,0:T(8,128)S(1)}, u32[]{:S(2)}, u32[]{:S(2)}) collective-permute-start(f32[2,16,256]{2,1,0:T(8,128)S(1)} %pad_maximum_fusion.1.refs_0_), channel_id=1, source_target_pairs={{0,4},{1,5},{2,6},{3,7},{4,0},{5,1},{6,2},{7,3},{8,12},{9,13},{10,... | collective-permute-start | bytes 98312 | tf_op jit(solution)/shard_map/ppermute | solution.py:124
  35.3 23.7 %collective-permute-start.10 = (bf16[256,1536]{1,0:T(8,128)(2,1)}, bf16[256,1536]{1,0:T(8,128)(2,1)}, u32[]{:S(2)}, u32[]{:S(2)}) collective-permute-start(bf16[256,1536]{1,0:T(8,128)(2,1)} %collective-permute-done.1.refs_5_), channel_id=1, source_target_pairs={{4,8},{5,9},{6,10},{7,11},{8,4},{9,5},{10,6},{11,7},{20,24},{21,25... | collective-permute-start | bytes 2359304 | tf_op jit(solution)/shard_map/ppermute | solution.py:124
  36.9 22.1 %collective-permute-start.8 = (bf16[256,1536]{1,0:T(8,128)(2,1)}, bf16[256,1536]{1,0:T(8,128)(2,1)}, u32[]{:S(2)}, u32[]{:S(2)}) collective-permute-start(bf16[256,1536]{1,0:T(8,128)(2,1)} %collective-permute-done.1.refs_5_), channel_id=1, source_target_pairs={{0,2},{1,3},{2,0},{3,1},{4,6},{5,7},{6,4},{7,5},{8,10},{9,11},{10,... | collective-permute-start | bytes 2359304 | tf_op jit(solution)/shard_map/ppermute | solution.py:124
  38.1 20.9 %collective-permute-start.9 = (bf16[256,1536]{1,0:T(8,128)(2,1)}, bf16[256,1536]{1,0:T(8,128)(2,1)}, u32[]{:S(2)}, u32[]{:S(2)}) collective-permute-start(bf16[256,1536]{1,0:T(8,128)(2,1)} %collective-permute-done.2), channel_id=1, source_target_pairs={{4,0},{5,1},{6,2},{7,3},{8,12},{9,13},{10,14},{11,15},{20,16},{21,... | collective-permute-start | bytes 2359304 | tf_op jit(solution)/shard_map/ppermute | solution.py:124
  39.4 19.7 %collective-permute-start.11 = (bf16[768,512]{1,0:T(8,128)(2,1)}, bf16[768,512]{1,0:T(8,128)(2,1)}, u32[]{:S(2)}, u32[]{:S(2)}) collective-permute-start(bf16[768,512]{1,0:T(8,128)(2,1)} %bitcast.20), channel_id=1, source_target_pairs={{0,16},{16,0},{1,17},{17,1},{2,18},{18,2},{3,19},{19,3},{4,20},{20... | collective-permute-start | bytes 2359304 | tf_op jit(solution)/shard_map/ppermute | solution.py:166
  40.9 18.1 %collective-permute-start.12 = (bf16[768,512]{1,0:T(8,128)(2,1)}, bf16[768,512]{1,0:T(8,128)(2,1)}, u32[]{:S(2)}, u32[]{:S(2)}) collective-permute-start(bf16[768,512]{1,0:T(8,128)(2,1)} %collective-permute-done.3.refs_7_.refs_5_), channel_id=1, source_target_pairs={{0,1},{1,0},{2,3},{3,2},{4,5},{5,4},{6,7},{7,6},{8,9},{9,8},{10,11... | collective-permute-start | bytes 2359304 | tf_op jit(solution)/shard_map/ppermute | solution.py:124
  40.9 22.7 %copy-start.2 = (bf16[1,512,768]{2,1,0:T(8,128)(2,1)S(1)}, bf16[1,512,768]{2,1,0:T(8,128)(2,1)}, u32[]{:S(2)}) copy-start(bf16[1,512,768]{2,1,0:T(8,128)(2,1)} %param.15) | copy-start | bytes 2359300
  60.3 17.7 %collective-permute-start.14 = (bf16[256,1536]{1,0:T(8,128)(2,1)S(1)}, bf16[256,1536]{1,0:T(8,128)(2,1)S(1)}, u32[]{:S(2)}, u32[]{:S(2)}) collective-permute-start(bf16[256,1536]{1,0:T(8,128)(2,1)S(1)} %broadcast_select_fusion.1.refs_3_), channel_id=1, source_target_pairs={{0,2},{1,3},{2,0},{3,1},{4,6},{5,7},{6,4},{7,5},{8,10},{9,11},{10,... | collective-permute-start | bytes 2359304 | tf_op jit(solution)/shard_map/ppermute | solution.py:124
  61.4 1.0 copy-start.13
  62.3 20.8 %collective-permute-start.15 = (bf16[256,1536]{1,0:T(8,128)(2,1)}, bf16[256,1536]{1,0:T(8,128)(2,1)S(1)}, u32[]{:S(2)}, u32[]{:S(2)}) collective-permute-start(bf16[256,1536]{1,0:T(8,128)(2,1)} %collective-permute-done.10), channel_id=1, source_target_pairs={{4,0},{5,1},{6,2},{7,3},{8,12},{9,13},{10,14},{11,15},{20,16},{21,... | collective-permute-start | bytes 2359304 | tf_op jit(solution)/shard_map/ppermute | solution.py:124
  63.6 19.5 %collective-permute-start.16 = (bf16[512,768]{1,0:T(8,128)(2,1)S(1)}, bf16[512,768]{1,0:T(8,128)(2,1)}, u32[]{:S(2)}, u32[]{:S(2)}) collective-permute-start(bf16[512,768]{1,0:T(8,128)(2,1)S(1)} %bitcast.26), channel_id=1, source_target_pairs={{0,16},{16,0},{1,17},{17,1},{2,18},{18,2},{3,19},{19,3},{4,20},{20... | collective-permute-start | bytes 2359304 | tf_op jit(solution)/shard_map/ppermute | solution.py:177
  65.2 18.0 %collective-permute-start.17 = (bf16[768,512]{1,0:T(8,128)(2,1)}, bf16[768,512]{1,0:T(8,128)(2,1)S(1)}, u32[]{:S(2)}, u32[]{:S(2)}) collective-permute-start(bf16[768,512]{1,0:T(8,128)(2,1)} %collective-permute-done.11.refs_9_.refs_7_), channel_id=1, source_target_pairs={{0,1},{1,0},{2,3},{3,2},{4,5},{5,4},{6,7},{7,6},{8,9},{9,8},{10,11... | collective-permute-start | bytes 2359304 | tf_op jit(solution)/shard_map/ppermute | solution.py:124
  65.2 21.5 %copy-start.1 = (bf16[1,768,512]{2,1,0:T(8,128)(2,1)S(1)}, bf16[1,768,512]{2,1,0:T(8,128)(2,1)}, u32[]{:S(2)}) copy-start(bf16[1,768,512]{2,1,0:T(8,128)(2,1)} %param.14) | copy-start | bytes 2359300
  65.2 6.1 %collective-permute-start.18 = (f32[4,16,256]{2,1,0:T(8,128)S(1)}, f32[4,16,256]{2,1,0:T(8,128)S(1)}, u32[]{:S(2)}, u32[]{:S(2)}) collective-permute-start(f32[4,16,256]{2,1,0:T(8,128)S(1)} %pad_maximum_fusion), channel_id=1, source_target_pairs={{0,8},{1,9},{2,10},{3,11},{8,0},{9,1},{10,2},{11,3},{4,12},{5,13},... | collective-permute-start | bytes 196616 | tf_op jit(solution)/shard_map/ppermute | solution.py:124
  78.0 0.9 copy-start.17
  84.1 2.6 %collective-permute-start.20 = (bf16[512,768]{1,0:T(8,128)(2,1)}, bf16[512,768]{1,0:T(8,128)(2,1)}, u32[]{:S(2)}, u32[]{:S(2)}) collective-permute-start(bf16[512,768]{1,0:T(8,128)(2,1)} %collective-permute-done.16.refs_11_.refs_9_), channel_id=1, source_target_pairs={{0,1},{1,0},{2,3},{3,2},{4,5},{5,4},{6,7},{7,6},{8,9},{9,8},{10,11... | collective-permute-start | bytes 2359304 | tf_op jit(solution)/shard_map/ppermute | solution.py:124
  85.0 20.3 %collective-permute-start.19 = (bf16[256,1536]{1,0:T(8,128)(2,1)}, bf16[256,1536]{1,0:T(8,128)(2,1)}, u32[]{:S(2)}, u32[]{:S(2)}) collective-permute-start(bf16[256,1536]{1,0:T(8,128)(2,1)} %broadcast_select_fusion.refs_3_), channel_id=1, source_target_pairs={{0,2},{1,3},{2,0},{3,1},{4,6},{5,7},{6,4},{7,5},{8,10},{9,11},{10,... | collective-permute-start | bytes 2359304 | tf_op jit(solution)/shard_map/ppermute | solution.py:124
  86.7 1.1 copy-start.4
  87.8 1.1 copy-start.7
  89.0 1.1 copy-start.10
  90.1 1.1 copy-start.18
  91.2 14.1 %copy-start.5 = (bf16[512,768]{1,0:T(8,128)(2,1)S(1)}, bf16[512,768]{1,0:T(8,128)(2,1)}, u32[]{:S(2)}) copy-start(bf16[512,768]{1,0:T(8,128)(2,1)} %copy-done.3) | copy-start | bytes 2359300
  91.2 14.1 %copy-start.8 = (bf16[768,512]{1,0:T(8,128)(2,1)S(1)}, bf16[768,512]{1,0:T(8,128)(2,1)}, u32[]{:S(2)}) copy-start(bf16[768,512]{1,0:T(8,128)(2,1)} %copy-done.6) | copy-start | bytes 2359300
  91.2 14.1 %copy-start.11 = (bf16[768,512]{1,0:T(8,128)(2,1)S(1)}, bf16[768,512]{1,0:T(8,128)(2,1)}, u32[]{:S(2)}) copy-start(bf16[768,512]{1,0:T(8,128)(2,1)} %copy-done.9) | copy-start | bytes 2359300
  105.3 6.8 %copy-start.14 = (bf16[256,1536]{1,0:T(8,128)(2,1)S(1)}, bf16[256,1536]{1,0:T(8,128)(2,1)}, u32[]{:S(2)}) copy-start(bf16[256,1536]{1,0:T(8,128)(2,1)} %copy-done.13) | copy-start | bytes 2359300
  105.3 6.8 %copy-start.16 = (bf16[256,1536]{1,0:T(8,128)(2,1)S(1)}, bf16[256,1536]{1,0:T(8,128)(2,1)}, u32[]{:S(2)}) copy-start(bf16[256,1536]{1,0:T(8,128)(2,1)} %copy-done.15) | copy-start | bytes 2359300
  111.1 19.3 %collective-permute-start.21 = (bf16[256,1536]{1,0:T(8,128)(2,1)S(1)}, bf16[256,1536]{1,0:T(8,128)(2,1)S(1)}, u32[]{:S(2)}, u32[]{:S(2)}) collective-permute-start(bf16[256,1536]{1,0:T(8,128)(2,1)S(1)} %experts_tc.1), channel_id=1, source_target_pairs={{0,2},{1,3},{2,0},{3,1},{4,6},{5,7},{6,4},{7,5},{8,10},{9,11},{10,... | collective-permute-start | bytes 2359304 | tf_op jit(solution)/shard_map/ppermute | solution.py:124
  130.3 5.1 %copy-start.12 = (bf16[256,1536]{1,0:T(8,128)(2,1)S(1)}, bf16[256,1536]{1,0:T(8,128)(2,1)}, u32[]{:S(2)}) copy-start(bf16[256,1536]{1,0:T(8,128)(2,1)} %get-tuple-element.120.refs_3_) | copy-start | bytes 2359300
  130.5 19.3 %collective-permute-start.23 = (bf16[256,1536]{1,0:T(8,128)(2,1)S(1)}, bf16[256,1536]{1,0:T(8,128)(2,1)S(1)}, u32[]{:S(2)}, u32[]{:S(2)}) collective-permute-start(bf16[256,1536]{1,0:T(8,128)(2,1)S(1)} %add_convert_fusion.5), channel_id=1, source_target_pairs={{0,4},{1,5},{2,6},{3,7},{12,8},{13,9},{14,10},{15,11},{16,20},{17,... | collective-permute-start | bytes 2359304 | tf_op jit(solution)/shard_map/ppermute | solution.py:124
  134.3 18.1 %collective-permute-start.22 = (bf16[256,1536]{1,0:T(8,128)(2,1)S(1)}, bf16[256,1536]{1,0:T(8,128)(2,1)S(1)}, u32[]{:S(2)}, u32[]{:S(2)}) collective-permute-start(bf16[256,1536]{1,0:T(8,128)(2,1)S(1)} %get-tuple-element.119), channel_id=1, source_target_pairs={{0,2},{1,3},{2,0},{3,1},{4,6},{5,7},{6,4},{7,5},{8,10},{9,11},{10,... | collective-permute-start | bytes 2359304 | tf_op jit(solution)/shard_map/ppermute | solution.py:124
  152.6 6.6 %collective-permute-start.25 = (bf16[256,1536]{1,0:T(8,128)(2,1)S(1)}, bf16[256,1536]{1,0:T(8,128)(2,1)S(1)}, u32[]{:S(2)}, u32[]{:S(2)}) collective-permute-start(bf16[256,1536]{1,0:T(8,128)(2,1)S(1)} %add_convert_fusion.4), channel_id=1, source_target_pairs={{4,8},{5,9},{6,10},{7,11},{8,4},{9,5},{10,6},{11,7},{20,24},{21,25... | collective-permute-start | bytes 2359304 | tf_op jit(solution)/shard_map/ppermute | solution.py:124
  153.3 17.2 %collective-permute-start.24 = (bf16[256,1536]{1,0:T(8,128)(2,1)S(1)}, bf16[256,1536]{1,0:T(8,128)(2,1)S(1)}, u32[]{:S(2)}, u32[]{:S(2)}) collective-permute-start(bf16[256,1536]{1,0:T(8,128)(2,1)S(1)} %get-tuple-element.123), channel_id=1, source_target_pairs={{0,2},{1,3},{2,0},{3,1},{4,6},{5,7},{6,4},{7,5},{8,10},{9,11},{10,... | collective-permute-start | bytes 2359304 | tf_op jit(solution)/shard_map/ppermute | solution.py:124
  154.6 18.9 %collective-permute-start.26 = (bf16[256,1536]{1,0:T(8,128)(2,1)S(1)}, bf16[256,1536]{1,0:T(8,128)(2,1)S(1)}, u32[]{:S(2)}, u32[]{:S(2)}) collective-permute-start(bf16[256,1536]{1,0:T(8,128)(2,1)S(1)} %add_convert_fusion.3), channel_id=1, source_target_pairs={{0,4},{1,5},{2,6},{3,7},{12,8},{13,9},{14,10},{15,11},{16,20},{17,... | collective-permute-start | bytes 2359304 | tf_op jit(solution)/shard_map/ppermute | solution.py:124
  173.6 20.1 %copy-start.19 = (bf16[256,1536]{1,0:T(8,128)(2,1)S(1)}, bf16[256,1536]{1,0:T(8,128)(2,1)}, u32[]{:S(2)}) copy-start(bf16[256,1536]{1,0:T(8,128)(2,1)} %tokens.1) | copy-start | bytes 2359300
  173.7 6.5 %collective-permute-start.28 = (bf16[256,1536]{1,0:T(8,128)(2,1)S(1)}, bf16[256,1536]{1,0:T(8,128)(2,1)S(1)}, u32[]{:S(2)}, u32[]{:S(2)}) collective-permute-start(bf16[256,1536]{1,0:T(8,128)(2,1)S(1)} %add_convert_fusion.2), channel_id=1, source_target_pairs={{4,8},{5,9},{6,10},{7,11},{8,4},{9,5},{10,6},{11,7},{20,24},{21,25... | collective-permute-start | bytes 2359304 | tf_op jit(solution)/shard_map/ppermute | solution.py:124
  174.5 15.9 %collective-permute-start.27 = (bf16[256,1536]{1,0:T(8,128)(2,1)S(1)}, bf16[256,1536]{1,0:T(8,128)(2,1)S(1)}, u32[]{:S(2)}, u32[]{:S(2)}) collective-permute-start(bf16[256,1536]{1,0:T(8,128)(2,1)S(1)} %get-tuple-element.129), channel_id=1, source_target_pairs={{0,2},{1,3},{2,0},{3,1},{4,6},{5,7},{6,4},{7,5},{8,10},{9,11},{10,... | collective-permute-start | bytes 2359304 | tf_op jit(solution)/shard_map/ppermute | solution.py:124
  175.7 18.0 %collective-permute-start.29 = (bf16[256,1536]{1,0:T(8,128)(2,1)S(1)}, bf16[256,1536]{1,0:T(8,128)(2,1)S(1)}, u32[]{:S(2)}, u32[]{:S(2)}) collective-permute-start(bf16[256,1536]{1,0:T(8,128)(2,1)S(1)} %add_convert_fusion.1), channel_id=1, source_target_pairs={{0,4},{1,5},{2,6},{3,7},{4,0},{5,1},{6,2},{7,3},{8,12},{9,13},{10,... | collective-permute-start | bytes 2359304 | tf_op jit(solution)/shard_map/ppermute | solution.py:124
  (2 other events, 1.8 us)

commit v3 on v1

v3 whole, which is shorter than its diff:
```python
import functools
import jax
import jax.numpy as jnp
from jax import lax
from jax.experimental import pallas as pl
from jax.experimental.pallas import tpu as pltpu
from jax.sharding import PartitionSpec as P

LMAX = 4096
F32 = jnp.float32
BF16 = jnp.bfloat16


def gate_of(logits, routes, lengths, experts):
    rows = logits.shape[0]
    position = lax.axis_index("tensor") * rows + jnp.arange(rows, dtype=jnp.int32)
    living = position % LMAX < lengths[position // LMAX]
    ids = jnp.arange(experts, dtype=jnp.int32)
    named = jnp.zeros((rows, experts), jnp.bool_)
    for k in range(routes.shape[1]):
        named = named | (routes[:, k : k + 1] == ids[None, :])
    return jnp.where(named & living[:, None], jax.nn.sigmoid(logits), 0.0)


def norm_of(tokens_f32, norm_gain):
    scale_rows = lax.rsqrt(jnp.mean(tokens_f32 * tokens_f32, axis=-1, keepdims=True) + 1e-06)
    return (tokens_f32 * scale_rows * norm_gain).astype(BF16)


def dot(a, b):
    return jnp.dot(a, b, preferred_element_type=F32)


def general(tokens, lengths, routes, norm_gain, router, w_gate, w_up, w_down):
    experts = router.shape[1]
    local = w_gate.shape[0]
    tokens_f32 = tokens.astype(F32)
    normed = norm_of(tokens_f32, norm_gain)
    gates = gate_of(dot(normed, router), routes, lengths, experts)
    gate_all = lax.all_gather(w_gate, "dp", axis=1, tiled=True)
    up_all = lax.all_gather(w_up, "dp", axis=1, tiled=True)
    down_all = lax.all_gather(w_down, "dp", axis=2, tiled=True)
    rows_all = lax.all_gather(normed, "tensor", axis=0, tiled=True)
    gates_all = lax.all_gather(gates, "tensor", axis=0, tiled=True)
    first = lax.axis_index("tensor") * local
    total = jnp.zeros(rows_all.shape, F32)
    for x in range(local):
        weight = lax.dynamic_slice_in_dim(gates_all, first + x, 1, axis=1)
        hidden = jax.nn.silu(dot(rows_all, gate_all[x])) * dot(rows_all, up_all[x])
        total = total + dot((hidden * weight).astype(BF16), down_all[x])
    combined = lax.psum_scatter(total.astype(BF16), "tensor", scatter_dimension=0, tiled=True)
    return (tokens_f32 + combined.astype(F32)).astype(BF16)


GATE_ROWS = 16
CHUNK = 256


def prologue_kernel(lengths, tokens, gain, router, routes_t, normed, order):
    v = tokens[...].astype(F32)
    scale_rows = lax.rsqrt(jnp.mean(v * v, axis=-1, keepdims=True) + 1e-06)
    out = (v * scale_rows * gain[...]).astype(BF16)
    rows, width = out.shape
    normed[GATE_ROWS:, :] = out
    logits_t = lax.dot_general(router[...], out, (((1,), (1,)), ((), ())), preferred_element_type=F32)
    ids = lax.broadcasted_iota(jnp.int32, logits_t.shape, 0)
    position = lax.axis_index("tensor") * rows + lax.broadcasted_iota(jnp.int32, logits_t.shape, 1)
    named = routes_t[0:1, :] == ids
    for k in range(1, routes_t.shape[0]):
        named = named | (routes_t[k : k + 1, :] == ids)
    living = position < lengths[0]
    gates = jnp.where(named & living, jax.nn.sigmoid(logits_t), 0.0)
    high = gates.astype(BF16)
    normed[:GATE_ROWS, :rows] = high
    normed[:GATE_ROWS, rows : 2 * rows] = (gates - high.astype(F32)).astype(BF16)
    normed[:GATE_ROWS, 2 * rows :] = jnp.zeros((GATE_ROWS, width - 2 * rows), BF16)
    order[...] = jnp.zeros_like(order)


def pack_kernel(gate, up, down, *packed):
    half = gate.shape[0]
    for h, chunk in enumerate(packed):
        units = slice(CHUNK * h, CHUNK * (h + 1))
        chunk[:, :CHUNK] = gate[:, units]
        chunk[:, CHUNK : 2 * CHUNK] = up[:, units]
        for i in range(half // CHUNK):
            columns = slice(CHUNK * i, CHUNK * (i + 1))
            chunk[columns, 2 * CHUNK :] = down[units, columns]


def expert_kernel(work, based, count, _, *refs):
    blocks, refs = refs[:count], refs[count:]
    bases, refs = (refs[: len(based)], refs[len(based) :])
    used = 4 * len(work)
    weights, refs = refs[:used], refs[used:]
    outs, (taken, weight, hidden, held, arrived) = refs[:count], refs[count:]
    rows, width = outs[0].shape
    half = width // 2
    x = lax.axis_index("dp")
    t = lax.axis_index("tensor")
    starts = (pl.multiple_of(x * half, half), pl.multiple_of((1 - x) * half, half))
    copies = [pltpu.make_async_copy(weights[i], held.at[i], arrived.at[i]) for i in range(used)]
    for copy in copies:
        copy.start()

    eye = lax.broadcasted_iota(jnp.int32, (rows, rows), 0) == lax.broadcasted_iota(jnp.int32, (rows, rows), 1)
    for b in range(count):
        here = pl.ds(b * rows, rows)
        taken[here, :] = blocks[b][GATE_ROWS:, :]
        lines = blocks[b][:GATE_ROWS, :rows].astype(F32) + blocks[b][:GATE_ROWS, rows : 2 * rows].astype(F32)
        ids = lax.broadcasted_iota(jnp.int32, lines.shape, 0)
        for n, (expert, first, last) in enumerate(work):
            if first <= b < last:
                line = jnp.sum(jnp.where(ids == jnp.bitwise_xor(t, 2 * expert), lines, 0.0), axis=0, keepdims=True)
                weight[n, here, :] = jnp.sum(jnp.where(eye, line, 0.0), axis=1, keepdims=True)

    for n, (_, first, last) in enumerate(work):
        here = pl.ds(first * rows, (last - first) * rows)
        near, away = (taken[here, pl.ds(start, half)] for start in starts)
        for h in range(2):
            own, far = 4 * n + 2 * h, 4 * n + 2 * h + 1
            copies[own].wait()
            copies[far].wait()
            gate = dot(near, held[own, :, :CHUNK]) + dot(away, held[far, :, :CHUNK])
            up = dot(near, held[own, :, CHUNK : 2 * CHUNK]) + dot(away, held[far, :, CHUNK : 2 * CHUNK])
            units = slice(CHUNK * h, CHUNK * (h + 1))
            hidden[n, here, units] = (jax.nn.silu(gate) * up * weight[n, here, :]).astype(BF16)

    edges = sorted({0, count}.union(*({first, last} for _, first, last in work)))
    for begin, end in zip(edges[:-1], edges[1:]):
        here = pl.ds(begin * rows, (end - begin) * rows)
        for side in range(2):
            for i in range(half // CHUNK):
                columns = pl.ds(pl.multiple_of(starts[side] + CHUNK * i, CHUNK), CHUNK)
                value = sum(
                    dot(hidden[n, here, CHUNK * h : CHUNK * (h + 1)], held[4 * n + 2 * h + side, CHUNK * i : CHUNK * (i + 1), 2 * CHUNK :])
                    for n, (_, first, last) in enumerate(work)
                    if first <= begin < last
                    for h in range(2)
                )
                for b in range(begin, end):
                    part = value[(b - begin) * rows : (b - begin + 1) * rows]
                    if b in based:
                        part = part + bases[based.index(b)][:, columns].astype(F32)
                    outs[b][:, columns] = part.astype(BF16)


def lanes(tokens, lengths, routes, norm_gain, router, w_gate, w_up, w_down):
    rows, width = tokens.shape
    half = width // 2
    hid = w_gate.shape[2]
    z = lax.axis_index("tensor") // 4
    middle = (z == 1) | (z == 2)

    def send(v, pairs):
        return lax.ppermute(v, "tensor", pairs)

    def across(v):
        return lax.ppermute(v, "dp", [(0, 1), (1, 0)])

    def over(*pairs):
        return [(a * 4 + r, b * 4 + r) for a, b in pairs for r in range(4)]

    by_core, by_y = ([(i, i ^ bit) for i in range(16)] for bit in (1, 2))
    outer = over((0, 1), (1, 0), (2, 3), (3, 2))
    inner = over((1, 2), (2, 1))
    outward = over((1, 0), (2, 3))
    inward = over((0, 1), (3, 2))
    smem = pl.BlockSpec(memory_space=pltpu.SMEM)
    vmem = pl.BlockSpec(memory_space=pltpu.VMEM)
    anywhere = pl.BlockSpec(memory_space=pl.ANY)

    own = pl.pallas_call(
        pack_kernel,
        out_shape=(jax.ShapeDtypeStruct((half, half), BF16),) * (hid // CHUNK),
        in_specs=[vmem] * 3,
        out_specs=(vmem,) * (hid // CHUNK),
        name="pack",
    )(w_gate[0], w_up[0], w_down[0])
    x_0 = across(own[0])
    y_1 = send(own[1], by_y)
    s_0, begin = pl.pallas_call(
        prologue_kernel,
        out_shape=(jax.ShapeDtypeStruct((rows + GATE_ROWS, width), BF16), jax.ShapeDtypeStruct((8, 128), F32)),
        in_specs=[smem] + [vmem] * 4,
        out_specs=(vmem,) * 2,
        name="prologue",
    )(lengths, tokens, norm_gain.reshape(1, width), router.T, routes.T)

    order = [begin]

    def together(*values):
        *values, order[0] = lax.optimization_barrier((*values, order[0]))
        return values

    def run(shards, work, bases):
        count = len(shards)
        based = tuple(b for b, base in enumerate(bases) if base is not None)
        used = 4 * len(work)
        return pl.pallas_call(
            functools.partial(expert_kernel, tuple((e, first, last) for e, _, first, last in work), based, count),
            out_shape=tuple(jax.ShapeDtypeStruct((rows, width), BF16) for _ in shards),
            in_specs=[anywhere] + [vmem] * (count + len(based)) + [anywhere] * used,
            out_specs=(vmem,) * count,
            scratch_shapes=[
                pltpu.VMEM((count * rows, width), BF16),
                pltpu.VMEM((len(work), count * rows, 1), F32),
                pltpu.VMEM((len(work), count * rows, 2 * CHUNK), BF16),
                pltpu.VMEM((used, half, half), BF16),
                pltpu.SemaphoreType.DMA((used,)),
            ],
            compiler_params=pltpu.CompilerParams(vmem_limit_bytes=36 * 2**20),
            cost_estimate=pl.CostEstimate(flops=1, bytes_accessed=1, transcendentals=0),
            name="experts",
        )(order[0], *shards, *(bases[b] for b in based), *(w for _, ws, _, _ in work for w in ws))

    def add(*terms):
        return sum(v.astype(F32) for v in terms).astype(BF16)

    s_m = send(s_0, inner)
    s_a = send(s_0, outer)
    m_0 = send(s_0, by_core)
    x_0, y_1, own_0, own_1 = together(x_0, y_1, *own)
    x_1 = across(own_1)
    y_0 = send(own_0, by_y)
    s_m, s_a, m_0 = together(s_m, s_a, m_0)
    s_b = send(s_m, outward)
    s_n = send(s_a, inner)
    m_a = send(s_a, by_core)
    x_1, y_0, x_0, y_1 = together(x_1, y_0, x_0, y_1)
    d_0 = send(x_0, by_y)
    d_1 = across(y_1)
    s_b, s_n, m_a = together(s_b, s_n, m_a)
    s_c = send(s_n, outward)
    s_b = jnp.where(middle, s_m, s_b)
    m_b = send(s_b, by_core)
    mine = (own[0], x_0, own[1], x_1)
    u_0, v_0, u_a, v_a = run((s_0, m_0, s_a, m_a), [(0, mine, 0, 4)], [None] * 4)
    m_b, u_0, v_0, u_a, v_a = together(m_b, u_0, v_0, u_a, v_a)
    u_b, v_b = run((s_b, m_b), [(0, mine, 0, 2)], [None] * 2)
    s_c, u_b, v_b = together(s_c, u_b, v_b)
    s_c = jnp.where(middle, s_n, s_c)
    m_c = send(s_c, by_core)
    (m_c,) = together(m_c)
    u_c, v_c = run((s_c, m_c), [(0, mine, 0, 2)], [None] * 2)
    d_0, d_1, u_c, v_c = together(d_0, d_1, u_c, v_c)
    theirs = (y_0, d_0, y_1, d_1)
    p_c, o_c = run((s_c, m_c), [(1, theirs, 0, 2)], [u_c, v_c])
    r_c = send(o_c, by_core)

    r_c, p_c = together(r_c, p_c)
    q_c = add(p_c, r_c)
    r_n = send(q_c, inward)
    p_b, o_b, p_a, o_a, p_0, o_0 = run((s_b, m_b, s_a, m_a, s_0, m_0), [(1, theirs, 0, 6)], [u_b, v_b, u_a, v_a, u_0, v_0])
    r_b, r_a, r_0 = send(o_b, by_core), send(o_a, by_core), send(o_0, by_core)
    r_b, r_a, r_0, r_n, p_b, p_a = together(r_b, r_a, r_0, r_n, p_b, p_a)
    q_b = add(p_b, r_b)
    r_m = send(q_b, inward)
    r_i = send(add(q_c, r_n), inner)
    r_m, r_i = together(r_m, r_i)
    r_o = send(add(p_a, r_a, r_i), outer)
    r_m = send(add(q_b, r_m), inner)
    return add(tokens, p_0, r_0, r_o, r_m)


def solution(mesh):
    placed = (
        P(("dp", "tensor"), None),
        P("dp"),
        P(("dp", "tensor"), None),
        P(),
        P(),
        P("tensor", "dp", None),
        P("tensor", "dp", None),
        P("tensor", None, "dp"),
    )

    def shards(*args):
        fits = mesh.shape["dp"] == 2 and mesh.shape["tensor"] == 16 and args[5].shape[0] == 1
        fits = fits and args[1].shape[0] == 1 and args[0].shape[0] == 256 and args[4].shape[1] == GATE_ROWS
        fits = fits and args[5].shape[2] == 512 and args[0].shape[1] == 1536
        return (lanes if fits else general)(*args)

    return jax.shard_map(
        shards, mesh=mesh, in_specs=placed, out_specs=P(("dp", "tensor"), None), check_vma=False
    )
```

time: 267 us -> 169 us (0.63)
  matrix products: 78.4 us -> 0 us
  Pallas kernels: 0 us -> 36.9 us
  blocking collectives: 30.9 us -> 0 us
  local copies, waits for them, and re-layouts: 26 us -> 3.83 us
  other arithmetic: 24.2 us -> 3.82 us
  waiting for transfers between devices: 78 us -> 86.8 us
  starting transfers between devices: 28.1 us -> 34.9 us
    dot_general x17 -> x0, matrix products: 78.4 us -> none  [dot(): return jnp.dot(a, b, preferred_element_type=F32)]
    pallas_call x0 -> x7, Pallas kernels: none -> 36.9 us  [the longest x5 31.2 us: run(): pl.pallas_call(functools.partial(expert_kernel, tuple(((e, first, last) f...]
    ppermute x2 -> x3, waiting for transfers between devices: 0.01 us -> 36.9 us  [across(): return lax.ppermute(v, 'dp', [(0, 1), (1, 0)])]
    all_gather x1 -> x0, blocking collectives: 30.9 us -> none  [lanes(): gates_all = lax.all_gather(gates.T, 'tensor', axis=0)]
    ppermute x22 -> x21, waiting for transfers between devices: 78 us -> 49.9 us  [send(): return lax.ppermute(v, 'tensor', pairs)]
    concatenate x2 -> x0, other arithmetic: 15.4 us -> none  [the longest x1 12.7 us: lanes(): jnp.concatenate([jnp.concatenate([p[:, :hid] for p in e], axis=0) for e i...]
    unnamed x54 -> x22, local copies, waits for them, and re-layouts: 11.5 us -> 3.24 us
    ppermute x22 -> x21, starting transfers between devices: 24.6 us -> 30.2 us  [send(): return lax.ppermute(v, 'tensor', pairs)]
  transfers between devices with their start and end apart: 24 -> 24, of which waited for: 8 -> 13; matrix products, arithmetic and copies ran while one was open for 43% -> 1% of each run, Pallas kernels for 0% -> 18%
where the time goes in v3:
time: 169 us; the launch traced here: 167 us
  waiting for transfers between devices  86.8 us (51%)
  Pallas kernels  36.9 us (22%)
  starting transfers between devices  34.9 us (21%)
  local copies, waits for them, and re-layouts  3.83 us (2%)
  other arithmetic  3.82 us (2%)
    ppermute x21, waiting for transfers between devices, send(): return lax.ppermute(v, 'tensor', pairs)  49.9 us
    ppermute x3, waiting for transfers between devices, across(): return lax.ppermute(v, 'dp', [(0, 1), (1, 0)])  36.9 us
    pallas_call x5, Pallas kernels, run(): pl.pallas_call(functools.partial(expert_kernel, tuple(((e, first, last) f...  31.2 us
    ppermute x21, starting transfers between devices, send(): return lax.ppermute(v, 'tensor', pairs)  30.2 us
    ppermute x3, starting transfers between devices, across(): return lax.ppermute(v, 'dp', [(0, 1), (1, 0)])  4.74 us
  transfers between devices with their start and end apart: 24, of which 13 were waited for; matrix products, arithmetic and copies ran while one was open for 1% of the time, Pallas kernels for 18%

profile of v3, /device:TPU:0, one launch (start us, length us, event | category | flops | bytes accessed | tf_op | source)
XLA Modules:
  0.0 167.2 jit_solution(7541357026820445352)
XLA Ops:
  0.0 3.1 %pack.1 = (bf16[768,768]{1,0:T(8,128)(2,1)}, bf16[768,768]{1,0:T(8,128)(2,1)}) custom-call(bf16[768,512]{1,0:T(8,128)(2,1)} %bitcast.5, bf16[768,512]{1,0:T(8,128)(2,1)} %bitcast.6, bf16[512,768]{1,0:T(8,128)(2,1)} %bitcast.7), custom_call_target="tpu_custom_call" | custom-call | tf_op jit(solution)/shard_map/pack/pallas_call | solution.py:173
  3.1 2.9 %collective-permute-start = (bf16[768,768]{1,0:T(8,128)(2,1)}, bf16[768,768]{1,0:T(8,128)(2,1)S(1)}, u32[]{:S(2)}, u32[]{:S(2)}) collective-permute-start(bf16[768,768]{1,0:T(8,128)(2,1)} %get-tuple-element.75.refs_4_.refs_2_), channel_id=1, source_target_pairs={{0,16},{16,0},{1,17},{17,1},{2,18},{18,2},{3,19},{19,3},{4,20},{20... | collective-permute-start | bytes 3538952 | tf_op jit(solution)/shard_map/ppermute | solution.py:159
  6.0 1.5 collective-permute-start.1
  7.5 0.6 reshape.3.gain
  8.8 2.6 %prologue.1 = (bf16[272,1536]{1,0:T(8,128)(2,1)}, f32[8,128]{1,0:T(8,128)}) custom-call(s32[1]{0:T(128)S(6)} %copy.9.lengths, bf16[256,1536]{1,0:T(8,128)(2,1)} %tokens.1, f32[1,1536]{1,0:T(1,128)} %reshape.3.gain, bf16[16,1536]{1,0:T(8,128)(2,1)} %bitcast.8, s32[8,256]{1,0:T(8,128)} %bitcast.9), custom_call_target="tpu_custom_call" | custom-call | tf_op jit(solution)/shard_map/prologue/pallas_call | solution.py:182
  11.4 1.6 collective-permute-start.4
  13.0 3.5 %collective-permute-start.5 = (bf16[272,1536]{1,0:T(8,128)(2,1)}, bf16[272,1536]{1,0:T(8,128)(2,1)}, u32[]{:S(2)}, u32[]{:S(2)}) collective-permute-start(bf16[272,1536]{1,0:T(8,128)(2,1)} %get-tuple-element.78.refs_0_.refs_4_), channel_id=1, source_target_pairs={{0,4},{1,5},{2,6},{3,7},{4,0},{5,1},{6,2},{7,3},{8,12},{9,13},{10,... | collective-permute-start | bytes 2506760 | tf_op jit(solution)/shard_map/ppermute | solution.py:156
  16.5 15.7 %collective-permute-done.refs_5_.refs_3_ = bf16[768,768]{1,0:T(8,128)(2,1)S(1)} collective-permute-done((bf16[768,768]{1,0:T(8,128)(2,1)}, bf16[768,768]{1,0:T(8,128)(2,1)S(1)}, u32[]{:S(2)}, u32[]{:S(2)}) %collective-permute-start) | collective-permute-done | bytes 1179680 | tf_op jit(solution)/shard_map/ppermute | solution.py:159
  32.2 1.5 collective-permute-done.1.refs_6_.refs_14_
  33.7 0.3 collective-permute-start.2
  34.0 1.7 %collective-permute-start.3 = (bf16[768,768]{1,0:T(8,128)(2,1)}, bf16[768,768]{1,0:T(8,128)(2,1)}, u32[]{:S(2)}, u32[]{:S(2)}) collective-permute-start(bf16[768,768]{1,0:T(8,128)(2,1)} %get-tuple-element.75.refs_4_.refs_2_), channel_id=1, source_target_pairs={{0,2},{1,3},{2,0},{3,1},{4,6},{5,7},{6,4},{7,5},{8,10},{9,11},{10,... | collective-permute-start | bytes 3538952 | tf_op jit(solution)/shard_map/ppermute | solution.py:156
  35.7 0.9 copy-done.5
  36.6 1.6 collective-permute-start.10
  38.2 1.3 collective-permute-start.9
  39.6 20.9 %collective-permute-done.2.refs_7_.refs_5_ = bf16[768,768]{1,0:T(8,128)(2,1)S(1)} collective-permute-done((bf16[768,768]{1,0:T(8,128)(2,1)}, bf16[768,768]{1,0:T(8,128)(2,1)S(1)}, u32[]{:S(2)}, u32[]{:S(2)}) %collective-permute-start.2) | collective-permute-done | bytes 1179680 | tf_op jit(solution)/shard_map/ppermute | solution.py:159
  60.5 0.5 collective-permute-done.3.refs_4_.refs_12_
  61.0 1.7 collective-permute-done.9
  62.6 1.2 broadcast_select_fusion.1.refs_0_
  63.9 1.3 collective-permute-start.12
  65.2 0.6 collective-permute-start.7
  65.8 1.5 collective-permute-start.8
  67.3 1.1 copy-done.3
  68.5 1.1 copy-done.6
  69.6 8.1 %experts.5 = (bf16[256,1536]{1,0:T(8,128)(2,1)S(1)}, bf16[256,1536]{1,0:T(8,128)(2,1)S(1)}, bf16[256,1536]{1,0:T(8,128)(2,1)S(1)}, bf16[256,1536]{1,0:T(8,128)(2,1)S(1)}) custom-call(f32[8,128]{1,0:T(8,128)S(1)} %copy-done.8, bf16[272,1536]{1,0:T(8,128)(2,1)S(1)} %copy-done.3, bf16[272,1536]{1,0:T(8,128)(2,1)S(1)} %copy-done.6, ...), custom_call_target="tpu_custom_call" | custom-call | flops 1 | bytes 1 | tf_op jit(solution)/shard_map/experts/pallas_call | solution.py:200
  77.8 4.0 %experts.6 = (bf16[256,1536]{1,0:T(8,128)(2,1)S(1)}, bf16[256,1536]{1,0:T(8,128)(2,1)S(1)}) custom-call(f32[8,128]{1,0:T(8,128)S(1)} %copy-done.8, bf16[272,1536]{1,0:T(8,128)(2,1)S(1)} %broadcast_select_fusion.1.refs_0_, bf16[272,1536]{1,0:T(8,128)(2,1)S(1)} %collective-permute-done.13.refs_1_, bf16[768,768]{1,0:T(8,128)(2,1)S(1)} %copy-done, ...), custom_call_target="tpu_custom_call" | custom-call | flops 1 | bytes 1 | tf_op jit(solution)/shard_map/experts/pallas_call | solution.py:200
  81.8 5.2 %collective-permute-done.12 = bf16[272,1536]{1,0:T(8,128)(2,1)S(1)} collective-permute-done((bf16[272,1536]{1,0:T(8,128)(2,1)}, bf16[272,1536]{1,0:T(8,128)(2,1)S(1)}, u32[]{:S(2)}, u32[]{:S(2)}) %collective-permute-start.12) | collective-permute-done | bytes 835616 | tf_op jit(solution)/shard_map/ppermute | solution.py:156
  87.0 0.1 broadcast_select_fusion.refs_0_
  87.2 2.3 %collective-permute-done.14.refs_1_ = bf16[272,1536]{1,0:T(8,128)(2,1)S(1)} collective-permute-done((bf16[272,1536]{1,0:T(8,128)(2,1)S(1)}, bf16[272,1536]{1,0:T(8,128)(2,1)S(1)}, u32[]{:S(2)}, u32[]{:S(2)}) %collective-permute-start.14) | collective-permute-done | bytes 835616 | tf_op jit(solution)/shard_map/ppermute | solution.py:156
  89.6 4.0 %experts.7 = (bf16[256,1536]{1,0:T(8,128)(2,1)S(1)}, bf16[256,1536]{1,0:T(8,128)(2,1)S(1)}) custom-call(f32[8,128]{1,0:T(8,128)S(1)} %copy-done.8, bf16[272,1536]{1,0:T(8,128)(2,1)S(1)} %broadcast_select_fusion.refs_0_, bf16[272,1536]{1,0:T(8,128)(2,1)S(1)} %collective-permute-done.14.refs_1_, bf16[768,768]{1,0:T(8,128)(2,1)S(1)} %copy-done, ...), custom_call_target="tpu_custom_call" | custom-call | flops 1 | bytes 1 | tf_op jit(solution)/shard_map/experts/pallas_call | solution.py:200
  93.7 0.2 collective-permute-done.8.refs_7_.refs_15_
  93.9 4.5 %experts.8 = (bf16[256,1536]{1,0:T(8,128)(2,1)S(1)}, bf16[256,1536]{1,0:T(8,128)(2,1)S(1)}) custom-call(f32[8,128]{1,0:T(8,128)S(1)} %copy-done.8, bf16[272,1536]{1,0:T(8,128)(2,1)S(1)} %broadcast_select_fusion.refs_0_, bf16[272,1536]{1,0:T(8,128)(2,1)S(1)} %collective-permute-done.14.refs_1_, bf16[256,1536]{1,0:T(8,128)(2,1)S(1)} %get-tuple-element.107.refs_2_, ...), custom_call_target="tpu_custom_call" | custom-call | flops 1 | bytes 1 | tf_op jit(solution)/shard_map/experts/pallas_call | solution.py:200
  98.5 2.3 %collective-permute-done.15 = bf16[256,1536]{1,0:T(8,128)(2,1)S(1)} collective-permute-done((bf16[256,1536]{1,0:T(8,128)(2,1)S(1)}, bf16[256,1536]{1,0:T(8,128)(2,1)S(1)}, u32[]{:S(2)}, u32[]{:S(2)}) %collective-permute-start.15) | collective-permute-done | bytes 786464 | tf_op jit(solution)/shard_map/ppermute | solution.py:156
  100.8 0.2 add_convert_fusion.5
  101.0 4.7 %collective-permute-start.19 = (bf16[256,1536]{1,0:T(8,128)(2,1)S(1)}, bf16[256,1536]{1,0:T(8,128)(2,1)S(1)}, u32[]{:S(2)}, u32[]{:S(2)}) collective-permute-start(bf16[256,1536]{1,0:T(8,128)(2,1)S(1)} %add_convert_fusion.5), channel_id=1, source_target_pairs={{0,4},{1,5},{2,6},{3,7},{12,8},{13,9},{14,10},{15,11},{16,20},{17,... | collective-permute-start | bytes 2359304 | tf_op jit(solution)/shard_map/ppermute | solution.py:156
  105.7 10.5 %experts.9 = (bf16[256,1536]{1,0:T(8,128)(2,1)S(1)}, bf16[256,1536]{1,0:T(8,128)(2,1)S(1)}, bf16[256,1536]{1,0:T(8,128)(2,1)S(1)}, bf16[256,1536]{1,0:T(8,128)(2...) custom-call(f32[8,128]{1,0:T(8,128)S(1)} %copy-done.8, ...), custom_call_target="tpu_custom_call" | custom-call | flops 1 | bytes 1 | tf_op jit(solution)/shard_map/experts/pallas_call | solution.py:200
  116.3 0.5 collective-permute-start.17
  116.9 5.6 %collective-permute-done.19 = bf16[256,1536]{1,0:T(8,128)(2,1)S(1)} collective-permute-done((bf16[256,1536]{1,0:T(8,128)(2,1)S(1)}, bf16[256,1536]{1,0:T(8,128)(2,1)S(1)}, u32[]{:S(2)}, u32[]{:S(2)}) %collective-permute-start.19) | collective-permute-done | bytes 786464 | tf_op jit(solution)/shard_map/ppermute | solution.py:156
  122.5 0.2 add_convert_fusion.3
  122.7 0.7 collective-permute-start.21
  123.4 0.2 add_convert_fusion.4
  123.6 7.6 %collective-permute-start.20 = (bf16[256,1536]{1,0:T(8,128)(2,1)S(1)}, bf16[256,1536]{1,0:T(8,128)(2,1)S(1)}, u32[]{:S(2)}, u32[]{:S(2)}) collective-permute-start(bf16[256,1536]{1,0:T(8,128)(2,1)S(1)} %add_convert_fusion.4), channel_id=1, source_target_pairs={{0,4},{1,5},{2,6},{3,7},{12,8},{13,9},{14,10},{15,11},{16,20},{17,... | collective-permute-start | bytes 2359304 | tf_op jit(solution)/shard_map/ppermute | solution.py:156
  131.2 15.9 %collective-permute-done.20 = bf16[256,1536]{1,0:T(8,128)(2,1)S(1)} collective-permute-done((bf16[256,1536]{1,0:T(8,128)(2,1)S(1)}, bf16[256,1536]{1,0:T(8,128)(2,1)S(1)}, u32[]{:S(2)}, u32[]{:S(2)}) %collective-permute-start.20) | collective-permute-done | bytes 786464 | tf_op jit(solution)/shard_map/ppermute | solution.py:156
  147.2 0.3 add_convert_fusion.2
  147.5 2.5 %collective-permute-start.22 = (bf16[256,1536]{1,0:T(8,128)(2,1)S(1)}, bf16[256,1536]{1,0:T(8,128)(2,1)S(1)}, u32[]{:S(2)}, u32[]{:S(2)}) collective-permute-start(bf16[256,1536]{1,0:T(8,128)(2,1)S(1)} %add_convert_fusion.2), channel_id=1, source_target_pairs={{0,4},{1,5},{2,6},{3,7},{4,0},{5,1},{6,2},{7,3},{8,12},{9,13},{10,... | collective-permute-start | bytes 2359304 | tf_op jit(solution)/shard_map/ppermute | solution.py:156
  150.0 0.2 add_convert_fusion.1
  150.2 0.7 collective-permute-start.23
  151.0 14.9 %collective-permute-done.22 = bf16[256,1536]{1,0:T(8,128)(2,1)S(1)} collective-permute-done((bf16[256,1536]{1,0:T(8,128)(2,1)S(1)}, bf16[256,1536]{1,0:T(8,128)(2,1)S(1)}, u32[]{:S(2)}, u32[]{:S(2)}) %collective-permute-start.22) | collective-permute-done | bytes 786464 | tf_op jit(solution)/shard_map/ppermute | solution.py:156
  165.8 1.4 add_convert_fusion
  (38 shorter events, 0.5 us)
Async XLA Ops:
  0.0 7.5 %copy-start.10 = (f32[1536]{0:T(1024)S(1)}, f32[1536]{0:T(1024)}, u32[]{:S(2)}) copy-start(f32[1536]{0:T(1024)} %param.11) | copy-start | bytes 18436
  3.1 29.1 %collective-permute-start = (bf16[768,768]{1,0:T(8,128)(2,1)}, bf16[768,768]{1,0:T(8,128)(2,1)S(1)}, u32[]{:S(2)}, u32[]{:S(2)}) collective-permute-start(bf16[768,768]{1,0:T(8,128)(2,1)} %get-tuple-element.75.refs_4_.refs_2_), channel_id=1, source_target_pairs={{0,16},{16,0},{1,17},{17,1},{2,18},{18,2},{3,19},{19,3},{4,20},{20... | collective-permute-start | bytes 3538952 | tf_op jit(solution)/shard_map/ppermute | solution.py:159
  6.0 27.6 %collective-permute-start.1 = (bf16[768,768]{1,0:T(8,128)(2,1)}, bf16[768,768]{1,0:T(8,128)(2,1)S(1)}, u32[]{:S(2)}, u32[]{:S(2)}) collective-permute-start(bf16[768,768]{1,0:T(8,128)(2,1)} %get-tuple-element.74.refs_6_.refs_4_), channel_id=1, source_target_pairs={{0,2},{1,3},{2,0},{3,1},{4,6},{5,7},{6,4},{7,5},{8,10},{9,11},{10,... | collective-permute-start | bytes 3538952 | tf_op jit(solution)/shard_map/ppermute | solution.py:156
  11.4 24.3 %collective-permute-start.4 = (bf16[272,1536]{1,0:T(8,128)(2,1)}, bf16[272,1536]{1,0:T(8,128)(2,1)}, u32[]{:S(2)}, u32[]{:S(2)}) collective-permute-start(bf16[272,1536]{1,0:T(8,128)(2,1)} %get-tuple-element.78.refs_0_.refs_4_), channel_id=1, source_target_pairs={{4,8},{5,9},{6,10},{7,11},{8,4},{9,5},{10,6},{11,7},{20,24},{21,25... | collective-permute-start | bytes 2506760 | tf_op jit(solution)/shard_map/ppermute | solution.py:156
  13.0 22.7 %collective-permute-start.5 = (bf16[272,1536]{1,0:T(8,128)(2,1)}, bf16[272,1536]{1,0:T(8,128)(2,1)}, u32[]{:S(2)}, u32[]{:S(2)}) collective-permute-start(bf16[272,1536]{1,0:T(8,128)(2,1)} %get-tuple-element.78.refs_0_.refs_4_), channel_id=1, source_target_pairs={{0,4},{1,5},{2,6},{3,7},{4,0},{5,1},{6,2},{7,3},{8,12},{9,13},{10,... | collective-permute-start | bytes 2506760 | tf_op jit(solution)/shard_map/ppermute | solution.py:156
  16.5 19.2 %collective-permute-start.6 = (bf16[272,1536]{1,0:T(8,128)(2,1)}, bf16[272,1536]{1,0:T(8,128)(2,1)S(1)}, u32[]{:S(2)}, u32[]{:S(2)}) collective-permute-start(bf16[272,1536]{1,0:T(8,128)(2,1)} %get-tuple-element.78.refs_0_.refs_4_), channel_id=1, source_target_pairs={{0,1},{1,0},{2,3},{3,2},{4,5},{5,4},{6,7},{7,6},{8,9},{9,8},{10,11... | collective-permute-start | bytes 2506760 | tf_op jit(solution)/shard_map/ppermute | solution.py:156
  33.7 26.8 %collective-permute-start.2 = (bf16[768,768]{1,0:T(8,128)(2,1)}, bf16[768,768]{1,0:T(8,128)(2,1)S(1)}, u32[]{:S(2)}, u32[]{:S(2)}) collective-permute-start(bf16[768,768]{1,0:T(8,128)(2,1)} %get-tuple-element.74.refs_6_.refs_4_), channel_id=1, source_target_pairs={{0,16},{16,0},{1,17},{17,1},{2,18},{18,2},{3,19},{19,3},{4,20},{20... | collective-permute-start | bytes 3538952 | tf_op jit(solution)/shard_map/ppermute | solution.py:159
  34.0 27.0 %collective-permute-start.3 = (bf16[768,768]{1,0:T(8,128)(2,1)}, bf16[768,768]{1,0:T(8,128)(2,1)}, u32[]{:S(2)}, u32[]{:S(2)}) collective-permute-start(bf16[768,768]{1,0:T(8,128)(2,1)} %get-tuple-element.75.refs_4_.refs_2_), channel_id=1, source_target_pairs={{0,2},{1,3},{2,0},{3,1},{4,6},{5,7},{6,4},{7,5},{8,10},{9,11},{10,... | collective-permute-start | bytes 3538952 | tf_op jit(solution)/shard_map/ppermute | solution.py:156
  35.7 0.9 copy-start.5
  36.6 24.3 %collective-permute-start.10 = (bf16[272,1536]{1,0:T(8,128)(2,1)}, bf16[272,1536]{1,0:T(8,128)(2,1)}, u32[]{:S(2)}, u32[]{:S(2)}) collective-permute-start(bf16[272,1536]{1,0:T(8,128)(2,1)} %collective-permute-done.5.refs_2_), channel_id=1, source_target_pairs={{4,8},{5,9},{6,10},{7,11},{8,4},{9,5},{10,6},{11,7},{20,24},{21,25... | collective-permute-start | bytes 2506760 | tf_op jit(solution)/shard_map/ppermute | solution.py:156
  38.2 22.7 %collective-permute-start.11 = (bf16[272,1536]{1,0:T(8,128)(2,1)}, bf16[272,1536]{1,0:T(8,128)(2,1)}, u32[]{:S(2)}, u32[]{:S(2)}) collective-permute-start(bf16[272,1536]{1,0:T(8,128)(2,1)} %collective-permute-done.5.refs_2_), channel_id=1, source_target_pairs={{0,1},{1,0},{2,3},{3,2},{4,5},{5,4},{6,7},{7,6},{8,9},{9,8},{10,11... | collective-permute-start | bytes 2506760 | tf_op jit(solution)/shard_map/ppermute | solution.py:156
  38.2 24.4 %collective-permute-start.9 = (bf16[272,1536]{1,0:T(8,128)(2,1)}, bf16[272,1536]{1,0:T(8,128)(2,1)}, u32[]{:S(2)}, u32[]{:S(2)}) collective-permute-start(bf16[272,1536]{1,0:T(8,128)(2,1)} %collective-permute-done.4), channel_id=1, source_target_pairs={{4,0},{5,1},{6,2},{7,3},{8,12},{9,13},{10,14},{11,15},{20,16},{21,... | collective-permute-start | bytes 2506760 | tf_op jit(solution)/shard_map/ppermute | solution.py:156
  39.5 27.8 %copy-start = (bf16[768,768]{1,0:T(8,128)(2,1)S(1)}, bf16[768,768]{1,0:T(8,128)(2,1)}, u32[]{:S(2)}) copy-start(bf16[768,768]{1,0:T(8,128)(2,1)} %get-tuple-element.75.refs_4_.refs_2_) | copy-start | bytes 3538948
  39.5 27.8 %copy-start.1 = (bf16[768,768]{1,0:T(8,128)(2,1)S(1)}, bf16[768,768]{1,0:T(8,128)(2,1)}, u32[]{:S(2)}) copy-start(bf16[768,768]{1,0:T(8,128)(2,1)} %get-tuple-element.74.refs_6_.refs_4_) | copy-start | bytes 3538948
  39.5 27.8 %copy-start.8 = (f32[8,128]{1,0:T(8,128)S(1)}, f32[8,128]{1,0:T(8,128)}, u32[]{:S(2)}) copy-start(f32[8,128]{1,0:T(8,128)} %get-tuple-element.114._) | copy-start | bytes 12292
  63.9 13.9 %collective-permute-start.13 = (bf16[272,1536]{1,0:T(8,128)(2,1)S(1)}, bf16[272,1536]{1,0:T(8,128)(2,1)S(1)}, u32[]{:S(2)}, u32[]{:S(2)}) collective-permute-start(bf16[272,1536]{1,0:T(8,128)(2,1)S(1)} %broadcast_select_fusion.1.refs_0_), channel_id=1, source_target_pairs={{0,1},{1,0},{2,3},{3,2},{4,5},{5,4},{6,7},{7,6},{8,9},{9,8},{10,11... | collective-permute-start | bytes 2506760 | tf_op jit(solution)/shard_map/ppermute | solution.py:156
  63.9 23.1 %collective-permute-start.12 = (bf16[272,1536]{1,0:T(8,128)(2,1)}, bf16[272,1536]{1,0:T(8,128)(2,1)S(1)}, u32[]{:S(2)}, u32[]{:S(2)}) collective-permute-start(bf16[272,1536]{1,0:T(8,128)(2,1)} %collective-permute-done.10), channel_id=1, source_target_pairs={{4,0},{5,1},{6,2},{7,3},{8,12},{9,13},{10,14},{11,15},{20,16},{21,... | collective-permute-start | bytes 2506760 | tf_op jit(solution)/shard_map/ppermute | solution.py:156
  65.2 28.4 %collective-permute-start.7 = (bf16[768,768]{1,0:T(8,128)(2,1)S(1)}, bf16[768,768]{1,0:T(8,128)(2,1)S(1)}, u32[]{:S(2)}, u32[]{:S(2)}) collective-permute-start(bf16[768,768]{1,0:T(8,128)(2,1)S(1)} %collective-permute-done.refs_5_.refs_3_), channel_id=1, source_target_pairs={{0,2},{1,3},{2,0},{3,1},{4,6},{5,7},{6,4},{7,5},{8,10},{9,11},{10,... | collective-permute-start | bytes 3538952 | tf_op jit(solution)/shard_map/ppermute | solution.py:156
  65.8 28.1 %collective-permute-start.8 = (bf16[768,768]{1,0:T(8,128)(2,1)S(1)}, bf16[768,768]{1,0:T(8,128)(2,1)S(1)}, u32[]{:S(2)}, u32[]{:S(2)}) collective-permute-start(bf16[768,768]{1,0:T(8,128)(2,1)S(1)} %collective-permute-done.1.refs_6_.refs_14_), channel_id=1, source_target_pairs={{0,16},{16,0},{1,17},{17,1},{2,18},{18,2},{3,19},{19,3},{4,20},{20... | collective-permute-start | bytes 3538952 | tf_op jit(solution)/shard_map/ppermute | solution.py:159
  67.3 1.2 copy-start.3
  68.5 1.1 copy-start.6
  87.1 2.4 %collective-permute-start.14 = (bf16[272,1536]{1,0:T(8,128)(2,1)S(1)}, bf16[272,1536]{1,0:T(8,128)(2,1)S(1)}, u32[]{:S(2)}, u32[]{:S(2)}) collective-permute-start(bf16[272,1536]{1,0:T(8,128)(2,1)S(1)} %broadcast_select_fusion.refs_0_), channel_id=1, source_target_pairs={{0,1},{1,0},{2,3},{3,2},{4,5},{5,4},{6,7},{7,6},{8,9},{9,8},{10,11... | collective-permute-start | bytes 2506760 | tf_op jit(solution)/shard_map/ppermute | solution.py:156
  93.9 4.5 %copy-start.2 = (bf16[768,768]{1,0:T(8,128)(2,1)}, bf16[768,768]{1,0:T(8,128)(2,1)S(1)}, u32[]{:S(2)}) copy-start(bf16[768,768]{1,0:T(8,128)(2,1)S(1)} %collective-permute-done.8.refs_7_.refs_15_) | copy-start | bytes 3538948
  98.4 2.4 %collective-permute-start.15 = (bf16[256,1536]{1,0:T(8,128)(2,1)S(1)}, bf16[256,1536]{1,0:T(8,128)(2,1)S(1)}, u32[]{:S(2)}, u32[]{:S(2)}) collective-permute-start(bf16[256,1536]{1,0:T(8,128)(2,1)S(1)} %get-tuple-element.112), channel_id=1, source_target_pairs={{0,1},{1,0},{2,3},{3,2},{4,5},{5,4},{6,7},{7,6},{8,9},{9,8},{10,11... | collective-permute-start | bytes 2359304 | tf_op jit(solution)/shard_map/ppermute | solution.py:156
  100.8 4.9 %copy-start.4 = (bf16[272,1536]{1,0:T(8,128)(2,1)S(1)}, bf16[272,1536]{1,0:T(8,128)(2,1)}, u32[]{:S(2)}) copy-start(bf16[272,1536]{1,0:T(8,128)(2,1)} %get-tuple-element.78.refs_0_.refs_4_) | copy-start | bytes 2506756
  100.8 4.9 %copy-start.7 = (bf16[272,1536]{1,0:T(8,128)(2,1)S(1)}, bf16[272,1536]{1,0:T(8,128)(2,1)}, u32[]{:S(2)}) copy-start(bf16[272,1536]{1,0:T(8,128)(2,1)} %copy-done.5) | copy-start | bytes 2506756
  101.0 21.5 %collective-permute-start.19 = (bf16[256,1536]{1,0:T(8,128)(2,1)S(1)}, bf16[256,1536]{1,0:T(8,128)(2,1)S(1)}, u32[]{:S(2)}, u32[]{:S(2)}) collective-permute-start(bf16[256,1536]{1,0:T(8,128)(2,1)S(1)} %add_convert_fusion.5), channel_id=1, source_target_pairs={{0,4},{1,5},{2,6},{3,7},{12,8},{13,9},{14,10},{15,11},{16,20},{17,... | collective-permute-start | bytes 2359304 | tf_op jit(solution)/shard_map/ppermute | solution.py:156
  116.2 6.3 %collective-permute-start.16 = (bf16[256,1536]{1,0:T(8,128)(2,1)S(1)}, bf16[256,1536]{1,0:T(8,128)(2,1)S(1)}, u32[]{:S(2)}, u32[]{:S(2)}) collective-permute-start(bf16[256,1536]{1,0:T(8,128)(2,1)S(1)} %get-tuple-element.122), channel_id=1, source_target_pairs={{0,1},{1,0},{2,3},{3,2},{4,5},{5,4},{6,7},{7,6},{8,9},{9,8},{10,11... | collective-permute-start | bytes 2359304 | tf_op jit(solution)/shard_map/ppermute | solution.py:156
  116.3 6.2 %collective-permute-start.17 = (bf16[256,1536]{1,0:T(8,128)(2,1)S(1)}, bf16[256,1536]{1,0:T(8,128)(2,1)S(1)}, u32[]{:S(2)}, u32[]{:S(2)}) collective-permute-start(bf16[256,1536]{1,0:T(8,128)(2,1)S(1)} %get-tuple-element.123), channel_id=1, source_target_pairs={{0,1},{1,0},{2,3},{3,2},{4,5},{5,4},{6,7},{7,6},{8,9},{9,8},{10,11... | collective-permute-start | bytes 2359304 | tf_op jit(solution)/shard_map/ppermute | solution.py:156
  116.8 5.7 %collective-permute-start.18 = (bf16[256,1536]{1,0:T(8,128)(2,1)S(1)}, bf16[256,1536]{1,0:T(8,128)(2,1)S(1)}, u32[]{:S(2)}, u32[]{:S(2)}) collective-permute-start(bf16[256,1536]{1,0:T(8,128)(2,1)S(1)} %get-tuple-element.124), channel_id=1, source_target_pairs={{0,1},{1,0},{2,3},{3,2},{4,5},{5,4},{6,7},{7,6},{8,9},{9,8},{10,11... | collective-permute-start | bytes 2359304 | tf_op jit(solution)/shard_map/ppermute | solution.py:156
  122.7 8.5 %collective-permute-start.21 = (bf16[256,1536]{1,0:T(8,128)(2,1)S(1)}, bf16[256,1536]{1,0:T(8,128)(2,1)S(1)}, u32[]{:S(2)}, u32[]{:S(2)}) collective-permute-start(bf16[256,1536]{1,0:T(8,128)(2,1)S(1)} %add_convert_fusion.3), channel_id=1, source_target_pairs={{4,8},{5,9},{6,10},{7,11},{8,4},{9,5},{10,6},{11,7},{20,24},{21,25... | collective-permute-start | bytes 2359304 | tf_op jit(solution)/shard_map/ppermute | solution.py:156
  123.6 23.5 %collective-permute-start.20 = (bf16[256,1536]{1,0:T(8,128)(2,1)S(1)}, bf16[256,1536]{1,0:T(8,128)(2,1)S(1)}, u32[]{:S(2)}, u32[]{:S(2)}) collective-permute-start(bf16[256,1536]{1,0:T(8,128)(2,1)S(1)} %add_convert_fusion.4), channel_id=1, source_target_pairs={{0,4},{1,5},{2,6},{3,7},{12,8},{13,9},{14,10},{15,11},{16,20},{17,... | collective-permute-start | bytes 2359304 | tf_op jit(solution)/shard_map/ppermute | solution.py:156
  147.5 18.4 %copy-start.9 = (bf16[256,1536]{1,0:T(8,128)(2,1)S(1)}, bf16[256,1536]{1,0:T(8,128)(2,1)}, u32[]{:S(2)}) copy-start(bf16[256,1536]{1,0:T(8,128)(2,1)} %tokens.1) | copy-start | bytes 2359300
  147.5 18.4 %collective-permute-start.22 = (bf16[256,1536]{1,0:T(8,128)(2,1)S(1)}, bf16[256,1536]{1,0:T(8,128)(2,1)S(1)}, u32[]{:S(2)}, u32[]{:S(2)}) collective-permute-start(bf16[256,1536]{1,0:T(8,128)(2,1)S(1)} %add_convert_fusion.2), channel_id=1, source_target_pairs={{0,4},{1,5},{2,6},{3,7},{4,0},{5,1},{6,2},{7,3},{8,12},{9,13},{10,... | collective-permute-start | bytes 2359304 | tf_op jit(solution)/shard_map/ppermute | solution.py:156
  150.2 15.6 %collective-permute-start.23 = (bf16[256,1536]{1,0:T(8,128)(2,1)S(1)}, bf16[256,1536]{1,0:T(8,128)(2,1)S(1)}, u32[]{:S(2)}, u32[]{:S(2)}) collective-permute-start(bf16[256,1536]{1,0:T(8,128)(2,1)S(1)} %add_convert_fusion.1), channel_id=1, source_target_pairs={{4,8},{5,9},{6,10},{7,11},{8,4},{9,5},{10,6},{11,7},{20,24},{21,25... | collective-permute-start | bytes 2359304 | tf_op jit(solution)/shard_map/ppermute | solution.py:156

commit v4 on v3

--- a/solution.py
+++ b/solution.py
@@ -77,15 +77,22 @@
     order[...] = jnp.zeros_like(order)
 
 
-def pack_kernel(gate, up, down, *packed):
+def pack_kernel(gate, up, down, *refs):
+    packed, sems = refs[:-1], refs[-1]
     half = gate.shape[0]
+    copies = []
     for h, chunk in enumerate(packed):
-        units = slice(CHUNK * h, CHUNK * (h + 1))
-        chunk[:, :CHUNK] = gate[:, units]
-        chunk[:, CHUNK : 2 * CHUNK] = up[:, units]
+        units = pl.ds(CHUNK * h, CHUNK)
+        copies.append((gate.at[:, units], chunk.at[:, pl.ds(0, CHUNK)]))
+        copies.append((up.at[:, units], chunk.at[:, pl.ds(CHUNK, CHUNK)]))
         for i in range(half // CHUNK):
-            columns = slice(CHUNK * i, CHUNK * (i + 1))
-            chunk[columns, 2 * CHUNK :] = down[units, columns]
+            columns = pl.ds(CHUNK * i, CHUNK)
+            copies.append((down.at[units, columns], chunk.at[columns, pl.ds(2 * CHUNK, CHUNK)]))
+    copies = [pltpu.make_async_copy(source, target, sems.at[i]) for i, (source, target) in enumerate(copies)]
+    for copy in copies:
+        copy.start()
+    for copy in copies:
+        copy.wait()
 
 
 def expert_kernel(work, based, count, _, *refs):
@@ -164,8 +171,6 @@
     by_core, by_y = ([(i, i ^ bit) for i in range(16)] for bit in (1, 2))
     outer = over((0, 1), (1, 0), (2, 3), (3, 2))
     inner = over((1, 2), (2, 1))
-    outward = over((1, 0), (2, 3))
-    inward = over((0, 1), (3, 2))
     smem = pl.BlockSpec(memory_space=pltpu.SMEM)
     vmem = pl.BlockSpec(memory_space=pltpu.VMEM)
     anywhere = pl.BlockSpec(memory_space=pl.ANY)
@@ -173,8 +178,9 @@
     own = pl.pallas_call(
         pack_kernel,
         out_shape=(jax.ShapeDtypeStruct((half, half), BF16),) * (hid // CHUNK),
-        in_specs=[vmem] * 3,
+        in_specs=[anywhere] * 3,
         out_specs=(vmem,) * (hid // CHUNK),
+        scratch_shapes=[pltpu.SemaphoreType.DMA((hid // CHUNK * (2 + half // CHUNK),))],
         name="pack",
     )(w_gate[0], w_up[0], w_down[0])
     x_0 = across(own[0])
@@ -224,14 +230,14 @@
     x_1 = across(own_1)
     y_0 = send(own_0, by_y)
     s_m, s_a, m_0 = together(s_m, s_a, m_0)
-    s_b = send(s_m, outward)
+    s_b = send(s_m, outer)
     s_n = send(s_a, inner)
     m_a = send(s_a, by_core)
     x_1, y_0, x_0, y_1 = together(x_1, y_0, x_0, y_1)
     d_0 = send(x_0, by_y)
     d_1 = across(y_1)
     s_b, s_n, m_a = together(s_b, s_n, m_a)
-    s_c = send(s_n, outward)
+    s_c = send(s_n, outer)
     s_b = jnp.where(middle, s_m, s_b)
     m_b = send(s_b, by_core)
     mine = (own[0], x_0, own[1], x_1)
@@ -250,16 +256,18 @@
 
     r_c, p_c = together(r_c, p_c)
     q_c = add(p_c, r_c)
-    r_n = send(q_c, inward)
+    r_n = send(q_c, outer)
     p_b, o_b, p_a, o_a, p_0, o_0 = run((s_b, m_b, s_a, m_a, s_0, m_0), [(1, theirs, 0, 6)], [u_b, v_b, u_a, v_a, u_0, v_0])
     r_b, r_a, r_0 = send(o_b, by_core), send(o_a, by_core), send(o_0, by_core)
-    r_b, r_a, r_0, r_n, p_b, p_a = together(r_b, r_a, r_0, r_n, p_b, p_a)
+    r_b, p_b = together(r_b, p_b)
     q_b = add(p_b, r_b)
-    r_m = send(q_b, inward)
+    r_m = send(q_b, outer)
+    r_n, r_a, r_0, p_a = together(r_n, r_a, r_0, p_a)
     r_i = send(add(q_c, r_n), inner)
-    r_m, r_i = together(r_m, r_i)
+    (r_m,) = together(r_m)
+    r_m = send(add(q_b, r_m), inner)
+    (r_i,) = together(r_i)
     r_o = send(add(p_a, r_a, r_i), outer)
-    r_m = send(add(q_b, r_m), inner)
     return add(tokens, p_0, r_0, r_o, r_m)
 
 

time: 169 us -> 162 us (0.959)
  waiting for transfers between devices: 86.8 us -> 69.1 us
  starting transfers between devices: 34.9 us -> 45.1 us
    ppermute x21, waiting for transfers between devices: 49.9 us -> 34.1 us  [send(): return lax.ppermute(v, 'tensor', pairs)]
    ppermute x21, starting transfers between devices: 30.2 us -> 40.3 us  [send(): return lax.ppermute(v, 'tensor', pairs)]
    ppermute x3, waiting for transfers between devices: 36.9 us -> 35 us  [across(): return lax.ppermute(v, 'dp', [(0, 1), (1, 0)])]
  transfers between devices with their start and end apart: 24 -> 24, of which waited for: 13 -> 12; matrix products, arithmetic and copies ran while one was open for 1% -> 1% of each run, Pallas kernels for 18% -> 18%
where the time goes in v4:
time: 162 us; the launch traced here: 160 us
  waiting for transfers between devices  69.1 us (43%)
  starting transfers between devices  45.1 us (28%)
  Pallas kernels  37.1 us (23%)
  local copies, waits for them, and re-layouts  4.51 us (3%)
  other arithmetic  3.82 us (2%)
    ppermute x21, starting transfers between devices, send(): return lax.ppermute(v, 'tensor', pairs)  40.3 us
    ppermute x3, waiting for transfers between devices, across(): return lax.ppermute(v, 'dp', [(0, 1), (1, 0)])  35 us
    ppermute x21, waiting for transfers between devices, send(): return lax.ppermute(v, 'tensor', pairs)  34.1 us
    pallas_call x5, Pallas kernels, run(): pl.pallas_call(functools.partial(expert_kernel, tuple(((e, first, last) f...  31.4 us
    ppermute x3, starting transfers between devices, across(): return lax.ppermute(v, 'dp', [(0, 1), (1, 0)])  4.79 us
    unnamed x22, local copies, waits for them, and re-layouts  3.91 us
  transfers between devices with their start and end apart: 24, of which 12 were waited for; matrix products, arithmetic and copies ran while one was open for 1% of the time, Pallas kernels for 18%

profile of v4, /device:TPU:0, one launch (start us, length us, event | category | flops | bytes accessed | tf_op | source)
XLA Modules:
  0.0 160.4 jit_solution(8023763885273851355)
XLA Ops:
  0.0 3.1 %pack.1 = (bf16[768,768]{1,0:T(8,128)(2,1)}, bf16[768,768]{1,0:T(8,128)(2,1)}) custom-call(bf16[768,512]{1,0:T(8,128)(2,1)} %bitcast.5, bf16[768,512]{1,0:T(8,128)(2,1)} %bitcast.6, bf16[512,768]{1,0:T(8,128)(2,1)} %bitcast.7), custom_call_target="tpu_custom_call" | custom-call | tf_op jit(solution)/shard_map/pack/pallas_call | solution.py:178
  3.1 3.0 %collective-permute-start = (bf16[768,768]{1,0:T(8,128)(2,1)}, bf16[768,768]{1,0:T(8,128)(2,1)S(1)}, u32[]{:S(2)}, u32[]{:S(2)}) collective-permute-start(bf16[768,768]{1,0:T(8,128)(2,1)} %get-tuple-element.73.refs_4_.refs_2_), channel_id=1, source_target_pairs={{0,16},{16,0},{1,17},{17,1},{2,18},{18,2},{3,19},{19,3},{4,20},{20... | collective-permute-start | bytes 3538952 | tf_op jit(solution)/shard_map/ppermute | solution.py:166
  6.1 1.5 collective-permute-start.1
  7.6 0.6 reshape.3.gain
  8.9 2.6 %prologue.1 = (bf16[272,1536]{1,0:T(8,128)(2,1)}, f32[8,128]{1,0:T(8,128)}) custom-call(s32[1]{0:T(128)S(6)} %copy.9.lengths, bf16[256,1536]{1,0:T(8,128)(2,1)} %tokens.1, f32[1,1536]{1,0:T(1,128)} %reshape.3.gain, bf16[16,1536]{1,0:T(8,128)(2,1)} %bitcast.8, s32[8,256]{1,0:T(8,128)} %bitcast.9), custom_call_target="tpu_custom_call" | custom-call | tf_op jit(solution)/shard_map/prologue/pallas_call | solution.py:188
  11.4 1.6 %collective-permute-start.4 = (bf16[272,1536]{1,0:T(8,128)(2,1)}, bf16[272,1536]{1,0:T(8,128)(2,1)}, u32[]{:S(2)}, u32[]{:S(2)}) collective-permute-start(bf16[272,1536]{1,0:T(8,128)(2,1)} %get-tuple-element.76.refs_0_.refs_4_), channel_id=1, source_target_pairs={{4,8},{5,9},{6,10},{7,11},{8,4},{9,5},{10,6},{11,7},{20,24},{21,25... | collective-permute-start | bytes 2506760 | tf_op jit(solution)/shard_map/ppermute | solution.py:163
  13.1 3.5 %collective-permute-start.5 = (bf16[272,1536]{1,0:T(8,128)(2,1)}, bf16[272,1536]{1,0:T(8,128)(2,1)}, u32[]{:S(2)}, u32[]{:S(2)}) collective-permute-start(bf16[272,1536]{1,0:T(8,128)(2,1)} %get-tuple-element.76.refs_0_.refs_4_), channel_id=1, source_target_pairs={{0,4},{1,5},{2,6},{3,7},{4,0},{5,1},{6,2},{7,3},{8,12},{9,13},{10,... | collective-permute-start | bytes 2506760 | tf_op jit(solution)/shard_map/ppermute | solution.py:163
  16.6 15.7 %collective-permute-done.refs_5_.refs_3_ = bf16[768,768]{1,0:T(8,128)(2,1)S(1)} collective-permute-done((bf16[768,768]{1,0:T(8,128)(2,1)}, bf16[768,768]{1,0:T(8,128)(2,1)S(1)}, u32[]{:S(2)}, u32[]{:S(2)}) %collective-permute-start) | collective-permute-done | bytes 1179680 | tf_op jit(solution)/shard_map/ppermute | solution.py:166
  32.3 1.5 collective-permute-done.1.refs_6_.refs_14_
  33.7 0.4 collective-permute-start.2
  34.1 1.7 %collective-permute-start.3 = (bf16[768,768]{1,0:T(8,128)(2,1)}, bf16[768,768]{1,0:T(8,128)(2,1)}, u32[]{:S(2)}, u32[]{:S(2)}) collective-permute-start(bf16[768,768]{1,0:T(8,128)(2,1)} %get-tuple-element.73.refs_4_.refs_2_), channel_id=1, source_target_pairs={{0,2},{1,3},{2,0},{3,1},{4,6},{5,7},{6,4},{7,5},{8,10},{9,11},{10,... | collective-permute-start | bytes 3538952 | tf_op jit(solution)/shard_map/ppermute | solution.py:163
  35.8 0.9 copy-done.5
  36.7 1.6 collective-permute-start.10
  38.3 3.6 %collective-permute-start.9 = (bf16[272,1536]{1,0:T(8,128)(2,1)}, bf16[272,1536]{1,0:T(8,128)(2,1)}, u32[]{:S(2)}, u32[]{:S(2)}) collective-permute-start(bf16[272,1536]{1,0:T(8,128)(2,1)} %collective-permute-done.4), channel_id=1, source_target_pairs={{0,4},{1,5},{2,6},{3,7},{4,0},{5,1},{6,2},{7,3},{8,12},{9,13},{10,... | collective-permute-start | bytes 2506760 | tf_op jit(solution)/shard_map/ppermute | solution.py:163
  41.9 18.6 %collective-permute-done.2.refs_7_.refs_5_ = bf16[768,768]{1,0:T(8,128)(2,1)S(1)} collective-permute-done((bf16[768,768]{1,0:T(8,128)(2,1)}, bf16[768,768]{1,0:T(8,128)(2,1)S(1)}, u32[]{:S(2)}, u32[]{:S(2)}) %collective-permute-start.2) | collective-permute-done | bytes 1179680 | tf_op jit(solution)/shard_map/ppermute | solution.py:166
  60.6 0.5 collective-permute-done.3.refs_4_.refs_12_
  61.1 0.3 collective-permute-done.9
  61.4 1.2 broadcast_select_fusion.1.refs_0_
  62.7 1.8 %collective-permute-start.12 = (bf16[272,1536]{1,0:T(8,128)(2,1)}, bf16[272,1536]{1,0:T(8,128)(2,1)S(1)}, u32[]{:S(2)}, u32[]{:S(2)}) collective-permute-start(bf16[272,1536]{1,0:T(8,128)(2,1)} %collective-permute-done.10), channel_id=1, source_target_pairs={{0,4},{1,5},{2,6},{3,7},{4,0},{5,1},{6,2},{7,3},{8,12},{9,13},{10,... | collective-permute-start | bytes 2506760 | tf_op jit(solution)/shard_map/ppermute | solution.py:163
  64.6 0.9 collective-permute-start.7
  65.5 1.4 collective-permute-start.8
  66.9 1.1 copy-done.3
  68.1 1.1 copy-done.6
  69.2 8.1 %experts.5 = (bf16[256,1536]{1,0:T(8,128)(2,1)S(1)}, bf16[256,1536]{1,0:T(8,128)(2,1)S(1)}, bf16[256,1536]{1,0:T(8,128)(2,1)S(1)}, bf16[256,1536]{1,0:T(8,128)(2,1)S(1)}) custom-call(f32[8,128]{1,0:T(8,128)S(1)} %copy-done.8, bf16[272,1536]{1,0:T(8,128)(2,1)S(1)} %copy-done.3, bf16[272,1536]{1,0:T(8,128)(2,1)S(1)} %copy-done.6, ...), custom_call_target="tpu_custom_call" | custom-call | flops 1 | bytes 1 | tf_op jit(solution)/shard_map/experts/pallas_call | solution.py:206
  77.4 4.0 %experts.6 = (bf16[256,1536]{1,0:T(8,128)(2,1)S(1)}, bf16[256,1536]{1,0:T(8,128)(2,1)S(1)}) custom-call(f32[8,128]{1,0:T(8,128)S(1)} %copy-done.8, bf16[272,1536]{1,0:T(8,128)(2,1)S(1)} %broadcast_select_fusion.1.refs_0_, bf16[272,1536]{1,0:T(8,128)(2,1)S(1)} %collective-permute-done.13.refs_1_, bf16[768,768]{1,0:T(8,128)(2,1)S(1)} %copy-done, ...), custom_call_target="tpu_custom_call" | custom-call | flops 1 | bytes 1 | tf_op jit(solution)/shard_map/experts/pallas_call | solution.py:206
  81.4 2.5 %collective-permute-done.12 = bf16[272,1536]{1,0:T(8,128)(2,1)S(1)} collective-permute-done((bf16[272,1536]{1,0:T(8,128)(2,1)}, bf16[272,1536]{1,0:T(8,128)(2,1)S(1)}, u32[]{:S(2)}, u32[]{:S(2)}) %collective-permute-start.12) | collective-permute-done | bytes 835616 | tf_op jit(solution)/shard_map/ppermute | solution.py:163
  84.2 2.3 %collective-permute-done.14.refs_1_ = bf16[272,1536]{1,0:T(8,128)(2,1)S(1)} collective-permute-done((bf16[272,1536]{1,0:T(8,128)(2,1)S(1)}, bf16[272,1536]{1,0:T(8,128)(2,1)S(1)}, u32[]{:S(2)}, u32[]{:S(2)}) %collective-permute-start.14) | collective-permute-done | bytes 835616 | tf_op jit(solution)/shard_map/ppermute | solution.py:163
  86.5 4.0 %experts.7 = (bf16[256,1536]{1,0:T(8,128)(2,1)S(1)}, bf16[256,1536]{1,0:T(8,128)(2,1)S(1)}) custom-call(f32[8,128]{1,0:T(8,128)S(1)} %copy-done.8, bf16[272,1536]{1,0:T(8,128)(2,1)S(1)} %broadcast_select_fusion.refs_0_, bf16[272,1536]{1,0:T(8,128)(2,1)S(1)} %collective-permute-done.14.refs_1_, bf16[768,768]{1,0:T(8,128)(2,1)S(1)} %copy-done, ...), custom_call_target="tpu_custom_call" | custom-call | flops 1 | bytes 1 | tf_op jit(solution)/shard_map/experts/pallas_call | solution.py:206
  90.5 2.1 %collective-permute-done.7.refs_5_.refs_13_ = bf16[768,768]{1,0:T(8,128)(2,1)S(1)} collective-permute-done((bf16[768,768]{1,0:T(8,128)(2,1)S(1)}, bf16[768,768]{1,0:T(8,128)(2,1)S(1)}, u32[]{:S(2)}, u32[]{:S(2)}) %collective-permute-start.7) | collective-permute-done | bytes 1179680 | tf_op jit(solution)/shard_map/ppermute | solution.py:163
  92.6 0.7 collective-permute-done.8.refs_7_.refs_15_
  93.3 4.5 %experts.8 = (bf16[256,1536]{1,0:T(8,128)(2,1)S(1)}, bf16[256,1536]{1,0:T(8,128)(2,1)S(1)}) custom-call(f32[8,128]{1,0:T(8,128)S(1)} %copy-done.8, bf16[272,1536]{1,0:T(8,128)(2,1)S(1)} %broadcast_select_fusion.refs_0_, bf16[272,1536]{1,0:T(8,128)(2,1)S(1)} %collective-permute-done.14.refs_1_, bf16[256,1536]{1,0:T(8,128)(2,1)S(1)} %get-tuple-element.105.refs_2_, ...), custom_call_target="tpu_custom_call" | custom-call | flops 1 | bytes 1 | tf_op jit(solution)/shard_map/experts/pallas_call | solution.py:206
  97.9 2.3 %collective-permute-done.15 = bf16[256,1536]{1,0:T(8,128)(2,1)S(1)} collective-permute-done((bf16[256,1536]{1,0:T(8,128)(2,1)S(1)}, bf16[256,1536]{1,0:T(8,128)(2,1)S(1)}, u32[]{:S(2)}, u32[]{:S(2)}) %collective-permute-start.15) | collective-permute-done | bytes 786464 | tf_op jit(solution)/shard_map/ppermute | solution.py:163
  100.4 0.5 collective-permute-start.16
  100.9 0.4 copy-done.4
  101.3 0.3 copy-done.7
  101.6 10.7 %experts.9 = (bf16[256,1536]{1,0:T(8,128)(2,1)S(1)}, bf16[256,1536]{1,0:T(8,128)(2,1)S(1)}, bf16[256,1536]{1,0:T(8,128)(2,1)S(1)}, bf16[256,1536]{1,0:T(8,128)(2...) custom-call(f32[8,128]{1,0:T(8,128)S(1)} %copy-done.8, ...), custom_call_target="tpu_custom_call" | custom-call | flops 1 | bytes 1 | tf_op jit(solution)/shard_map/experts/pallas_call | solution.py:206
  112.3 0.2 collective-permute-start.17
  112.5 0.4 collective-permute-start.18
  113.0 7.0 %collective-permute-done.16 = bf16[256,1536]{1,0:T(8,128)(2,1)S(1)} collective-permute-done((bf16[256,1536]{1,0:T(8,128)(2,1)S(1)}, bf16[256,1536]{1,0:T(8,128)(2,1)S(1)}, u32[]{:S(2)}, u32[]{:S(2)}) %collective-permute-start.16) | collective-permute-done | bytes 786464 | tf_op jit(solution)/shard_map/ppermute | solution.py:163
  120.2 0.7 collective-permute-start.19
  120.9 0.2 add_convert_fusion.2
  121.1 4.3 %collective-permute-start.22 = (bf16[256,1536]{1,0:T(8,128)(2,1)S(1)}, bf16[256,1536]{1,0:T(8,128)(2,1)S(1)}, u32[]{:S(2)}, u32[]{:S(2)}) collective-permute-start(bf16[256,1536]{1,0:T(8,128)(2,1)S(1)} %add_convert_fusion.2), channel_id=1, source_target_pairs={{0,4},{1,5},{2,6},{3,7},{4,0},{5,1},{6,2},{7,3},{8,12},{9,13},{10,... | collective-permute-start | bytes 2359304 | tf_op jit(solution)/shard_map/ppermute | solution.py:163
  125.5 0.3 add_convert_fusion.3
  125.8 16.8 %collective-permute-start.20 = (bf16[256,1536]{1,0:T(8,128)(2,1)S(1)}, bf16[256,1536]{1,0:T(8,128)(2,1)S(1)}, u32[]{:S(2)}, u32[]{:S(2)}) collective-permute-start(bf16[256,1536]{1,0:T(8,128)(2,1)S(1)} %add_convert_fusion.3), channel_id=1, source_target_pairs={{0,4},{1,5},{2,6},{3,7},{4,0},{5,1},{6,2},{7,3},{8,12},{9,13},{10,... | collective-permute-start | bytes 2359304 | tf_op jit(solution)/shard_map/ppermute | solution.py:163
  142.6 0.2 add_convert_fusion.1
  142.8 0.7 collective-permute-start.23
  143.5 15.5 %collective-permute-done.20 = bf16[256,1536]{1,0:T(8,128)(2,1)S(1)} collective-permute-done((bf16[256,1536]{1,0:T(8,128)(2,1)S(1)}, bf16[256,1536]{1,0:T(8,128)(2,1)S(1)}, u32[]{:S(2)}, u32[]{:S(2)}) %collective-permute-start.20) | collective-permute-done | bytes 786464 | tf_op jit(solution)/shard_map/ppermute | solution.py:163
  159.0 1.4 add_convert_fusion
  (38 shorter events, 0.9 us)
Async XLA Ops:
  0.0 7.6 %copy-start.10 = (f32[1536]{0:T(1024)S(1)}, f32[1536]{0:T(1024)}, u32[]{:S(2)}) copy-start(f32[1536]{0:T(1024)} %param.11) | copy-start | bytes 18436
  3.1 29.2 %collective-permute-start = (bf16[768,768]{1,0:T(8,128)(2,1)}, bf16[768,768]{1,0:T(8,128)(2,1)S(1)}, u32[]{:S(2)}, u32[]{:S(2)}) collective-permute-start(bf16[768,768]{1,0:T(8,128)(2,1)} %get-tuple-element.73.refs_4_.refs_2_), channel_id=1, source_target_pairs={{0,16},{16,0},{1,17},{17,1},{2,18},{18,2},{3,19},{19,3},{4,20},{20... | collective-permute-start | bytes 3538952 | tf_op jit(solution)/shard_map/ppermute | solution.py:166
  6.1 27.6 %collective-permute-start.1 = (bf16[768,768]{1,0:T(8,128)(2,1)}, bf16[768,768]{1,0:T(8,128)(2,1)S(1)}, u32[]{:S(2)}, u32[]{:S(2)}) collective-permute-start(bf16[768,768]{1,0:T(8,128)(2,1)} %get-tuple-element.72.refs_6_.refs_4_), channel_id=1, source_target_pairs={{0,2},{1,3},{2,0},{3,1},{4,6},{5,7},{6,4},{7,5},{8,10},{9,11},{10,... | collective-permute-start | bytes 3538952 | tf_op jit(solution)/shard_map/ppermute | solution.py:163
  11.4 24.3 %collective-permute-start.4 = (bf16[272,1536]{1,0:T(8,128)(2,1)}, bf16[272,1536]{1,0:T(8,128)(2,1)}, u32[]{:S(2)}, u32[]{:S(2)}) collective-permute-start(bf16[272,1536]{1,0:T(8,128)(2,1)} %get-tuple-element.76.refs_0_.refs_4_), channel_id=1, source_target_pairs={{4,8},{5,9},{6,10},{7,11},{8,4},{9,5},{10,6},{11,7},{20,24},{21,25... | collective-permute-start | bytes 2506760 | tf_op jit(solution)/shard_map/ppermute | solution.py:163
  13.1 22.7 %collective-permute-start.5 = (bf16[272,1536]{1,0:T(8,128)(2,1)}, bf16[272,1536]{1,0:T(8,128)(2,1)}, u32[]{:S(2)}, u32[]{:S(2)}) collective-permute-start(bf16[272,1536]{1,0:T(8,128)(2,1)} %get-tuple-element.76.refs_0_.refs_4_), channel_id=1, source_target_pairs={{0,4},{1,5},{2,6},{3,7},{4,0},{5,1},{6,2},{7,3},{8,12},{9,13},{10,... | collective-permute-start | bytes 2506760 | tf_op jit(solution)/shard_map/ppermute | solution.py:163
  16.6 19.2 %collective-permute-start.6 = (bf16[272,1536]{1,0:T(8,128)(2,1)}, bf16[272,1536]{1,0:T(8,128)(2,1)S(1)}, u32[]{:S(2)}, u32[]{:S(2)}) collective-permute-start(bf16[272,1536]{1,0:T(8,128)(2,1)} %get-tuple-element.76.refs_0_.refs_4_), channel_id=1, source_target_pairs={{0,1},{1,0},{2,3},{3,2},{4,5},{5,4},{6,7},{7,6},{8,9},{9,8},{10,11... | collective-permute-start | bytes 2506760 | tf_op jit(solution)/shard_map/ppermute | solution.py:163
  33.7 26.8 %collective-permute-start.2 = (bf16[768,768]{1,0:T(8,128)(2,1)}, bf16[768,768]{1,0:T(8,128)(2,1)S(1)}, u32[]{:S(2)}, u32[]{:S(2)}) collective-permute-start(bf16[768,768]{1,0:T(8,128)(2,1)} %get-tuple-element.72.refs_6_.refs_4_), channel_id=1, source_target_pairs={{0,16},{16,0},{1,17},{17,1},{2,18},{18,2},{3,19},{19,3},{4,20},{20... | collective-permute-start | bytes 3538952 | tf_op jit(solution)/shard_map/ppermute | solution.py:166
  34.1 27.0 %collective-permute-start.3 = (bf16[768,768]{1,0:T(8,128)(2,1)}, bf16[768,768]{1,0:T(8,128)(2,1)}, u32[]{:S(2)}, u32[]{:S(2)}) collective-permute-start(bf16[768,768]{1,0:T(8,128)(2,1)} %get-tuple-element.73.refs_4_.refs_2_), channel_id=1, source_target_pairs={{0,2},{1,3},{2,0},{3,1},{4,6},{5,7},{6,4},{7,5},{8,10},{9,11},{10,... | collective-permute-start | bytes 3538952 | tf_op jit(solution)/shard_map/ppermute | solution.py:163
  35.8 0.9 copy-start.5
  36.7 24.4 %collective-permute-start.10 = (bf16[272,1536]{1,0:T(8,128)(2,1)}, bf16[272,1536]{1,0:T(8,128)(2,1)}, u32[]{:S(2)}, u32[]{:S(2)}) collective-permute-start(bf16[272,1536]{1,0:T(8,128)(2,1)} %collective-permute-done.5.refs_2_), channel_id=1, source_target_pairs={{4,8},{5,9},{6,10},{7,11},{8,4},{9,5},{10,6},{11,7},{20,24},{21,25... | collective-permute-start | bytes 2506760 | tf_op jit(solution)/shard_map/ppermute | solution.py:163
  38.3 22.8 %collective-permute-start.11 = (bf16[272,1536]{1,0:T(8,128)(2,1)}, bf16[272,1536]{1,0:T(8,128)(2,1)}, u32[]{:S(2)}, u32[]{:S(2)}) collective-permute-start(bf16[272,1536]{1,0:T(8,128)(2,1)} %collective-permute-done.5.refs_2_), channel_id=1, source_target_pairs={{0,1},{1,0},{2,3},{3,2},{4,5},{5,4},{6,7},{7,6},{8,9},{9,8},{10,11... | collective-permute-start | bytes 2506760 | tf_op jit(solution)/shard_map/ppermute | solution.py:163
  38.3 23.1 %collective-permute-start.9 = (bf16[272,1536]{1,0:T(8,128)(2,1)}, bf16[272,1536]{1,0:T(8,128)(2,1)}, u32[]{:S(2)}, u32[]{:S(2)}) collective-permute-start(bf16[272,1536]{1,0:T(8,128)(2,1)} %collective-permute-done.4), channel_id=1, source_target_pairs={{0,4},{1,5},{2,6},{3,7},{4,0},{5,1},{6,2},{7,3},{8,12},{9,13},{10,... | collective-permute-start | bytes 2506760 | tf_op jit(solution)/shard_map/ppermute | solution.py:163
  41.9 25.0 %copy-start = (bf16[768,768]{1,0:T(8,128)(2,1)S(1)}, bf16[768,768]{1,0:T(8,128)(2,1)}, u32[]{:S(2)}) copy-start(bf16[768,768]{1,0:T(8,128)(2,1)} %get-tuple-element.73.refs_4_.refs_2_) | copy-start | bytes 3538948
  41.9 25.0 %copy-start.1 = (bf16[768,768]{1,0:T(8,128)(2,1)S(1)}, bf16[768,768]{1,0:T(8,128)(2,1)}, u32[]{:S(2)}) copy-start(bf16[768,768]{1,0:T(8,128)(2,1)} %get-tuple-element.72.refs_6_.refs_4_) | copy-start | bytes 3538948
  41.9 25.0 %copy-start.8 = (f32[8,128]{1,0:T(8,128)S(1)}, f32[8,128]{1,0:T(8,128)}, u32[]{:S(2)}) copy-start(f32[8,128]{1,0:T(8,128)} %get-tuple-element.112._) | copy-start | bytes 12292
  62.7 14.7 %collective-permute-start.13 = (bf16[272,1536]{1,0:T(8,128)(2,1)S(1)}, bf16[272,1536]{1,0:T(8,128)(2,1)S(1)}, u32[]{:S(2)}, u32[]{:S(2)}) collective-permute-start(bf16[272,1536]{1,0:T(8,128)(2,1)S(1)} %broadcast_select_fusion.1.refs_0_), channel_id=1, source_target_pairs={{0,1},{1,0},{2,3},{3,2},{4,5},{5,4},{6,7},{7,6},{8,9},{9,8},{10,11... | collective-permute-start | bytes 2506760 | tf_op jit(solution)/shard_map/ppermute | solution.py:163
  62.7 21.2 %collective-permute-start.12 = (bf16[272,1536]{1,0:T(8,128)(2,1)}, bf16[272,1536]{1,0:T(8,128)(2,1)S(1)}, u32[]{:S(2)}, u32[]{:S(2)}) collective-permute-start(bf16[272,1536]{1,0:T(8,128)(2,1)} %collective-permute-done.10), channel_id=1, source_target_pairs={{0,4},{1,5},{2,6},{3,7},{4,0},{5,1},{6,2},{7,3},{8,12},{9,13},{10,... | collective-permute-start | bytes 2506760 | tf_op jit(solution)/shard_map/ppermute | solution.py:163
  64.6 28.0 %collective-permute-start.7 = (bf16[768,768]{1,0:T(8,128)(2,1)S(1)}, bf16[768,768]{1,0:T(8,128)(2,1)S(1)}, u32[]{:S(2)}, u32[]{:S(2)}) collective-permute-start(bf16[768,768]{1,0:T(8,128)(2,1)S(1)} %collective-permute-done.refs_5_.refs_3_), channel_id=1, source_target_pairs={{0,2},{1,3},{2,0},{3,1},{4,6},{5,7},{6,4},{7,5},{8,10},{9,11},{10,... | collective-permute-start | bytes 3538952 | tf_op jit(solution)/shard_map/ppermute | solution.py:163
  65.5 27.8 %collective-permute-start.8 = (bf16[768,768]{1,0:T(8,128)(2,1)S(1)}, bf16[768,768]{1,0:T(8,128)(2,1)S(1)}, u32[]{:S(2)}, u32[]{:S(2)}) collective-permute-start(bf16[768,768]{1,0:T(8,128)(2,1)S(1)} %collective-permute-done.1.refs_6_.refs_14_), channel_id=1, source_target_pairs={{0,16},{16,0},{1,17},{17,1},{2,18},{18,2},{3,19},{19,3},{4,20},{20... | collective-permute-start | bytes 3538952 | tf_op jit(solution)/shard_map/ppermute | solution.py:166
  66.9 1.2 copy-start.3
  68.1 1.1 copy-start.6
  84.1 2.4 %collective-permute-start.14 = (bf16[272,1536]{1,0:T(8,128)(2,1)S(1)}, bf16[272,1536]{1,0:T(8,128)(2,1)S(1)}, u32[]{:S(2)}, u32[]{:S(2)}) collective-permute-start(bf16[272,1536]{1,0:T(8,128)(2,1)S(1)} %broadcast_select_fusion.refs_0_), channel_id=1, source_target_pairs={{0,1},{1,0},{2,3},{3,2},{4,5},{5,4},{6,7},{7,6},{8,9},{9,8},{10,11... | collective-permute-start | bytes 2506760 | tf_op jit(solution)/shard_map/ppermute | solution.py:163
  93.3 4.5 %copy-start.2 = (bf16[768,768]{1,0:T(8,128)(2,1)}, bf16[768,768]{1,0:T(8,128)(2,1)S(1)}, u32[]{:S(2)}) copy-start(bf16[768,768]{1,0:T(8,128)(2,1)S(1)} %collective-permute-done.8.refs_7_.refs_15_) | copy-start | bytes 3538948
  97.8 2.4 %collective-permute-start.15 = (bf16[256,1536]{1,0:T(8,128)(2,1)S(1)}, bf16[256,1536]{1,0:T(8,128)(2,1)S(1)}, u32[]{:S(2)}, u32[]{:S(2)}) collective-permute-start(bf16[256,1536]{1,0:T(8,128)(2,1)S(1)} %get-tuple-element.110), channel_id=1, source_target_pairs={{0,1},{1,0},{2,3},{3,2},{4,5},{5,4},{6,7},{7,6},{8,9},{9,8},{10,11... | collective-permute-start | bytes 2359304 | tf_op jit(solution)/shard_map/ppermute | solution.py:163
  100.2 1.2 copy-start.4
  100.2 1.4 copy-start.7
  100.4 19.6 %collective-permute-start.16 = (bf16[256,1536]{1,0:T(8,128)(2,1)S(1)}, bf16[256,1536]{1,0:T(8,128)(2,1)S(1)}, u32[]{:S(2)}, u32[]{:S(2)}) collective-permute-start(bf16[256,1536]{1,0:T(8,128)(2,1)S(1)} %add_convert_fusion.5), channel_id=1, source_target_pairs={{0,4},{1,5},{2,6},{3,7},{4,0},{5,1},{6,2},{7,3},{8,12},{9,13},{10,... | collective-permute-start | bytes 2359304 | tf_op jit(solution)/shard_map/ppermute | solution.py:163
  112.3 7.8 %collective-permute-start.17 = (bf16[256,1536]{1,0:T(8,128)(2,1)S(1)}, bf16[256,1536]{1,0:T(8,128)(2,1)S(1)}, u32[]{:S(2)}, u32[]{:S(2)}) collective-permute-start(bf16[256,1536]{1,0:T(8,128)(2,1)S(1)} %get-tuple-element.122), channel_id=1, source_target_pairs={{0,1},{1,0},{2,3},{3,2},{4,5},{5,4},{6,7},{7,6},{8,9},{9,8},{10,11... | collective-permute-start | bytes 2359304 | tf_op jit(solution)/shard_map/ppermute | solution.py:163
  112.5 7.5 %collective-permute-start.18 = (bf16[256,1536]{1,0:T(8,128)(2,1)S(1)}, bf16[256,1536]{1,0:T(8,128)(2,1)S(1)}, u32[]{:S(2)}, u32[]{:S(2)}) collective-permute-start(bf16[256,1536]{1,0:T(8,128)(2,1)S(1)} %get-tuple-element.123), channel_id=1, source_target_pairs={{0,1},{1,0},{2,3},{3,2},{4,5},{5,4},{6,7},{7,6},{8,9},{9,8},{10,11... | collective-permute-start | bytes 2359304 | tf_op jit(solution)/shard_map/ppermute | solution.py:163
  112.8 8.1 %collective-permute-start.21 = (bf16[256,1536]{1,0:T(8,128)(2,1)S(1)}, bf16[256,1536]{1,0:T(8,128)(2,1)S(1)}, u32[]{:S(2)}, u32[]{:S(2)}) collective-permute-start(bf16[256,1536]{1,0:T(8,128)(2,1)S(1)} %get-tuple-element.129), channel_id=1, source_target_pairs={{0,1},{1,0},{2,3},{3,2},{4,5},{5,4},{6,7},{7,6},{8,9},{9,8},{10,11... | collective-permute-start | bytes 2359304 | tf_op jit(solution)/shard_map/ppermute | solution.py:163
  120.2 5.2 %collective-permute-start.19 = (bf16[256,1536]{1,0:T(8,128)(2,1)S(1)}, bf16[256,1536]{1,0:T(8,128)(2,1)S(1)}, u32[]{:S(2)}, u32[]{:S(2)}) collective-permute-start(bf16[256,1536]{1,0:T(8,128)(2,1)S(1)} %add_convert_fusion.4), channel_id=1, source_target_pairs={{4,8},{5,9},{6,10},{7,11},{8,4},{9,5},{10,6},{11,7},{20,24},{21,25... | collective-permute-start | bytes 2359304 | tf_op jit(solution)/shard_map/ppermute | solution.py:163
  121.1 21.4 %collective-permute-start.22 = (bf16[256,1536]{1,0:T(8,128)(2,1)S(1)}, bf16[256,1536]{1,0:T(8,128)(2,1)S(1)}, u32[]{:S(2)}, u32[]{:S(2)}) collective-permute-start(bf16[256,1536]{1,0:T(8,128)(2,1)S(1)} %add_convert_fusion.2), channel_id=1, source_target_pairs={{0,4},{1,5},{2,6},{3,7},{4,0},{5,1},{6,2},{7,3},{8,12},{9,13},{10,... | collective-permute-start | bytes 2359304 | tf_op jit(solution)/shard_map/ppermute | solution.py:163
  125.7 33.3 %copy-start.9 = (bf16[256,1536]{1,0:T(8,128)(2,1)S(1)}, bf16[256,1536]{1,0:T(8,128)(2,1)}, u32[]{:S(2)}) copy-start(bf16[256,1536]{1,0:T(8,128)(2,1)} %tokens.1) | copy-start | bytes 2359300
  125.8 33.3 %collective-permute-start.20 = (bf16[256,1536]{1,0:T(8,128)(2,1)S(1)}, bf16[256,1536]{1,0:T(8,128)(2,1)S(1)}, u32[]{:S(2)}, u32[]{:S(2)}) collective-permute-start(bf16[256,1536]{1,0:T(8,128)(2,1)S(1)} %add_convert_fusion.3), channel_id=1, source_target_pairs={{0,4},{1,5},{2,6},{3,7},{4,0},{5,1},{6,2},{7,3},{8,12},{9,13},{10,... | collective-permute-start | bytes 2359304 | tf_op jit(solution)/shard_map/ppermute | solution.py:163
  142.8 16.3 %collective-permute-start.23 = (bf16[256,1536]{1,0:T(8,128)(2,1)S(1)}, bf16[256,1536]{1,0:T(8,128)(2,1)S(1)}, u32[]{:S(2)}, u32[]{:S(2)}) collective-permute-start(bf16[256,1536]{1,0:T(8,128)(2,1)S(1)} %add_convert_fusion.1), channel_id=1, source_target_pairs={{4,8},{5,9},{6,10},{7,11},{8,4},{9,5},{10,6},{11,7},{20,24},{21,25... | collective-permute-start | bytes 2359304 | tf_op jit(solution)/shard_map/ppermute | solution.py:163

commit v5 on v4

--- a/solution.py
+++ b/solution.py
@@ -156,8 +156,6 @@
     rows, width = tokens.shape
     half = width // 2
     hid = w_gate.shape[2]
-    z = lax.axis_index("tensor") // 4
-    middle = (z == 1) | (z == 2)
 
     def send(v, pairs):
         return lax.ppermute(v, "tensor", pairs)
@@ -165,12 +163,7 @@
     def across(v):
         return lax.ppermute(v, "dp", [(0, 1), (1, 0)])
 
-    def over(*pairs):
-        return [(a * 4 + r, b * 4 + r) for a, b in pairs for r in range(4)]
-
-    by_core, by_y = ([(i, i ^ bit) for i in range(16)] for bit in (1, 2))
-    outer = over((0, 1), (1, 0), (2, 3), (3, 2))
-    inner = over((1, 2), (2, 1))
+    by_core, by_y, outer, skip = ([(i, i ^ bit) for i in range(16)] for bit in (1, 2, 4, 8))
     smem = pl.BlockSpec(memory_space=pltpu.SMEM)
     vmem = pl.BlockSpec(memory_space=pltpu.VMEM)
     anywhere = pl.BlockSpec(memory_space=pl.ANY)
@@ -223,29 +216,23 @@
     def add(*terms):
         return sum(v.astype(F32) for v in terms).astype(BF16)
 
-    s_m = send(s_0, inner)
     s_a = send(s_0, outer)
+    s_b = send(s_0, skip)
     m_0 = send(s_0, by_core)
     x_0, y_1, own_0, own_1 = together(x_0, y_1, *own)
     x_1 = across(own_1)
     y_0 = send(own_0, by_y)
-    s_m, s_a, m_0 = together(s_m, s_a, m_0)
-    s_b = send(s_m, outer)
-    s_n = send(s_a, inner)
-    m_a = send(s_a, by_core)
+    s_a, m_0 = together(s_a, m_0)
+    s_b, s_a = together(s_b, s_a)
+    s_c = send(s_b, outer)
+    m_a, m_b = send(s_a, by_core), send(s_b, by_core)
     x_1, y_0, x_0, y_1 = together(x_1, y_0, x_0, y_1)
     d_0 = send(x_0, by_y)
     d_1 = across(y_1)
-    s_b, s_n, m_a = together(s_b, s_n, m_a)
-    s_c = send(s_n, outer)
-    s_b = jnp.where(middle, s_m, s_b)
-    m_b = send(s_b, by_core)
     mine = (own[0], x_0, own[1], x_1)
-    u_0, v_0, u_a, v_a = run((s_0, m_0, s_a, m_a), [(0, mine, 0, 4)], [None] * 4)
-    m_b, u_0, v_0, u_a, v_a = together(m_b, u_0, v_0, u_a, v_a)
-    u_b, v_b = run((s_b, m_b), [(0, mine, 0, 2)], [None] * 2)
-    s_c, u_b, v_b = together(s_c, u_b, v_b)
-    s_c = jnp.where(middle, s_n, s_c)
+    m_a, m_b = together(m_a, m_b)
+    u_0, v_0, u_a, v_a, u_b, v_b = run((s_0, m_0, s_a, m_a, s_b, m_b), [(0, mine, 0, 6)], [None] * 6)
+    s_c, u_0, v_0, u_a, v_a, u_b, v_b = together(s_c, u_0, v_0, u_a, v_a, u_b, v_b)
     m_c = send(s_c, by_core)
     (m_c,) = together(m_c)
     u_c, v_c = run((s_c, m_c), [(0, mine, 0, 2)], [None] * 2)
@@ -255,20 +242,17 @@
     r_c = send(o_c, by_core)
 
     r_c, p_c = together(r_c, p_c)
-    q_c = add(p_c, r_c)
-    r_n = send(q_c, outer)
+    r_n = send(add(p_c, r_c), outer)
     p_b, o_b, p_a, o_a, p_0, o_0 = run((s_b, m_b, s_a, m_a, s_0, m_0), [(1, theirs, 0, 6)], [u_b, v_b, u_a, v_a, u_0, v_0])
     r_b, r_a, r_0 = send(o_b, by_core), send(o_a, by_core), send(o_0, by_core)
-    r_b, p_b = together(r_b, p_b)
-    q_b = add(p_b, r_b)
-    r_m = send(q_b, outer)
-    r_n, r_a, r_0, p_a = together(r_n, r_a, r_0, p_a)
-    r_i = send(add(q_c, r_n), inner)
+    r_n, p_a = lax.optimization_barrier((r_n, p_a))
+    r_b, r_a, p_b, r_n = lax.optimization_barrier((r_b, r_a, p_b, r_n))
+    r_o = send(add(p_a, r_a), outer)
+    r_m = send(add(p_b, r_b, r_n), skip)
+    order[0] = p_0
+    (r_o,) = together(r_o)
     (r_m,) = together(r_m)
-    r_m = send(add(q_b, r_m), inner)
-    (r_i,) = together(r_i)
-    r_o = send(add(p_a, r_a, r_i), outer)
-    return add(tokens, p_0, r_0, r_o, r_m)
+    return add(tokens, order[0], r_0, r_o, r_m)
 
 
 def solution(mesh):

time: 162 us -> 154 us (0.951)
  starting transfers between devices: 45.1 us -> 20.8 us
  waiting for transfers between devices: 69.1 us -> 92.3 us
  Pallas kernels: 37.1 us -> 32.8 us
  other arithmetic: 3.82 us -> 2.04 us
    ppermute x21 -> x17, waiting for transfers between devices: 34.1 us -> 67.9 us  [send(): return lax.ppermute(v, 'tensor', pairs)]
    ppermute x21 -> x17, starting transfers between devices: 40.3 us -> 16 us  [send(): return lax.ppermute(v, 'tensor', pairs)]
    ppermute x3, waiting for transfers between devices: 35 us -> 24.4 us  [across(): return lax.ppermute(v, 'dp', [(0, 1), (1, 0)])]
    pallas_call x5 -> x4, Pallas kernels: 31.4 us -> 27.1 us  [run(): pl.pallas_call(functools.partial(expert_kernel, tuple(((e, first, last) f...]
  transfers between devices with their start and end apart: 24 -> 20, of which waited for: 12 -> 13; matrix products, arithmetic and copies ran while one was open for 1% -> 1% of each run, Pallas kernels for 18% -> 17%
where the time goes in v5:
time: 154 us
  waiting for transfers between devices  92.3 us (60%)
  Pallas kernels  32.8 us (21%)
  starting transfers between devices  20.8 us (14%)
  local copies, waits for them, and re-layouts  5 us (3%)
  other arithmetic  2.04 us (1%)
    ppermute x17, waiting for transfers between devices, send(): return lax.ppermute(v, 'tensor', pairs)  67.9 us
    pallas_call x4, Pallas kernels, run(): pl.pallas_call(functools.partial(expert_kernel, tuple(((e, first, last) f...  27.1 us
    ppermute x3, waiting for transfers between devices, across(): return lax.ppermute(v, 'dp', [(0, 1), (1, 0)])  24.4 us
    ppermute x17, starting transfers between devices, send(): return lax.ppermute(v, 'tensor', pairs)  16 us
    ppermute x3, starting transfers between devices, across(): return lax.ppermute(v, 'dp', [(0, 1), (1, 0)])  4.79 us
    unnamed x22, local copies, waits for them, and re-layouts  4.4 us
    pallas_call x1, Pallas kernels, lanes(): pl.pallas_call(pack_kernel, out_shape=(jax.ShapeDtypeStruct((half, half),...  3.1 us
  transfers between devices with their start and end apart: 20, of which 13 were waited for; matrix products, arithmetic and copies ran while one was open for 1% of the time, Pallas kernels for 17%

profile of v5, /device:TPU:0, one launch (start us, length us, event | category | flops | bytes accessed | tf_op | source)
XLA Modules:
  0.0 153.7 jit_solution(6520470901602618850)
XLA Ops:
  0.0 3.1 %pack.1 = (bf16[768,768]{1,0:T(8,128)(2,1)}, bf16[768,768]{1,0:T(8,128)(2,1)}) custom-call(bf16[768,512]{1,0:T(8,128)(2,1)} %bitcast.5, bf16[768,512]{1,0:T(8,128)(2,1)} %bitcast.6, bf16[512,768]{1,0:T(8,128)(2,1)} %bitcast.7), custom_call_target="tpu_custom_call" | custom-call | tf_op jit(solution)/shard_map/pack/pallas_call | solution.py:171
  3.1 3.0 %collective-permute-start = (bf16[768,768]{1,0:T(8,128)(2,1)}, bf16[768,768]{1,0:T(8,128)(2,1)S(1)}, u32[]{:S(2)}, u32[]{:S(2)}) collective-permute-start(bf16[768,768]{1,0:T(8,128)(2,1)} %get-tuple-element.76.refs_6_.refs_2_), channel_id=1, source_target_pairs={{0,16},{16,0},{1,17},{17,1},{2,18},{18,2},{3,19},{19,3},{4,20},{20... | collective-permute-start | bytes 3538952 | tf_op jit(solution)/shard_map/ppermute | solution.py:164
  6.1 1.5 collective-permute-start.1
  7.6 0.6 reshape.3.gain
  8.9 2.6 %prologue.1 = (bf16[272,1536]{1,0:T(8,128)(2,1)}, f32[8,128]{1,0:T(8,128)}) custom-call(s32[1]{0:T(128)S(6)} %copy.9.lengths, bf16[256,1536]{1,0:T(8,128)(2,1)} %tokens.1, f32[1,1536]{1,0:T(1,128)} %reshape.3.gain, bf16[16,1536]{1,0:T(8,128)(2,1)} %bitcast.8, s32[8,256]{1,0:T(8,128)} %bitcast.9), custom_call_target="tpu_custom_call" | custom-call | tf_op jit(solution)/shard_map/prologue/pallas_call | solution.py:181
  11.5 1.6 %collective-permute-start.5 = (bf16[272,1536]{1,0:T(8,128)(2,1)}, bf16[272,1536]{1,0:T(8,128)(2,1)S(1)}, u32[]{:S(2)}, u32[]{:S(2)}) collective-permute-start(bf16[272,1536]{1,0:T(8,128)(2,1)} %get-tuple-element.79.refs_0_.refs_4_), channel_id=1, source_target_pairs={{0,4},{1,5},{2,6},{3,7},{4,0},{5,1},{6,2},{7,3},{8,12},{9,13},{10,... | collective-permute-start | bytes 2506760 | tf_op jit(solution)/shard_map/ppermute | solution.py:161
  13.0 2.6 %collective-permute-start.4 = (bf16[272,1536]{1,0:T(8,128)(2,1)}, bf16[272,1536]{1,0:T(8,128)(2,1)S(1)}, u32[]{:S(2)}, u32[]{:S(2)}) collective-permute-start(bf16[272,1536]{1,0:T(8,128)(2,1)} %get-tuple-element.79.refs_0_.refs_4_), channel_id=1, source_target_pairs={{0,8},{1,9},{2,10},{3,11},{4,12},{5,13},{6,14},{7,15},{8,0},{9,1},... | collective-permute-start | bytes 2506760 | tf_op jit(solution)/shard_map/ppermute | solution.py:161
  15.6 16.7 %collective-permute-done.refs_7_.refs_3_ = bf16[768,768]{1,0:T(8,128)(2,1)S(1)} collective-permute-done((bf16[768,768]{1,0:T(8,128)(2,1)}, bf16[768,768]{1,0:T(8,128)(2,1)S(1)}, u32[]{:S(2)}, u32[]{:S(2)}) %collective-permute-start) | collective-permute-done | bytes 1179680 | tf_op jit(solution)/shard_map/ppermute | solution.py:164
  32.3 1.5 collective-permute-done.1.refs_6_.refs_14_
  33.8 0.4 collective-permute-start.2
  34.1 1.7 %collective-permute-start.3 = (bf16[768,768]{1,0:T(8,128)(2,1)}, bf16[768,768]{1,0:T(8,128)(2,1)S(1)}, u32[]{:S(2)}, u32[]{:S(2)}) collective-permute-start(bf16[768,768]{1,0:T(8,128)(2,1)} %get-tuple-element.76.refs_6_.refs_2_), channel_id=1, source_target_pairs={{0,2},{1,3},{2,0},{3,1},{4,6},{5,7},{6,4},{7,5},{8,10},{9,11},{10,... | collective-permute-start | bytes 3538952 | tf_op jit(solution)/shard_map/ppermute | solution.py:161
  35.8 11.9 %collective-permute-done.5.refs_2_ = bf16[272,1536]{1,0:T(8,128)(2,1)S(1)} collective-permute-done((bf16[272,1536]{1,0:T(8,128)(2,1)}, bf16[272,1536]{1,0:T(8,128)(2,1)S(1)}, u32[]{:S(2)}, u32[]{:S(2)}) %collective-permute-start.5) | collective-permute-done | bytes 835616 | tf_op jit(solution)/shard_map/ppermute | solution.py:161
  47.7 0.0 collective-permute-done.6.refs_1_.refs_5_
  47.7 5.4 %collective-permute-done.4.refs_4_.refs_0_ = bf16[272,1536]{1,0:T(8,128)(2,1)S(1)} collective-permute-done((bf16[272,1536]{1,0:T(8,128)(2,1)}, bf16[272,1536]{1,0:T(8,128)(2,1)S(1)}, u32[]{:S(2)}, u32[]{:S(2)}) %collective-permute-start.4) | collective-permute-done | bytes 835616 | tf_op jit(solution)/shard_map/ppermute | solution.py:161
  53.1 0.0 collective-permute-start.11
  53.1 0.5 collective-permute-start.10
  53.6 6.9 %collective-permute-done.2.refs_9_.refs_5_ = bf16[768,768]{1,0:T(8,128)(2,1)S(1)} collective-permute-done((bf16[768,768]{1,0:T(8,128)(2,1)}, bf16[768,768]{1,0:T(8,128)(2,1)S(1)}, u32[]{:S(2)}, u32[]{:S(2)}) %collective-permute-start.2) | collective-permute-done | bytes 1179680 | tf_op jit(solution)/shard_map/ppermute | solution.py:164
  60.5 0.4 collective-permute-done.3.refs_4_.refs_12_
  60.9 1.4 collective-permute-start.7
  62.3 1.4 collective-permute-start.8
  63.8 1.3 copy-done
  65.0 1.3 copy-done.2
  66.3 1.1 copy-done.5
  67.4 0.7 copy-done.7
  68.1 9.5 %experts.4 = (bf16[256,1536]{1,0:T(8,128)(2,1)S(1)}, bf16[256,1536]{1,0:T(8,128)(2,1)S(1)}, bf16[256,1536]{1,0:T(8,128)(2,1)S(1)}, bf16[256,1536]{1,0:T(8,128)(2...) custom-call(f32[8,128]{1,0:T(8,128)S(1)} %copy-done.7, bf16[272,1536]{1,0:T(8,128)(2,1)S(1)} %copy-done.5, ...), custom_call_target="tpu_custom_call" | custom-call | flops 1 | bytes 1 | tf_op jit(solution)/shard_map/experts/pallas_call | solution.py:199
  77.7 0.0 collective-permute-done.9.refs_0_
  77.7 0.1 collective-permute-start.12
  77.8 2.3 %collective-permute-done.12.refs_1_ = bf16[272,1536]{1,0:T(8,128)(2,1)S(1)} collective-permute-done((bf16[272,1536]{1,0:T(8,128)(2,1)S(1)}, bf16[272,1536]{1,0:T(8,128)(2,1)S(1)}, u32[]{:S(2)}, u32[]{:S(2)}) %collective-permute-start.12) | collective-permute-done | bytes 835616 | tf_op jit(solution)/shard_map/ppermute | solution.py:161
  80.1 4.0 %experts.5 = (bf16[256,1536]{1,0:T(8,128)(2,1)S(1)}, bf16[256,1536]{1,0:T(8,128)(2,1)S(1)}) custom-call(f32[8,128]{1,0:T(8,128)S(1)} %copy-done.8, bf16[272,1536]{1,0:T(8,128)(2,1)S(1)} %collective-permute-done.9.refs_0_, bf16[272,1536]{1,0:T(8,128)(2,1)S(1)} %collective-permute-done.12.refs_1_, bf16[768,768]{1,0:T(8,128)(2,1)S(1)} %copy-done.1, ...), custom_call_target="tpu_custom_call" | custom-call | flops 1 | bytes 1 | tf_op jit(solution)/shard_map/experts/pallas_call | solution.py:199
  84.2 2.4 %collective-permute-done.7.refs_5_.refs_13_ = bf16[768,768]{1,0:T(8,128)(2,1)S(1)} collective-permute-done((bf16[768,768]{1,0:T(8,128)(2,1)S(1)}, bf16[768,768]{1,0:T(8,128)(2,1)S(1)}, u32[]{:S(2)}, u32[]{:S(2)}) %collective-permute-start.7) | collective-permute-done | bytes 1179680 | tf_op jit(solution)/shard_map/ppermute | solution.py:161
  86.5 0.9 collective-permute-done.8.refs_7_.refs_15_
  87.4 4.2 %experts.6 = (bf16[256,1536]{1,0:T(8,128)(2,1)S(1)}, bf16[256,1536]{1,0:T(8,128)(2,1)S(1)}) custom-call(f32[8,128]{1,0:T(8,128)S(1)} %copy-done.8, bf16[272,1536]{1,0:T(8,128)(2,1)S(1)} %collective-permute-done.9.refs_0_, bf16[272,1536]{1,0:T(8,128)(2,1)S(1)} %collective-permute-done.12.refs_1_, bf16[256,1536]{1,0:T(8,128)(2,1)S(1)} %get-tuple-element.107.refs_2_, ...), custom_call_target="tpu_custom_call" | custom-call | flops 1 | bytes 1 | tf_op jit(solution)/shard_map/experts/pallas_call | solution.py:199
  91.7 0.1 collective-permute-start.13
  91.8 2.3 %collective-permute-done.13 = bf16[256,1536]{1,0:T(8,128)(2,1)S(1)} collective-permute-done((bf16[256,1536]{1,0:T(8,128)(2,1)S(1)}, bf16[256,1536]{1,0:T(8,128)(2,1)S(1)}, u32[]{:S(2)}, u32[]{:S(2)}) %collective-permute-start.13) | collective-permute-done | bytes 786464 | tf_op jit(solution)/shard_map/ppermute | solution.py:161
  94.0 0.2 add_convert_fusion.3
  94.2 1.6 %collective-permute-start.16 = (bf16[256,1536]{1,0:T(8,128)(2,1)S(1)}, bf16[256,1536]{1,0:T(8,128)(2,1)S(1)}, u32[]{:S(2)}, u32[]{:S(2)}) collective-permute-start(bf16[256,1536]{1,0:T(8,128)(2,1)S(1)} %add_convert_fusion.3), channel_id=1, source_target_pairs={{0,4},{1,5},{2,6},{3,7},{4,0},{5,1},{6,2},{7,3},{8,12},{9,13},{10,... | collective-permute-start | bytes 2359304 | tf_op jit(solution)/shard_map/ppermute | solution.py:161
  95.9 9.3 %experts.7 = (bf16[256,1536]{1,0:T(8,128)(2,1)S(1)}, bf16[256,1536]{1,0:T(8,128)(2,1)S(1)}, bf16[256,1536]{1,0:T(8,128)(2,1)S(1)}, bf16[256,1536]{1,0:T(8,128)(2...) custom-call(f32[8,128]{1,0:T(8,128)S(1)} %copy-done.8, ...), custom_call_target="tpu_custom_call" | custom-call | flops 1 | bytes 1 | tf_op jit(solution)/shard_map/experts/pallas_call | solution.py:199
  105.2 0.1 collective-permute-start.14
  105.3 0.5 collective-permute-start.15
  105.8 8.1 %collective-permute-done.16 = bf16[256,1536]{1,0:T(8,128)(2,1)S(1)} collective-permute-done((bf16[256,1536]{1,0:T(8,128)(2,1)S(1)}, bf16[256,1536]{1,0:T(8,128)(2,1)S(1)}, u32[]{:S(2)}, u32[]{:S(2)}) %collective-permute-start.16) | collective-permute-done | bytes 786464 | tf_op jit(solution)/shard_map/ppermute | solution.py:161
  113.9 0.2 add_convert_fusion.1
  114.1 0.0 copy-start.9
  114.1 1.6 %collective-permute-start.18 = (bf16[256,1536]{1,0:T(8,128)(2,1)S(1)}, bf16[256,1536]{1,0:T(8,128)(2,1)S(1)}, u32[]{:S(2)}, u32[]{:S(2)}) collective-permute-start(bf16[256,1536]{1,0:T(8,128)(2,1)S(1)} %add_convert_fusion.1), channel_id=1, source_target_pairs={{0,4},{1,5},{2,6},{3,7},{4,0},{5,1},{6,2},{7,3},{8,12},{9,13},{10,... | collective-permute-start | bytes 2359304 | tf_op jit(solution)/shard_map/ppermute | solution.py:161
  115.7 0.3 add_convert_fusion.2
  116.0 2.6 %collective-permute-start.17 = (bf16[256,1536]{1,0:T(8,128)(2,1)S(1)}, bf16[256,1536]{1,0:T(8,128)(2,1)S(1)}, u32[]{:S(2)}, u32[]{:S(2)}) collective-permute-start(bf16[256,1536]{1,0:T(8,128)(2,1)S(1)} %add_convert_fusion.2), channel_id=1, source_target_pairs={{0,8},{1,9},{2,10},{3,11},{4,12},{5,13},{6,14},{7,15},{8,0},{9,1},... | collective-permute-start | bytes 2359304 | tf_op jit(solution)/shard_map/ppermute | solution.py:161
  118.7 30.6 %collective-permute-done.18 = bf16[256,1536]{1,0:T(8,128)(2,1)S(1)} collective-permute-done((bf16[256,1536]{1,0:T(8,128)(2,1)S(1)}, bf16[256,1536]{1,0:T(8,128)(2,1)S(1)}, u32[]{:S(2)}, u32[]{:S(2)}) %collective-permute-start.18) | collective-permute-done | bytes 786464 | tf_op jit(solution)/shard_map/ppermute | solution.py:161
  149.3 3.1 %collective-permute-done.17 = bf16[256,1536]{1,0:T(8,128)(2,1)S(1)} collective-permute-done((bf16[256,1536]{1,0:T(8,128)(2,1)S(1)}, bf16[256,1536]{1,0:T(8,128)(2,1)S(1)}, u32[]{:S(2)}, u32[]{:S(2)}) %collective-permute-start.17) | collective-permute-done | bytes 786464 | tf_op jit(solution)/shard_map/ppermute | solution.py:161
  152.4 1.4 add_convert_fusion
  (25 shorter events, 0.1 us)
Async XLA Ops:
  0.0 7.6 %copy-start.10 = (f32[1536]{0:T(1024)S(1)}, f32[1536]{0:T(1024)}, u32[]{:S(2)}) copy-start(f32[1536]{0:T(1024)} %param.11) | copy-start | bytes 18436
  3.1 29.2 %collective-permute-start = (bf16[768,768]{1,0:T(8,128)(2,1)}, bf16[768,768]{1,0:T(8,128)(2,1)S(1)}, u32[]{:S(2)}, u32[]{:S(2)}) collective-permute-start(bf16[768,768]{1,0:T(8,128)(2,1)} %get-tuple-element.76.refs_6_.refs_2_), channel_id=1, source_target_pairs={{0,16},{16,0},{1,17},{17,1},{2,18},{18,2},{3,19},{19,3},{4,20},{20... | collective-permute-start | bytes 3538952 | tf_op jit(solution)/shard_map/ppermute | solution.py:164
  6.1 27.6 %collective-permute-start.1 = (bf16[768,768]{1,0:T(8,128)(2,1)}, bf16[768,768]{1,0:T(8,128)(2,1)S(1)}, u32[]{:S(2)}, u32[]{:S(2)}) collective-permute-start(bf16[768,768]{1,0:T(8,128)(2,1)} %get-tuple-element.75.refs_8_.refs_4_), channel_id=1, source_target_pairs={{0,2},{1,3},{2,0},{3,1},{4,6},{5,7},{6,4},{7,5},{8,10},{9,11},{10,... | collective-permute-start | bytes 3538952 | tf_op jit(solution)/shard_map/ppermute | solution.py:161
  11.5 36.3 %collective-permute-start.5 = (bf16[272,1536]{1,0:T(8,128)(2,1)}, bf16[272,1536]{1,0:T(8,128)(2,1)S(1)}, u32[]{:S(2)}, u32[]{:S(2)}) collective-permute-start(bf16[272,1536]{1,0:T(8,128)(2,1)} %get-tuple-element.79.refs_0_.refs_4_), channel_id=1, source_target_pairs={{0,4},{1,5},{2,6},{3,7},{4,0},{5,1},{6,2},{7,3},{8,12},{9,13},{10,... | collective-permute-start | bytes 2506760 | tf_op jit(solution)/shard_map/ppermute | solution.py:161
  13.0 34.7 %collective-permute-start.6 = (bf16[272,1536]{1,0:T(8,128)(2,1)}, bf16[272,1536]{1,0:T(8,128)(2,1)S(1)}, u32[]{:S(2)}, u32[]{:S(2)}) collective-permute-start(bf16[272,1536]{1,0:T(8,128)(2,1)} %get-tuple-element.79.refs_0_.refs_4_), channel_id=1, source_target_pairs={{0,1},{1,0},{2,3},{3,2},{4,5},{5,4},{6,7},{7,6},{8,9},{9,8},{10,11... | collective-permute-start | bytes 2506760 | tf_op jit(solution)/shard_map/ppermute | solution.py:161
  13.0 40.1 %collective-permute-start.4 = (bf16[272,1536]{1,0:T(8,128)(2,1)}, bf16[272,1536]{1,0:T(8,128)(2,1)S(1)}, u32[]{:S(2)}, u32[]{:S(2)}) collective-permute-start(bf16[272,1536]{1,0:T(8,128)(2,1)} %get-tuple-element.79.refs_0_.refs_4_), channel_id=1, source_target_pairs={{0,8},{1,9},{2,10},{3,11},{4,12},{5,13},{6,14},{7,15},{8,0},{9,1},... | collective-permute-start | bytes 2506760 | tf_op jit(solution)/shard_map/ppermute | solution.py:161
  33.8 26.7 %collective-permute-start.2 = (bf16[768,768]{1,0:T(8,128)(2,1)}, bf16[768,768]{1,0:T(8,128)(2,1)S(1)}, u32[]{:S(2)}, u32[]{:S(2)}) collective-permute-start(bf16[768,768]{1,0:T(8,128)(2,1)} %get-tuple-element.75.refs_8_.refs_4_), channel_id=1, source_target_pairs={{0,16},{16,0},{1,17},{17,1},{2,18},{18,2},{3,19},{19,3},{4,20},{20... | collective-permute-start | bytes 3538952 | tf_op jit(solution)/shard_map/ppermute | solution.py:164
  34.1 26.8 %collective-permute-start.3 = (bf16[768,768]{1,0:T(8,128)(2,1)}, bf16[768,768]{1,0:T(8,128)(2,1)S(1)}, u32[]{:S(2)}, u32[]{:S(2)}) collective-permute-start(bf16[768,768]{1,0:T(8,128)(2,1)} %get-tuple-element.76.refs_6_.refs_2_), channel_id=1, source_target_pairs={{0,2},{1,3},{2,0},{3,1},{4,6},{5,7},{6,4},{7,5},{8,10},{9,11},{10,... | collective-permute-start | bytes 3538952 | tf_op jit(solution)/shard_map/ppermute | solution.py:161
  53.1 10.6 %collective-permute-start.11 = (bf16[272,1536]{1,0:T(8,128)(2,1)S(1)}, bf16[272,1536]{1,0:T(8,128)(2,1)S(1)}, u32[]{:S(2)}, u32[]{:S(2)}) collective-permute-start(bf16[272,1536]{1,0:T(8,128)(2,1)S(1)} %collective-permute-done.4.refs_4_.refs_0_), channel_id=1, source_target_pairs={{0,1},{1,0},{2,3},{3,2},{4,5},{5,4},{6,7},{7,6},{8,9},{9,8},{10,11... | collective-permute-start | bytes 2506760 | tf_op jit(solution)/shard_map/ppermute | solution.py:161
  53.1 10.6 %collective-permute-start.10 = (bf16[272,1536]{1,0:T(8,128)(2,1)S(1)}, bf16[272,1536]{1,0:T(8,128)(2,1)S(1)}, u32[]{:S(2)}, u32[]{:S(2)}) collective-permute-start(bf16[272,1536]{1,0:T(8,128)(2,1)S(1)} %collective-permute-done.5.refs_2_), channel_id=1, source_target_pairs={{0,1},{1,0},{2,3},{3,2},{4,5},{5,4},{6,7},{7,6},{8,9},{9,8},{10,11... | collective-permute-start | bytes 2506760 | tf_op jit(solution)/shard_map/ppermute | solution.py:161
  53.6 24.0 %collective-permute-start.9 = (bf16[272,1536]{1,0:T(8,128)(2,1)S(1)}, bf16[272,1536]{1,0:T(8,128)(2,1)S(1)}, u32[]{:S(2)}, u32[]{:S(2)}) collective-permute-start(bf16[272,1536]{1,0:T(8,128)(2,1)S(1)} %collective-permute-done.4.refs_4_.refs_0_), channel_id=1, source_target_pairs={{0,4},{1,5},{2,6},{3,7},{4,0},{5,1},{6,2},{7,3},{8,12},{9,13},{10,... | collective-permute-start | bytes 2506760 | tf_op jit(solution)/shard_map/ppermute | solution.py:161
  60.9 25.6 %collective-permute-start.7 = (bf16[768,768]{1,0:T(8,128)(2,1)S(1)}, bf16[768,768]{1,0:T(8,128)(2,1)S(1)}, u32[]{:S(2)}, u32[]{:S(2)}) collective-permute-start(bf16[768,768]{1,0:T(8,128)(2,1)S(1)} %collective-permute-done.refs_7_.refs_3_), channel_id=1, source_target_pairs={{0,2},{1,3},{2,0},{3,1},{4,6},{5,7},{6,4},{7,5},{8,10},{9,11},{10,... | collective-permute-start | bytes 3538952 | tf_op jit(solution)/shard_map/ppermute | solution.py:161
  62.3 25.1 %collective-permute-start.8 = (bf16[768,768]{1,0:T(8,128)(2,1)S(1)}, bf16[768,768]{1,0:T(8,128)(2,1)S(1)}, u32[]{:S(2)}, u32[]{:S(2)}) collective-permute-start(bf16[768,768]{1,0:T(8,128)(2,1)S(1)} %collective-permute-done.1.refs_6_.refs_14_), channel_id=1, source_target_pairs={{0,16},{16,0},{1,17},{17,1},{2,18},{18,2},{3,19},{19,3},{4,20},{20... | collective-permute-start | bytes 3538952 | tf_op jit(solution)/shard_map/ppermute | solution.py:164
  63.8 1.3 copy-start
  65.0 1.3 copy-start.2
  66.3 1.1 copy-start.5
  67.4 0.7 copy-start.7
  68.1 12.0 %copy-start.1 = (bf16[768,768]{1,0:T(8,128)(2,1)S(1)}, bf16[768,768]{1,0:T(8,128)(2,1)}, u32[]{:S(2)}) copy-start(bf16[768,768]{1,0:T(8,128)(2,1)} %get-tuple-element.76.refs_6_.refs_2_) | copy-start | bytes 3538948
  68.1 12.0 %copy-start.3 = (bf16[768,768]{1,0:T(8,128)(2,1)S(1)}, bf16[768,768]{1,0:T(8,128)(2,1)}, u32[]{:S(2)}) copy-start(bf16[768,768]{1,0:T(8,128)(2,1)} %get-tuple-element.75.refs_8_.refs_4_) | copy-start | bytes 3538948
  68.1 12.0 %copy-start.8 = (f32[8,128]{1,0:T(8,128)S(1)}, f32[8,128]{1,0:T(8,128)}, u32[]{:S(2)}) copy-start(f32[8,128]{1,0:T(8,128)} %get-tuple-element.114._) | copy-start | bytes 12292
  77.7 2.4 %collective-permute-start.12 = (bf16[272,1536]{1,0:T(8,128)(2,1)S(1)}, bf16[272,1536]{1,0:T(8,128)(2,1)S(1)}, u32[]{:S(2)}, u32[]{:S(2)}) collective-permute-start(bf16[272,1536]{1,0:T(8,128)(2,1)S(1)} %collective-permute-done.9.refs_0_), channel_id=1, source_target_pairs={{0,1},{1,0},{2,3},{3,2},{4,5},{5,4},{6,7},{7,6},{8,9},{9,8},{10,11... | collective-permute-start | bytes 2506760 | tf_op jit(solution)/shard_map/ppermute | solution.py:161
  87.4 4.2 %copy-start.4 = (bf16[768,768]{1,0:T(8,128)(2,1)}, bf16[768,768]{1,0:T(8,128)(2,1)S(1)}, u32[]{:S(2)}) copy-start(bf16[768,768]{1,0:T(8,128)(2,1)S(1)} %collective-permute-done.8.refs_7_.refs_15_) | copy-start | bytes 3538948
  91.7 2.4 %collective-permute-start.13 = (bf16[256,1536]{1,0:T(8,128)(2,1)S(1)}, bf16[256,1536]{1,0:T(8,128)(2,1)S(1)}, u32[]{:S(2)}, u32[]{:S(2)}) collective-permute-start(bf16[256,1536]{1,0:T(8,128)(2,1)S(1)} %get-tuple-element.112), channel_id=1, source_target_pairs={{0,1},{1,0},{2,3},{3,2},{4,5},{5,4},{6,7},{7,6},{8,9},{9,8},{10,11... | collective-permute-start | bytes 2359304 | tf_op jit(solution)/shard_map/ppermute | solution.py:161
  94.0 1.8 %copy-start.6 = (bf16[272,1536]{1,0:T(8,128)(2,1)S(1)}, bf16[272,1536]{1,0:T(8,128)(2,1)}, u32[]{:S(2)}) copy-start(bf16[272,1536]{1,0:T(8,128)(2,1)} %get-tuple-element.79.refs_0_.refs_4_) | copy-start | bytes 2506756
  94.2 19.6 %collective-permute-start.16 = (bf16[256,1536]{1,0:T(8,128)(2,1)S(1)}, bf16[256,1536]{1,0:T(8,128)(2,1)S(1)}, u32[]{:S(2)}, u32[]{:S(2)}) collective-permute-start(bf16[256,1536]{1,0:T(8,128)(2,1)S(1)} %add_convert_fusion.3), channel_id=1, source_target_pairs={{0,4},{1,5},{2,6},{3,7},{4,0},{5,1},{6,2},{7,3},{8,12},{9,13},{10,... | collective-permute-start | bytes 2359304 | tf_op jit(solution)/shard_map/ppermute | solution.py:161
  105.2 8.7 %collective-permute-start.14 = (bf16[256,1536]{1,0:T(8,128)(2,1)S(1)}, bf16[256,1536]{1,0:T(8,128)(2,1)S(1)}, u32[]{:S(2)}, u32[]{:S(2)}) collective-permute-start(bf16[256,1536]{1,0:T(8,128)(2,1)S(1)} %get-tuple-element.121), channel_id=1, source_target_pairs={{0,1},{1,0},{2,3},{3,2},{4,5},{5,4},{6,7},{7,6},{8,9},{9,8},{10,11... | collective-permute-start | bytes 2359304 | tf_op jit(solution)/shard_map/ppermute | solution.py:161
  105.3 8.6 %collective-permute-start.15 = (bf16[256,1536]{1,0:T(8,128)(2,1)S(1)}, bf16[256,1536]{1,0:T(8,128)(2,1)S(1)}, u32[]{:S(2)}, u32[]{:S(2)}) collective-permute-start(bf16[256,1536]{1,0:T(8,128)(2,1)S(1)} %get-tuple-element.122), channel_id=1, source_target_pairs={{0,1},{1,0},{2,3},{3,2},{4,5},{5,4},{6,7},{7,6},{8,9},{9,8},{10,11... | collective-permute-start | bytes 2359304 | tf_op jit(solution)/shard_map/ppermute | solution.py:161
  114.1 38.3 %copy-start.9 = (bf16[256,1536]{1,0:T(8,128)(2,1)S(1)}, bf16[256,1536]{1,0:T(8,128)(2,1)}, u32[]{:S(2)}) copy-start(bf16[256,1536]{1,0:T(8,128)(2,1)} %tokens.1) | copy-start | bytes 2359300
  114.1 35.2 %collective-permute-start.18 = (bf16[256,1536]{1,0:T(8,128)(2,1)S(1)}, bf16[256,1536]{1,0:T(8,128)(2,1)S(1)}, u32[]{:S(2)}, u32[]{:S(2)}) collective-permute-start(bf16[256,1536]{1,0:T(8,128)(2,1)S(1)} %add_convert_fusion.1), channel_id=1, source_target_pairs={{0,4},{1,5},{2,6},{3,7},{4,0},{5,1},{6,2},{7,3},{8,12},{9,13},{10,... | collective-permute-start | bytes 2359304 | tf_op jit(solution)/shard_map/ppermute | solution.py:161
  116.0 36.3 %collective-permute-start.17 = (bf16[256,1536]{1,0:T(8,128)(2,1)S(1)}, bf16[256,1536]{1,0:T(8,128)(2,1)S(1)}, u32[]{:S(2)}, u32[]{:S(2)}) collective-permute-start(bf16[256,1536]{1,0:T(8,128)(2,1)S(1)} %add_convert_fusion.2), channel_id=1, source_target_pairs={{0,8},{1,9},{2,10},{3,11},{4,12},{5,13},{6,14},{7,15},{8,0},{9,1},... | collective-permute-start | bytes 2359304 | tf_op jit(solution)/shard_map/ppermute | solution.py:161
  118.7 33.7 %collective-permute-start.19 = (bf16[256,1536]{1,0:T(8,128)(2,1)S(1)}, bf16[256,1536]{1,0:T(8,128)(2,1)S(1)}, u32[]{:S(2)}, u32[]{:S(2)}) collective-permute-start(bf16[256,1536]{1,0:T(8,128)(2,1)S(1)} %get-tuple-element.136), channel_id=1, source_target_pairs={{0,1},{1,0},{2,3},{3,2},{4,5},{5,4},{6,7},{7,6},{8,9},{9,8},{10,11... | collective-permute-start | bytes 2359304 | tf_op jit(solution)/shard_map/ppermute | solution.py:161

commit v6 on v5

--- a/solution.py
+++ b/solution.py
@@ -226,11 +226,11 @@
     s_b, s_a = together(s_b, s_a)
     s_c = send(s_b, outer)
     m_a, m_b = send(s_a, by_core), send(s_b, by_core)
-    x_1, y_0, x_0, y_1 = together(x_1, y_0, x_0, y_1)
+    m_a, m_b, x_0, y_1 = together(m_a, m_b, x_0, y_1)
     d_0 = send(x_0, by_y)
     d_1 = across(y_1)
+    x_1, y_0 = together(x_1, y_0)
     mine = (own[0], x_0, own[1], x_1)
-    m_a, m_b = together(m_a, m_b)
     u_0, v_0, u_a, v_a, u_b, v_b = run((s_0, m_0, s_a, m_a, s_b, m_b), [(0, mine, 0, 6)], [None] * 6)
     s_c, u_0, v_0, u_a, v_a, u_b, v_b = together(s_c, u_0, v_0, u_a, v_a, u_b, v_b)
     m_c = send(s_c, by_core)

time: 154 us -> 153 us (level)
  starting transfers between devices: 20.8 us -> 18.8 us
    ppermute x17, waiting for transfers between devices: 67.9 us -> 72.7 us  [send(): return lax.ppermute(v, 'tensor', pairs)]
    ppermute x3, waiting for transfers between devices: 24.4 us -> 20.2 us  [across(): return lax.ppermute(v, 'dp', [(0, 1), (1, 0)])]
  transfers between devices with their start and end apart: 20 -> 20, of which waited for: 13 -> 14; matrix products, arithmetic and copies ran while one was open for 1% -> 1% of each run, Pallas kernels for 17% -> 17%
where the time goes in v6:
time: 153 us; the launch traced here: 152 us
  waiting for transfers between devices  93 us (61%)
  Pallas kernels  32.8 us (21%)
  starting transfers between devices  18.8 us (12%)
  local copies, waits for them, and re-layouts  5 us (3%)
  other arithmetic  2.04 us (1%)
    ppermute x17, waiting for transfers between devices, send(): return lax.ppermute(v, 'tensor', pairs)  72.7 us
    pallas_call x4, Pallas kernels, run(): pl.pallas_call(functools.partial(expert_kernel, tuple(((e, first, last) f...  27.1 us
    ppermute x3, waiting for transfers between devices, across(): return lax.ppermute(v, 'dp', [(0, 1), (1, 0)])  20.2 us
    ppermute x17, starting transfers between devices, send(): return lax.ppermute(v, 'tensor', pairs)  14.9 us
    unnamed x22, local copies, waits for them, and re-layouts  4.4 us
    ppermute x3, starting transfers between devices, across(): return lax.ppermute(v, 'dp', [(0, 1), (1, 0)])  3.89 us
    pallas_call x1, Pallas kernels, lanes(): pl.pallas_call(pack_kernel, out_shape=(jax.ShapeDtypeStruct((half, half),...  3.1 us
  transfers between devices with their start and end apart: 20, of which 14 were waited for; matrix products, arithmetic and copies ran while one was open for 1% of the time, Pallas kernels for 17%

profile of v6, /device:TPU:0, one launch (start us, length us, event | category | flops | bytes accessed | tf_op | source)
XLA Modules:
  0.0 152.4 jit_solution(2449815162781704504)
XLA Ops:
  0.0 3.1 %pack.1 = (bf16[768,768]{1,0:T(8,128)(2,1)}, bf16[768,768]{1,0:T(8,128)(2,1)}) custom-call(bf16[768,512]{1,0:T(8,128)(2,1)} %bitcast.5, bf16[768,512]{1,0:T(8,128)(2,1)} %bitcast.6, bf16[512,768]{1,0:T(8,128)(2,1)} %bitcast.7), custom_call_target="tpu_custom_call" | custom-call | tf_op jit(solution)/shard_map/pack/pallas_call | solution.py:171
  3.1 3.0 %collective-permute-start.3 = (bf16[768,768]{1,0:T(8,128)(2,1)}, bf16[768,768]{1,0:T(8,128)(2,1)S(1)}, u32[]{:S(2)}, u32[]{:S(2)}) collective-permute-start(bf16[768,768]{1,0:T(8,128)(2,1)} %get-tuple-element.87.refs_6_.refs_2_), channel_id=1, source_target_pairs={{0,16},{16,0},{1,17},{17,1},{2,18},{18,2},{3,19},{19,3},{4,20},{20... | collective-permute-start | bytes 3538952 | tf_op jit(solution)/shard_map/ppermute | solution.py:164
  6.1 1.5 collective-permute-start.4
  7.6 0.6 reshape.3.gain
  8.9 2.6 %prologue.1 = (bf16[272,1536]{1,0:T(8,128)(2,1)}, f32[8,128]{1,0:T(8,128)}) custom-call(s32[1]{0:T(128)S(6)} %copy.9.lengths, bf16[256,1536]{1,0:T(8,128)(2,1)} %tokens.1, f32[1,1536]{1,0:T(1,128)} %reshape.3.gain, bf16[16,1536]{1,0:T(8,128)(2,1)} %bitcast.8, s32[8,256]{1,0:T(8,128)} %bitcast.9), custom_call_target="tpu_custom_call" | custom-call | tf_op jit(solution)/shard_map/prologue/pallas_call | solution.py:181
  11.5 1.6 %collective-permute-start.1 = (bf16[272,1536]{1,0:T(8,128)(2,1)}, bf16[272,1536]{1,0:T(8,128)(2,1)S(1)}, u32[]{:S(2)}, u32[]{:S(2)}) collective-permute-start(bf16[272,1536]{1,0:T(8,128)(2,1)} %get-tuple-element.72.refs_0_.refs_4_), channel_id=1, source_target_pairs={{0,4},{1,5},{2,6},{3,7},{4,0},{5,1},{6,2},{7,3},{8,12},{9,13},{10,... | collective-permute-start | bytes 2506760 | tf_op jit(solution)/shard_map/ppermute | solution.py:161
  13.0 0.0 collective-permute-start.2
  13.0 2.6 %collective-permute-start = (bf16[272,1536]{1,0:T(8,128)(2,1)}, bf16[272,1536]{1,0:T(8,128)(2,1)S(1)}, u32[]{:S(2)}, u32[]{:S(2)}) collective-permute-start(bf16[272,1536]{1,0:T(8,128)(2,1)} %get-tuple-element.72.refs_0_.refs_4_), channel_id=1, source_target_pairs={{0,8},{1,9},{2,10},{3,11},{4,12},{5,13},{6,14},{7,15},{8,0},{9,1},... | collective-permute-start | bytes 2506760 | tf_op jit(solution)/shard_map/ppermute | solution.py:161
  15.6 16.7 %collective-permute-done.3.refs_7_.refs_3_ = bf16[768,768]{1,0:T(8,128)(2,1)S(1)} collective-permute-done((bf16[768,768]{1,0:T(8,128)(2,1)}, bf16[768,768]{1,0:T(8,128)(2,1)S(1)}, u32[]{:S(2)}, u32[]{:S(2)}) %collective-permute-start.3) | collective-permute-done | bytes 1179680 | tf_op jit(solution)/shard_map/ppermute | solution.py:164
  32.3 1.5 collective-permute-done.4.refs_6_.refs_14_
  33.8 0.4 collective-permute-start.10
  34.1 1.7 %collective-permute-start.11 = (bf16[768,768]{1,0:T(8,128)(2,1)}, bf16[768,768]{1,0:T(8,128)(2,1)S(1)}, u32[]{:S(2)}, u32[]{:S(2)}) collective-permute-start(bf16[768,768]{1,0:T(8,128)(2,1)} %get-tuple-element.87.refs_6_.refs_2_), channel_id=1, source_target_pairs={{0,2},{1,3},{2,0},{3,1},{4,6},{5,7},{6,4},{7,5},{8,10},{9,11},{10,... | collective-permute-start | bytes 3538952 | tf_op jit(solution)/shard_map/ppermute | solution.py:161
  35.8 11.9 %collective-permute-done.1.refs_2_ = bf16[272,1536]{1,0:T(8,128)(2,1)S(1)} collective-permute-done((bf16[272,1536]{1,0:T(8,128)(2,1)}, bf16[272,1536]{1,0:T(8,128)(2,1)S(1)}, u32[]{:S(2)}, u32[]{:S(2)}) %collective-permute-start.1) | collective-permute-done | bytes 835616 | tf_op jit(solution)/shard_map/ppermute | solution.py:161
  47.7 5.4 %collective-permute-done.refs_4_.refs_0_ = bf16[272,1536]{1,0:T(8,128)(2,1)S(1)} collective-permute-done((bf16[272,1536]{1,0:T(8,128)(2,1)}, bf16[272,1536]{1,0:T(8,128)(2,1)S(1)}, u32[]{:S(2)}, u32[]{:S(2)}) %collective-permute-start) | collective-permute-done | bytes 835616 | tf_op jit(solution)/shard_map/ppermute | solution.py:161
  53.1 0.0 collective-permute-start.6
  53.1 0.5 collective-permute-start.5
  53.6 1.8 %collective-permute-done.6.refs_5_.refs_1_ = bf16[272,1536]{1,0:T(8,128)(2,1)S(1)} collective-permute-done((bf16[272,1536]{1,0:T(8,128)(2,1)S(1)}, bf16[272,1536]{1,0:T(8,128)(2,1)S(1)}, u32[]{:S(2)}, u32[]{:S(2)}) %collective-permute-start.6) | collective-permute-done | bytes 835616 | tf_op jit(solution)/shard_map/ppermute | solution.py:161
  55.5 1.2 collective-permute-done.5.refs_3_
  56.7 0.5 collective-permute-start.7
  57.2 0.5 collective-permute-start.8
  57.7 3.6 %collective-permute-done.10.refs_9_.refs_5_ = bf16[768,768]{1,0:T(8,128)(2,1)S(1)} collective-permute-done((bf16[768,768]{1,0:T(8,128)(2,1)}, bf16[768,768]{1,0:T(8,128)(2,1)S(1)}, u32[]{:S(2)}, u32[]{:S(2)}) %collective-permute-start.10) | collective-permute-done | bytes 1179680 | tf_op jit(solution)/shard_map/ppermute | solution.py:164
  61.3 1.0 collective-permute-done.11.refs_4_.refs_12_
  62.3 1.3 copy-done
  63.6 1.3 copy-done.2
  64.8 1.1 copy-done.5
  66.0 0.7 copy-done.7
  66.7 9.5 %experts.4 = (bf16[256,1536]{1,0:T(8,128)(2,1)S(1)}, bf16[256,1536]{1,0:T(8,128)(2,1)S(1)}, bf16[256,1536]{1,0:T(8,128)(2,1)S(1)}, bf16[256,1536]{1,0:T(8,128)(2...) custom-call(f32[8,128]{1,0:T(8,128)S(1)} %copy-done.7, bf16[272,1536]{1,0:T(8,128)(2,1)S(1)} %copy-done.5, ...), custom_call_target="tpu_custom_call" | custom-call | flops 1 | bytes 1 | tf_op jit(solution)/shard_map/experts/pallas_call | solution.py:199
  76.2 0.1 collective-permute-start.12
  76.3 2.3 %collective-permute-done.12.refs_1_ = bf16[272,1536]{1,0:T(8,128)(2,1)S(1)} collective-permute-done((bf16[272,1536]{1,0:T(8,128)(2,1)S(1)}, bf16[272,1536]{1,0:T(8,128)(2,1)S(1)}, u32[]{:S(2)}, u32[]{:S(2)}) %collective-permute-start.12) | collective-permute-done | bytes 835616 | tf_op jit(solution)/shard_map/ppermute | solution.py:161
  78.6 4.0 %experts.5 = (bf16[256,1536]{1,0:T(8,128)(2,1)S(1)}, bf16[256,1536]{1,0:T(8,128)(2,1)S(1)}) custom-call(f32[8,128]{1,0:T(8,128)S(1)} %copy-done.8, bf16[272,1536]{1,0:T(8,128)(2,1)S(1)} %collective-permute-done.9.refs_0_, bf16[272,1536]{1,0:T(8,128)(2,1)S(1)} %collective-permute-done.12.refs_1_, bf16[768,768]{1,0:T(8,128)(2,1)S(1)} %copy-done.1, ...), custom_call_target="tpu_custom_call" | custom-call | flops 1 | bytes 1 | tf_op jit(solution)/shard_map/experts/pallas_call | solution.py:199
  82.7 3.5 %collective-permute-done.7.refs_5_.refs_13_ = bf16[768,768]{1,0:T(8,128)(2,1)S(1)} collective-permute-done((bf16[768,768]{1,0:T(8,128)(2,1)S(1)}, bf16[768,768]{1,0:T(8,128)(2,1)S(1)}, u32[]{:S(2)}, u32[]{:S(2)}) %collective-permute-start.7) | collective-permute-done | bytes 1179680 | tf_op jit(solution)/shard_map/ppermute | solution.py:161
  86.2 4.2 %experts.6 = (bf16[256,1536]{1,0:T(8,128)(2,1)S(1)}, bf16[256,1536]{1,0:T(8,128)(2,1)S(1)}) custom-call(f32[8,128]{1,0:T(8,128)S(1)} %copy-done.8, bf16[272,1536]{1,0:T(8,128)(2,1)S(1)} %collective-permute-done.9.refs_0_, bf16[272,1536]{1,0:T(8,128)(2,1)S(1)} %collective-permute-done.12.refs_1_, bf16[256,1536]{1,0:T(8,128)(2,1)S(1)} %get-tuple-element.107.refs_2_, ...), custom_call_target="tpu_custom_call" | custom-call | flops 1 | bytes 1 | tf_op jit(solution)/shard_map/experts/pallas_call | solution.py:199
  90.4 0.1 collective-permute-start.13
  90.5 2.3 %collective-permute-done.13 = bf16[256,1536]{1,0:T(8,128)(2,1)S(1)} collective-permute-done((bf16[256,1536]{1,0:T(8,128)(2,1)S(1)}, bf16[256,1536]{1,0:T(8,128)(2,1)S(1)}, u32[]{:S(2)}, u32[]{:S(2)}) %collective-permute-start.13) | collective-permute-done | bytes 786464 | tf_op jit(solution)/shard_map/ppermute | solution.py:161
  92.8 0.2 add_convert_fusion.3
  93.0 1.6 %collective-permute-start.16 = (bf16[256,1536]{1,0:T(8,128)(2,1)S(1)}, bf16[256,1536]{1,0:T(8,128)(2,1)S(1)}, u32[]{:S(2)}, u32[]{:S(2)}) collective-permute-start(bf16[256,1536]{1,0:T(8,128)(2,1)S(1)} %add_convert_fusion.3), channel_id=1, source_target_pairs={{0,4},{1,5},{2,6},{3,7},{4,0},{5,1},{6,2},{7,3},{8,12},{9,13},{10,... | collective-permute-start | bytes 2359304 | tf_op jit(solution)/shard_map/ppermute | solution.py:161
  94.5 9.3 %experts.7 = (bf16[256,1536]{1,0:T(8,128)(2,1)S(1)}, bf16[256,1536]{1,0:T(8,128)(2,1)S(1)}, bf16[256,1536]{1,0:T(8,128)(2,1)S(1)}, bf16[256,1536]{1,0:T(8,128)(2...) custom-call(f32[8,128]{1,0:T(8,128)S(1)} %copy-done.8, ...), custom_call_target="tpu_custom_call" | custom-call | flops 1 | bytes 1 | tf_op jit(solution)/shard_map/experts/pallas_call | solution.py:199
  103.9 0.1 collective-permute-start.14
  104.0 0.5 collective-permute-start.15
  104.5 8.1 %collective-permute-done.16 = bf16[256,1536]{1,0:T(8,128)(2,1)S(1)} collective-permute-done((bf16[256,1536]{1,0:T(8,128)(2,1)S(1)}, bf16[256,1536]{1,0:T(8,128)(2,1)S(1)}, u32[]{:S(2)}, u32[]{:S(2)}) %collective-permute-start.16) | collective-permute-done | bytes 786464 | tf_op jit(solution)/shard_map/ppermute | solution.py:161
  112.6 0.2 add_convert_fusion.1
  112.8 0.0 copy-start.9
  112.8 1.6 %collective-permute-start.18 = (bf16[256,1536]{1,0:T(8,128)(2,1)S(1)}, bf16[256,1536]{1,0:T(8,128)(2,1)S(1)}, u32[]{:S(2)}, u32[]{:S(2)}) collective-permute-start(bf16[256,1536]{1,0:T(8,128)(2,1)S(1)} %add_convert_fusion.1), channel_id=1, source_target_pairs={{0,4},{1,5},{2,6},{3,7},{4,0},{5,1},{6,2},{7,3},{8,12},{9,13},{10,... | collective-permute-start | bytes 2359304 | tf_op jit(solution)/shard_map/ppermute | solution.py:161
  114.4 0.3 add_convert_fusion.2
  114.7 2.6 %collective-permute-start.17 = (bf16[256,1536]{1,0:T(8,128)(2,1)S(1)}, bf16[256,1536]{1,0:T(8,128)(2,1)S(1)}, u32[]{:S(2)}, u32[]{:S(2)}) collective-permute-start(bf16[256,1536]{1,0:T(8,128)(2,1)S(1)} %add_convert_fusion.2), channel_id=1, source_target_pairs={{0,8},{1,9},{2,10},{3,11},{4,12},{5,13},{6,14},{7,15},{8,0},{9,1},... | collective-permute-start | bytes 2359304 | tf_op jit(solution)/shard_map/ppermute | solution.py:161
  117.3 30.7 %collective-permute-done.18 = bf16[256,1536]{1,0:T(8,128)(2,1)S(1)} collective-permute-done((bf16[256,1536]{1,0:T(8,128)(2,1)S(1)}, bf16[256,1536]{1,0:T(8,128)(2,1)S(1)}, u32[]{:S(2)}, u32[]{:S(2)}) %collective-permute-start.18) | collective-permute-done | bytes 786464 | tf_op jit(solution)/shard_map/ppermute | solution.py:161
  148.0 3.0 %collective-permute-done.17 = bf16[256,1536]{1,0:T(8,128)(2,1)S(1)} collective-permute-done((bf16[256,1536]{1,0:T(8,128)(2,1)S(1)}, bf16[256,1536]{1,0:T(8,128)(2,1)S(1)}, u32[]{:S(2)}, u32[]{:S(2)}) %collective-permute-start.17) | collective-permute-done | bytes 786464 | tf_op jit(solution)/shard_map/ppermute | solution.py:161
  151.0 1.4 add_convert_fusion
  (25 shorter events, 0.1 us)
Async XLA Ops:
  0.0 7.6 %copy-start.10 = (f32[1536]{0:T(1024)S(1)}, f32[1536]{0:T(1024)}, u32[]{:S(2)}) copy-start(f32[1536]{0:T(1024)} %param.11) | copy-start | bytes 18436
  3.1 29.2 %collective-permute-start.3 = (bf16[768,768]{1,0:T(8,128)(2,1)}, bf16[768,768]{1,0:T(8,128)(2,1)S(1)}, u32[]{:S(2)}, u32[]{:S(2)}) collective-permute-start(bf16[768,768]{1,0:T(8,128)(2,1)} %get-tuple-element.87.refs_6_.refs_2_), channel_id=1, source_target_pairs={{0,16},{16,0},{1,17},{17,1},{2,18},{18,2},{3,19},{19,3},{4,20},{20... | collective-permute-start | bytes 3538952 | tf_op jit(solution)/shard_map/ppermute | solution.py:164
  6.1 27.6 %collective-permute-start.4 = (bf16[768,768]{1,0:T(8,128)(2,1)}, bf16[768,768]{1,0:T(8,128)(2,1)S(1)}, u32[]{:S(2)}, u32[]{:S(2)}) collective-permute-start(bf16[768,768]{1,0:T(8,128)(2,1)} %get-tuple-element.86.refs_8_.refs_4_), channel_id=1, source_target_pairs={{0,2},{1,3},{2,0},{3,1},{4,6},{5,7},{6,4},{7,5},{8,10},{9,11},{10,... | collective-permute-start | bytes 3538952 | tf_op jit(solution)/shard_map/ppermute | solution.py:161
  11.5 36.3 %collective-permute-start.1 = (bf16[272,1536]{1,0:T(8,128)(2,1)}, bf16[272,1536]{1,0:T(8,128)(2,1)S(1)}, u32[]{:S(2)}, u32[]{:S(2)}) collective-permute-start(bf16[272,1536]{1,0:T(8,128)(2,1)} %get-tuple-element.72.refs_0_.refs_4_), channel_id=1, source_target_pairs={{0,4},{1,5},{2,6},{3,7},{4,0},{5,1},{6,2},{7,3},{8,12},{9,13},{10,... | collective-permute-start | bytes 2506760 | tf_op jit(solution)/shard_map/ppermute | solution.py:161
  13.0 34.7 %collective-permute-start.2 = (bf16[272,1536]{1,0:T(8,128)(2,1)}, bf16[272,1536]{1,0:T(8,128)(2,1)S(1)}, u32[]{:S(2)}, u32[]{:S(2)}) collective-permute-start(bf16[272,1536]{1,0:T(8,128)(2,1)} %get-tuple-element.72.refs_0_.refs_4_), channel_id=1, source_target_pairs={{0,1},{1,0},{2,3},{3,2},{4,5},{5,4},{6,7},{7,6},{8,9},{9,8},{10,11... | collective-permute-start | bytes 2506760 | tf_op jit(solution)/shard_map/ppermute | solution.py:161
  13.0 40.1 %collective-permute-start = (bf16[272,1536]{1,0:T(8,128)(2,1)}, bf16[272,1536]{1,0:T(8,128)(2,1)S(1)}, u32[]{:S(2)}, u32[]{:S(2)}) collective-permute-start(bf16[272,1536]{1,0:T(8,128)(2,1)} %get-tuple-element.72.refs_0_.refs_4_), channel_id=1, source_target_pairs={{0,8},{1,9},{2,10},{3,11},{4,12},{5,13},{6,14},{7,15},{8,0},{9,1},... | collective-permute-start | bytes 2506760 | tf_op jit(solution)/shard_map/ppermute | solution.py:161
  33.8 27.5 %collective-permute-start.10 = (bf16[768,768]{1,0:T(8,128)(2,1)}, bf16[768,768]{1,0:T(8,128)(2,1)S(1)}, u32[]{:S(2)}, u32[]{:S(2)}) collective-permute-start(bf16[768,768]{1,0:T(8,128)(2,1)} %get-tuple-element.86.refs_8_.refs_4_), channel_id=1, source_target_pairs={{0,16},{16,0},{1,17},{17,1},{2,18},{18,2},{3,19},{19,3},{4,20},{20... | collective-permute-start | bytes 3538952 | tf_op jit(solution)/shard_map/ppermute | solution.py:164
  34.1 28.2 %collective-permute-start.11 = (bf16[768,768]{1,0:T(8,128)(2,1)}, bf16[768,768]{1,0:T(8,128)(2,1)S(1)}, u32[]{:S(2)}, u32[]{:S(2)}) collective-permute-start(bf16[768,768]{1,0:T(8,128)(2,1)} %get-tuple-element.87.refs_6_.refs_2_), channel_id=1, source_target_pairs={{0,2},{1,3},{2,0},{3,1},{4,6},{5,7},{6,4},{7,5},{8,10},{9,11},{10,... | collective-permute-start | bytes 3538952 | tf_op jit(solution)/shard_map/ppermute | solution.py:161
  53.1 2.4 %collective-permute-start.6 = (bf16[272,1536]{1,0:T(8,128)(2,1)S(1)}, bf16[272,1536]{1,0:T(8,128)(2,1)S(1)}, u32[]{:S(2)}, u32[]{:S(2)}) collective-permute-start(bf16[272,1536]{1,0:T(8,128)(2,1)S(1)} %collective-permute-done.refs_4_.refs_0_), channel_id=1, source_target_pairs={{0,1},{1,0},{2,3},{3,2},{4,5},{5,4},{6,7},{7,6},{8,9},{9,8},{10,11... | collective-permute-start | bytes 2506760 | tf_op jit(solution)/shard_map/ppermute | solution.py:161
  53.1 3.5 %collective-permute-start.5 = (bf16[272,1536]{1,0:T(8,128)(2,1)S(1)}, bf16[272,1536]{1,0:T(8,128)(2,1)S(1)}, u32[]{:S(2)}, u32[]{:S(2)}) collective-permute-start(bf16[272,1536]{1,0:T(8,128)(2,1)S(1)} %collective-permute-done.1.refs_2_), channel_id=1, source_target_pairs={{0,1},{1,0},{2,3},{3,2},{4,5},{5,4},{6,7},{7,6},{8,9},{9,8},{10,11... | collective-permute-start | bytes 2506760 | tf_op jit(solution)/shard_map/ppermute | solution.py:161
  53.6 22.6 %collective-permute-start.9 = (bf16[272,1536]{1,0:T(8,128)(2,1)S(1)}, bf16[272,1536]{1,0:T(8,128)(2,1)S(1)}, u32[]{:S(2)}, u32[]{:S(2)}) collective-permute-start(bf16[272,1536]{1,0:T(8,128)(2,1)S(1)} %collective-permute-done.refs_4_.refs_0_), channel_id=1, source_target_pairs={{0,4},{1,5},{2,6},{3,7},{4,0},{5,1},{6,2},{7,3},{8,12},{9,13},{10,... | collective-permute-start | bytes 2506760 | tf_op jit(solution)/shard_map/ppermute | solution.py:161
  56.7 29.5 %collective-permute-start.7 = (bf16[768,768]{1,0:T(8,128)(2,1)S(1)}, bf16[768,768]{1,0:T(8,128)(2,1)S(1)}, u32[]{:S(2)}, u32[]{:S(2)}) collective-permute-start(bf16[768,768]{1,0:T(8,128)(2,1)S(1)} %collective-permute-done.3.refs_7_.refs_3_), channel_id=1, source_target_pairs={{0,2},{1,3},{2,0},{3,1},{4,6},{5,7},{6,4},{7,5},{8,10},{9,11},{10,... | collective-permute-start | bytes 3538952 | tf_op jit(solution)/shard_map/ppermute | solution.py:161
  57.2 29.0 %collective-permute-start.8 = (bf16[768,768]{1,0:T(8,128)(2,1)S(1)}, bf16[768,768]{1,0:T(8,128)(2,1)S(1)}, u32[]{:S(2)}, u32[]{:S(2)}) collective-permute-start(bf16[768,768]{1,0:T(8,128)(2,1)S(1)} %collective-permute-done.4.refs_6_.refs_14_), channel_id=1, source_target_pairs={{0,16},{16,0},{1,17},{17,1},{2,18},{18,2},{3,19},{19,3},{4,20},{20... | collective-permute-start | bytes 3538952 | tf_op jit(solution)/shard_map/ppermute | solution.py:164
  62.3 1.3 copy-start
  63.6 1.3 copy-start.2
  64.8 1.1 copy-start.5
  66.0 0.7 copy-start.7
  66.7 12.0 %copy-start.1 = (bf16[768,768]{1,0:T(8,128)(2,1)S(1)}, bf16[768,768]{1,0:T(8,128)(2,1)}, u32[]{:S(2)}) copy-start(bf16[768,768]{1,0:T(8,128)(2,1)} %get-tuple-element.87.refs_6_.refs_2_) | copy-start | bytes 3538948
  66.7 12.0 %copy-start.3 = (bf16[768,768]{1,0:T(8,128)(2,1)S(1)}, bf16[768,768]{1,0:T(8,128)(2,1)}, u32[]{:S(2)}) copy-start(bf16[768,768]{1,0:T(8,128)(2,1)} %get-tuple-element.86.refs_8_.refs_4_) | copy-start | bytes 3538948
  66.7 12.0 %copy-start.8 = (f32[8,128]{1,0:T(8,128)S(1)}, f32[8,128]{1,0:T(8,128)}, u32[]{:S(2)}) copy-start(f32[8,128]{1,0:T(8,128)} %get-tuple-element.114._) | copy-start | bytes 12292
  76.2 2.4 %collective-permute-start.12 = (bf16[272,1536]{1,0:T(8,128)(2,1)S(1)}, bf16[272,1536]{1,0:T(8,128)(2,1)S(1)}, u32[]{:S(2)}, u32[]{:S(2)}) collective-permute-start(bf16[272,1536]{1,0:T(8,128)(2,1)S(1)} %collective-permute-done.9.refs_0_), channel_id=1, source_target_pairs={{0,1},{1,0},{2,3},{3,2},{4,5},{5,4},{6,7},{7,6},{8,9},{9,8},{10,11... | collective-permute-start | bytes 2506760 | tf_op jit(solution)/shard_map/ppermute | solution.py:161
  86.2 4.2 %copy-start.4 = (bf16[768,768]{1,0:T(8,128)(2,1)}, bf16[768,768]{1,0:T(8,128)(2,1)S(1)}, u32[]{:S(2)}) copy-start(bf16[768,768]{1,0:T(8,128)(2,1)S(1)} %collective-permute-done.8.refs_7_.refs_15_) | copy-start | bytes 3538948
  90.4 2.4 %collective-permute-start.13 = (bf16[256,1536]{1,0:T(8,128)(2,1)S(1)}, bf16[256,1536]{1,0:T(8,128)(2,1)S(1)}, u32[]{:S(2)}, u32[]{:S(2)}) collective-permute-start(bf16[256,1536]{1,0:T(8,128)(2,1)S(1)} %get-tuple-element.112), channel_id=1, source_target_pairs={{0,1},{1,0},{2,3},{3,2},{4,5},{5,4},{6,7},{7,6},{8,9},{9,8},{10,11... | collective-permute-start | bytes 2359304 | tf_op jit(solution)/shard_map/ppermute | solution.py:161
  92.8 1.8 %copy-start.6 = (bf16[272,1536]{1,0:T(8,128)(2,1)S(1)}, bf16[272,1536]{1,0:T(8,128)(2,1)}, u32[]{:S(2)}) copy-start(bf16[272,1536]{1,0:T(8,128)(2,1)} %get-tuple-element.72.refs_0_.refs_4_) | copy-start | bytes 2506756
  93.0 19.6 %collective-permute-start.16 = (bf16[256,1536]{1,0:T(8,128)(2,1)S(1)}, bf16[256,1536]{1,0:T(8,128)(2,1)S(1)}, u32[]{:S(2)}, u32[]{:S(2)}) collective-permute-start(bf16[256,1536]{1,0:T(8,128)(2,1)S(1)} %add_convert_fusion.3), channel_id=1, source_target_pairs={{0,4},{1,5},{2,6},{3,7},{4,0},{5,1},{6,2},{7,3},{8,12},{9,13},{10,... | collective-permute-start | bytes 2359304 | tf_op jit(solution)/shard_map/ppermute | solution.py:161
  103.9 8.7 %collective-permute-start.14 = (bf16[256,1536]{1,0:T(8,128)(2,1)S(1)}, bf16[256,1536]{1,0:T(8,128)(2,1)S(1)}, u32[]{:S(2)}, u32[]{:S(2)}) collective-permute-start(bf16[256,1536]{1,0:T(8,128)(2,1)S(1)} %get-tuple-element.121), channel_id=1, source_target_pairs={{0,1},{1,0},{2,3},{3,2},{4,5},{5,4},{6,7},{7,6},{8,9},{9,8},{10,11... | collective-permute-start | bytes 2359304 | tf_op jit(solution)/shard_map/ppermute | solution.py:161
  104.0 8.6 %collective-permute-start.15 = (bf16[256,1536]{1,0:T(8,128)(2,1)S(1)}, bf16[256,1536]{1,0:T(8,128)(2,1)S(1)}, u32[]{:S(2)}, u32[]{:S(2)}) collective-permute-start(bf16[256,1536]{1,0:T(8,128)(2,1)S(1)} %get-tuple-element.122), channel_id=1, source_target_pairs={{0,1},{1,0},{2,3},{3,2},{4,5},{5,4},{6,7},{7,6},{8,9},{9,8},{10,11... | collective-permute-start | bytes 2359304 | tf_op jit(solution)/shard_map/ppermute | solution.py:161
  112.8 38.2 %copy-start.9 = (bf16[256,1536]{1,0:T(8,128)(2,1)S(1)}, bf16[256,1536]{1,0:T(8,128)(2,1)}, u32[]{:S(2)}) copy-start(bf16[256,1536]{1,0:T(8,128)(2,1)} %tokens.1) | copy-start | bytes 2359300
  112.8 35.2 %collective-permute-start.18 = (bf16[256,1536]{1,0:T(8,128)(2,1)S(1)}, bf16[256,1536]{1,0:T(8,128)(2,1)S(1)}, u32[]{:S(2)}, u32[]{:S(2)}) collective-permute-start(bf16[256,1536]{1,0:T(8,128)(2,1)S(1)} %add_convert_fusion.1), channel_id=1, source_target_pairs={{0,4},{1,5},{2,6},{3,7},{4,0},{5,1},{6,2},{7,3},{8,12},{9,13},{10,... | collective-permute-start | bytes 2359304 | tf_op jit(solution)/shard_map/ppermute | solution.py:161
  114.7 36.3 %collective-permute-start.17 = (bf16[256,1536]{1,0:T(8,128)(2,1)S(1)}, bf16[256,1536]{1,0:T(8,128)(2,1)S(1)}, u32[]{:S(2)}, u32[]{:S(2)}) collective-permute-start(bf16[256,1536]{1,0:T(8,128)(2,1)S(1)} %add_convert_fusion.2), channel_id=1, source_target_pairs={{0,8},{1,9},{2,10},{3,11},{4,12},{5,13},{6,14},{7,15},{8,0},{9,1},... | collective-permute-start | bytes 2359304 | tf_op jit(solution)/shard_map/ppermute | solution.py:161
  117.3 33.7 %collective-permute-start.19 = (bf16[256,1536]{1,0:T(8,128)(2,1)S(1)}, bf16[256,1536]{1,0:T(8,128)(2,1)S(1)}, u32[]{:S(2)}, u32[]{:S(2)}) collective-permute-start(bf16[256,1536]{1,0:T(8,128)(2,1)S(1)} %get-tuple-element.136), channel_id=1, source_target_pairs={{0,1},{1,0},{2,3},{3,2},{4,5},{5,4},{6,7},{7,6},{8,9},{9,8},{10,11... | collective-permute-start | bytes 2359304 | tf_op jit(solution)/shard_map/ppermute | solution.py:161

commit v7 on v6

--- a/solution.py
+++ b/solution.py
@@ -250,8 +250,8 @@
     r_o = send(add(p_a, r_a), outer)
     r_m = send(add(p_b, r_b, r_n), skip)
     order[0] = p_0
+    (r_m,) = together(r_m)
     (r_o,) = together(r_o)
-    (r_m,) = together(r_m)
     return add(tokens, order[0], r_0, r_o, r_m)
 
 

time: 153 us -> 152 us (level)
  no operation moved by 1% of the time
where the time goes in v7:
time: 152 us; the launch traced here: 151 us
  waiting for transfers between devices  92 us (61%)
  Pallas kernels  32.8 us (22%)
  starting transfers between devices  18.8 us (12%)
  local copies, waits for them, and re-layouts  5 us (3%)
  other arithmetic  2.04 us (1%)
    ppermute x17, waiting for transfers between devices, send(): return lax.ppermute(v, 'tensor', pairs)  71.8 us
    pallas_call x4, Pallas kernels, run(): pl.pallas_call(functools.partial(expert_kernel, tuple(((e, first, last) f...  27.1 us
    ppermute x3, waiting for transfers between devices, across(): return lax.ppermute(v, 'dp', [(0, 1), (1, 0)])  20.2 us
    ppermute x17, starting transfers between devices, send(): return lax.ppermute(v, 'tensor', pairs)  14.9 us
    unnamed x22, local copies, waits for them, and re-layouts  4.4 us
    ppermute x3, starting transfers between devices, across(): return lax.ppermute(v, 'dp', [(0, 1), (1, 0)])  3.89 us
    pallas_call x1, Pallas kernels, lanes(): pl.pallas_call(pack_kernel, out_shape=(jax.ShapeDtypeStruct((half, half),...  3.1 us
  transfers between devices with their start and end apart: 20, of which 14 were waited for; matrix products, arithmetic and copies ran while one was open for 1% of the time, Pallas kernels for 17%

profile of v7, /device:TPU:0, one launch (start us, length us, event | category | flops | bytes accessed | tf_op | source)
XLA Modules:
  0.0 151.4 jit_solution(14166019294176217593)
XLA Ops:
  0.0 3.1 %pack.1 = (bf16[768,768]{1,0:T(8,128)(2,1)}, bf16[768,768]{1,0:T(8,128)(2,1)}) custom-call(bf16[768,512]{1,0:T(8,128)(2,1)} %bitcast.5, bf16[768,512]{1,0:T(8,128)(2,1)} %bitcast.6, bf16[512,768]{1,0:T(8,128)(2,1)} %bitcast.7), custom_call_target="tpu_custom_call" | custom-call | tf_op jit(solution)/shard_map/pack/pallas_call | solution.py:171
  3.1 3.0 %collective-permute-start.3 = (bf16[768,768]{1,0:T(8,128)(2,1)}, bf16[768,768]{1,0:T(8,128)(2,1)S(1)}, u32[]{:S(2)}, u32[]{:S(2)}) collective-permute-start(bf16[768,768]{1,0:T(8,128)(2,1)} %get-tuple-element.87.refs_6_.refs_2_), channel_id=1, source_target_pairs={{0,16},{16,0},{1,17},{17,1},{2,18},{18,2},{3,19},{19,3},{4,20},{20... | collective-permute-start | bytes 3538952 | tf_op jit(solution)/shard_map/ppermute | solution.py:164
  6.1 1.5 %collective-permute-start.4 = (bf16[768,768]{1,0:T(8,128)(2,1)}, bf16[768,768]{1,0:T(8,128)(2,1)S(1)}, u32[]{:S(2)}, u32[]{:S(2)}) collective-permute-start(bf16[768,768]{1,0:T(8,128)(2,1)} %get-tuple-element.86.refs_8_.refs_4_), channel_id=1, source_target_pairs={{0,2},{1,3},{2,0},{3,1},{4,6},{5,7},{6,4},{7,5},{8,10},{9,11},{10,... | collective-permute-start | bytes 3538952 | tf_op jit(solution)/shard_map/ppermute | solution.py:161
  7.6 0.6 reshape.3.gain
  8.9 2.6 %prologue.1 = (bf16[272,1536]{1,0:T(8,128)(2,1)}, f32[8,128]{1,0:T(8,128)}) custom-call(s32[1]{0:T(128)S(6)} %copy.9.lengths, bf16[256,1536]{1,0:T(8,128)(2,1)} %tokens.1, f32[1,1536]{1,0:T(1,128)} %reshape.3.gain, bf16[16,1536]{1,0:T(8,128)(2,1)} %bitcast.8, s32[8,256]{1,0:T(8,128)} %bitcast.9), custom_call_target="tpu_custom_call" | custom-call | tf_op jit(solution)/shard_map/prologue/pallas_call | solution.py:181
  11.5 1.6 %collective-permute-start.1 = (bf16[272,1536]{1,0:T(8,128)(2,1)}, bf16[272,1536]{1,0:T(8,128)(2,1)S(1)}, u32[]{:S(2)}, u32[]{:S(2)}) collective-permute-start(bf16[272,1536]{1,0:T(8,128)(2,1)} %get-tuple-element.72.refs_0_.refs_4_), channel_id=1, source_target_pairs={{0,4},{1,5},{2,6},{3,7},{4,0},{5,1},{6,2},{7,3},{8,12},{9,13},{10,... | collective-permute-start | bytes 2506760 | tf_op jit(solution)/shard_map/ppermute | solution.py:161
  13.0 0.0 collective-permute-start.2
  13.0 2.6 %collective-permute-start = (bf16[272,1536]{1,0:T(8,128)(2,1)}, bf16[272,1536]{1,0:T(8,128)(2,1)S(1)}, u32[]{:S(2)}, u32[]{:S(2)}) collective-permute-start(bf16[272,1536]{1,0:T(8,128)(2,1)} %get-tuple-element.72.refs_0_.refs_4_), channel_id=1, source_target_pairs={{0,8},{1,9},{2,10},{3,11},{4,12},{5,13},{6,14},{7,15},{8,0},{9,1},... | collective-permute-start | bytes 2506760 | tf_op jit(solution)/shard_map/ppermute | solution.py:161
  15.6 16.7 %collective-permute-done.3.refs_7_.refs_3_ = bf16[768,768]{1,0:T(8,128)(2,1)S(1)} collective-permute-done((bf16[768,768]{1,0:T(8,128)(2,1)}, bf16[768,768]{1,0:T(8,128)(2,1)S(1)}, u32[]{:S(2)}, u32[]{:S(2)}) %collective-permute-start.3) | collective-permute-done | bytes 1179680 | tf_op jit(solution)/shard_map/ppermute | solution.py:164
  32.3 1.5 collective-permute-done.4.refs_6_.refs_14_
  33.8 0.4 collective-permute-start.10
  34.1 1.7 %collective-permute-start.11 = (bf16[768,768]{1,0:T(8,128)(2,1)}, bf16[768,768]{1,0:T(8,128)(2,1)S(1)}, u32[]{:S(2)}, u32[]{:S(2)}) collective-permute-start(bf16[768,768]{1,0:T(8,128)(2,1)} %get-tuple-element.87.refs_6_.refs_2_), channel_id=1, source_target_pairs={{0,2},{1,3},{2,0},{3,1},{4,6},{5,7},{6,4},{7,5},{8,10},{9,11},{10,... | collective-permute-start | bytes 3538952 | tf_op jit(solution)/shard_map/ppermute | solution.py:161
  35.8 11.9 %collective-permute-done.1.refs_2_ = bf16[272,1536]{1,0:T(8,128)(2,1)S(1)} collective-permute-done((bf16[272,1536]{1,0:T(8,128)(2,1)}, bf16[272,1536]{1,0:T(8,128)(2,1)S(1)}, u32[]{:S(2)}, u32[]{:S(2)}) %collective-permute-start.1) | collective-permute-done | bytes 835616 | tf_op jit(solution)/shard_map/ppermute | solution.py:161
  47.7 5.4 %collective-permute-done.refs_4_.refs_0_ = bf16[272,1536]{1,0:T(8,128)(2,1)S(1)} collective-permute-done((bf16[272,1536]{1,0:T(8,128)(2,1)}, bf16[272,1536]{1,0:T(8,128)(2,1)S(1)}, u32[]{:S(2)}, u32[]{:S(2)}) %collective-permute-start) | collective-permute-done | bytes 835616 | tf_op jit(solution)/shard_map/ppermute | solution.py:161
  53.1 0.0 collective-permute-start.6
  53.1 0.5 collective-permute-start.5
  53.6 1.8 %collective-permute-done.6.refs_5_.refs_1_ = bf16[272,1536]{1,0:T(8,128)(2,1)S(1)} collective-permute-done((bf16[272,1536]{1,0:T(8,128)(2,1)S(1)}, bf16[272,1536]{1,0:T(8,128)(2,1)S(1)}, u32[]{:S(2)}, u32[]{:S(2)}) %collective-permute-start.6) | collective-permute-done | bytes 835616 | tf_op jit(solution)/shard_map/ppermute | solution.py:161
  55.5 1.2 collective-permute-done.5.refs_3_
  56.7 0.5 collective-permute-start.7
  57.2 0.5 collective-permute-start.8
  57.7 3.6 %collective-permute-done.10.refs_9_.refs_5_ = bf16[768,768]{1,0:T(8,128)(2,1)S(1)} collective-permute-done((bf16[768,768]{1,0:T(8,128)(2,1)}, bf16[768,768]{1,0:T(8,128)(2,1)S(1)}, u32[]{:S(2)}, u32[]{:S(2)}) %collective-permute-start.10) | collective-permute-done | bytes 1179680 | tf_op jit(solution)/shard_map/ppermute | solution.py:164
  61.3 1.0 collective-permute-done.11.refs_4_.refs_12_
  62.3 1.3 copy-done
  63.6 1.3 copy-done.2
  64.8 1.1 copy-done.5
  66.0 0.7 copy-done.7
  66.7 9.5 %experts.4 = (bf16[256,1536]{1,0:T(8,128)(2,1)S(1)}, bf16[256,1536]{1,0:T(8,128)(2,1)S(1)}, bf16[256,1536]{1,0:T(8,128)(2,1)S(1)}, bf16[256,1536]{1,0:T(8,128)(2...) custom-call(f32[8,128]{1,0:T(8,128)S(1)} %copy-done.7, bf16[272,1536]{1,0:T(8,128)(2,1)S(1)} %copy-done.5, ...), custom_call_target="tpu_custom_call" | custom-call | flops 1 | bytes 1 | tf_op jit(solution)/shard_map/experts/pallas_call | solution.py:199
  76.2 0.1 collective-permute-start.12
  76.3 2.3 %collective-permute-done.12.refs_1_ = bf16[272,1536]{1,0:T(8,128)(2,1)S(1)} collective-permute-done((bf16[272,1536]{1,0:T(8,128)(2,1)S(1)}, bf16[272,1536]{1,0:T(8,128)(2,1)S(1)}, u32[]{:S(2)}, u32[]{:S(2)}) %collective-permute-start.12) | collective-permute-done | bytes 835616 | tf_op jit(solution)/shard_map/ppermute | solution.py:161
  78.6 4.0 %experts.5 = (bf16[256,1536]{1,0:T(8,128)(2,1)S(1)}, bf16[256,1536]{1,0:T(8,128)(2,1)S(1)}) custom-call(f32[8,128]{1,0:T(8,128)S(1)} %copy-done.8, bf16[272,1536]{1,0:T(8,128)(2,1)S(1)} %collective-permute-done.9.refs_0_, bf16[272,1536]{1,0:T(8,128)(2,1)S(1)} %collective-permute-done.12.refs_1_, bf16[768,768]{1,0:T(8,128)(2,1)S(1)} %copy-done.1, ...), custom_call_target="tpu_custom_call" | custom-call | flops 1 | bytes 1 | tf_op jit(solution)/shard_map/experts/pallas_call | solution.py:199
  82.7 3.5 %collective-permute-done.7.refs_5_.refs_13_ = bf16[768,768]{1,0:T(8,128)(2,1)S(1)} collective-permute-done((bf16[768,768]{1,0:T(8,128)(2,1)S(1)}, bf16[768,768]{1,0:T(8,128)(2,1)S(1)}, u32[]{:S(2)}, u32[]{:S(2)}) %collective-permute-start.7) | collective-permute-done | bytes 1179680 | tf_op jit(solution)/shard_map/ppermute | solution.py:161
  86.2 4.2 %experts.6 = (bf16[256,1536]{1,0:T(8,128)(2,1)S(1)}, bf16[256,1536]{1,0:T(8,128)(2,1)S(1)}) custom-call(f32[8,128]{1,0:T(8,128)S(1)} %copy-done.8, bf16[272,1536]{1,0:T(8,128)(2,1)S(1)} %collective-permute-done.9.refs_0_, bf16[272,1536]{1,0:T(8,128)(2,1)S(1)} %collective-permute-done.12.refs_1_, bf16[256,1536]{1,0:T(8,128)(2,1)S(1)} %get-tuple-element.107.refs_2_, ...), custom_call_target="tpu_custom_call" | custom-call | flops 1 | bytes 1 | tf_op jit(solution)/shard_map/experts/pallas_call | solution.py:199
  90.4 0.1 collective-permute-start.13
  90.5 2.3 %collective-permute-done.13 = bf16[256,1536]{1,0:T(8,128)(2,1)S(1)} collective-permute-done((bf16[256,1536]{1,0:T(8,128)(2,1)S(1)}, bf16[256,1536]{1,0:T(8,128)(2,1)S(1)}, u32[]{:S(2)}, u32[]{:S(2)}) %collective-permute-start.13) | collective-permute-done | bytes 786464 | tf_op jit(solution)/shard_map/ppermute | solution.py:161
  92.8 0.2 add_convert_fusion.3
  93.0 1.6 %collective-permute-start.14 = (bf16[256,1536]{1,0:T(8,128)(2,1)S(1)}, bf16[256,1536]{1,0:T(8,128)(2,1)S(1)}, u32[]{:S(2)}, u32[]{:S(2)}) collective-permute-start(bf16[256,1536]{1,0:T(8,128)(2,1)S(1)} %add_convert_fusion.3), channel_id=1, source_target_pairs={{0,4},{1,5},{2,6},{3,7},{4,0},{5,1},{6,2},{7,3},{8,12},{9,13},{10,... | collective-permute-start | bytes 2359304 | tf_op jit(solution)/shard_map/ppermute | solution.py:161
  94.5 9.3 %experts.7 = (bf16[256,1536]{1,0:T(8,128)(2,1)S(1)}, bf16[256,1536]{1,0:T(8,128)(2,1)S(1)}, bf16[256,1536]{1,0:T(8,128)(2,1)S(1)}, bf16[256,1536]{1,0:T(8,128)(2...) custom-call(f32[8,128]{1,0:T(8,128)S(1)} %copy-done.8, ...), custom_call_target="tpu_custom_call" | custom-call | flops 1 | bytes 1 | tf_op jit(solution)/shard_map/experts/pallas_call | solution.py:199
  103.9 0.1 collective-permute-start.15
  104.0 0.5 collective-permute-start.16
  104.5 8.1 %collective-permute-done.14 = bf16[256,1536]{1,0:T(8,128)(2,1)S(1)} collective-permute-done((bf16[256,1536]{1,0:T(8,128)(2,1)S(1)}, bf16[256,1536]{1,0:T(8,128)(2,1)S(1)}, u32[]{:S(2)}, u32[]{:S(2)}) %collective-permute-start.14) | collective-permute-done | bytes 786464 | tf_op jit(solution)/shard_map/ppermute | solution.py:161
  112.6 0.3 add_convert_fusion.1
  112.9 0.0 copy-start.9
  112.9 2.6 %collective-permute-start.18 = (bf16[256,1536]{1,0:T(8,128)(2,1)S(1)}, bf16[256,1536]{1,0:T(8,128)(2,1)S(1)}, u32[]{:S(2)}, u32[]{:S(2)}) collective-permute-start(bf16[256,1536]{1,0:T(8,128)(2,1)S(1)} %add_convert_fusion.1), channel_id=1, source_target_pairs={{0,8},{1,9},{2,10},{3,11},{4,12},{5,13},{6,14},{7,15},{8,0},{9,1},... | collective-permute-start | bytes 2359304 | tf_op jit(solution)/shard_map/ppermute | solution.py:161
  115.5 0.2 add_convert_fusion.2
  115.7 1.6 %collective-permute-start.17 = (bf16[256,1536]{1,0:T(8,128)(2,1)S(1)}, bf16[256,1536]{1,0:T(8,128)(2,1)S(1)}, u32[]{:S(2)}, u32[]{:S(2)}) collective-permute-start(bf16[256,1536]{1,0:T(8,128)(2,1)S(1)} %add_convert_fusion.2), channel_id=1, source_target_pairs={{0,4},{1,5},{2,6},{3,7},{4,0},{5,1},{6,2},{7,3},{8,12},{9,13},{10,... | collective-permute-start | bytes 2359304 | tf_op jit(solution)/shard_map/ppermute | solution.py:161
  117.3 32.3 %collective-permute-done.18 = bf16[256,1536]{1,0:T(8,128)(2,1)S(1)} collective-permute-done((bf16[256,1536]{1,0:T(8,128)(2,1)S(1)}, bf16[256,1536]{1,0:T(8,128)(2,1)S(1)}, u32[]{:S(2)}, u32[]{:S(2)}) %collective-permute-start.18) | collective-permute-done | bytes 786464 | tf_op jit(solution)/shard_map/ppermute | solution.py:161
  149.6 0.4 collective-permute-done.17
  150.0 1.4 add_convert_fusion
  (25 shorter events, 0.1 us)
Async XLA Ops:
  0.0 7.6 %copy-start.10 = (f32[1536]{0:T(1024)S(1)}, f32[1536]{0:T(1024)}, u32[]{:S(2)}) copy-start(f32[1536]{0:T(1024)} %param.11) | copy-start | bytes 18436
  3.1 29.2 %collective-permute-start.3 = (bf16[768,768]{1,0:T(8,128)(2,1)}, bf16[768,768]{1,0:T(8,128)(2,1)S(1)}, u32[]{:S(2)}, u32[]{:S(2)}) collective-permute-start(bf16[768,768]{1,0:T(8,128)(2,1)} %get-tuple-element.87.refs_6_.refs_2_), channel_id=1, source_target_pairs={{0,16},{16,0},{1,17},{17,1},{2,18},{18,2},{3,19},{19,3},{4,20},{20... | collective-permute-start | bytes 3538952 | tf_op jit(solution)/shard_map/ppermute | solution.py:164
  6.1 27.6 %collective-permute-start.4 = (bf16[768,768]{1,0:T(8,128)(2,1)}, bf16[768,768]{1,0:T(8,128)(2,1)S(1)}, u32[]{:S(2)}, u32[]{:S(2)}) collective-permute-start(bf16[768,768]{1,0:T(8,128)(2,1)} %get-tuple-element.86.refs_8_.refs_4_), channel_id=1, source_target_pairs={{0,2},{1,3},{2,0},{3,1},{4,6},{5,7},{6,4},{7,5},{8,10},{9,11},{10,... | collective-permute-start | bytes 3538952 | tf_op jit(solution)/shard_map/ppermute | solution.py:161
  11.5 36.3 %collective-permute-start.1 = (bf16[272,1536]{1,0:T(8,128)(2,1)}, bf16[272,1536]{1,0:T(8,128)(2,1)S(1)}, u32[]{:S(2)}, u32[]{:S(2)}) collective-permute-start(bf16[272,1536]{1,0:T(8,128)(2,1)} %get-tuple-element.72.refs_0_.refs_4_), channel_id=1, source_target_pairs={{0,4},{1,5},{2,6},{3,7},{4,0},{5,1},{6,2},{7,3},{8,12},{9,13},{10,... | collective-permute-start | bytes 2506760 | tf_op jit(solution)/shard_map/ppermute | solution.py:161
  13.0 34.7 %collective-permute-start.2 = (bf16[272,1536]{1,0:T(8,128)(2,1)}, bf16[272,1536]{1,0:T(8,128)(2,1)S(1)}, u32[]{:S(2)}, u32[]{:S(2)}) collective-permute-start(bf16[272,1536]{1,0:T(8,128)(2,1)} %get-tuple-element.72.refs_0_.refs_4_), channel_id=1, source_target_pairs={{0,1},{1,0},{2,3},{3,2},{4,5},{5,4},{6,7},{7,6},{8,9},{9,8},{10,11... | collective-permute-start | bytes 2506760 | tf_op jit(solution)/shard_map/ppermute | solution.py:161
  13.0 40.1 %collective-permute-start = (bf16[272,1536]{1,0:T(8,128)(2,1)}, bf16[272,1536]{1,0:T(8,128)(2,1)S(1)}, u32[]{:S(2)}, u32[]{:S(2)}) collective-permute-start(bf16[272,1536]{1,0:T(8,128)(2,1)} %get-tuple-element.72.refs_0_.refs_4_), channel_id=1, source_target_pairs={{0,8},{1,9},{2,10},{3,11},{4,12},{5,13},{6,14},{7,15},{8,0},{9,1},... | collective-permute-start | bytes 2506760 | tf_op jit(solution)/shard_map/ppermute | solution.py:161
  33.8 27.5 %collective-permute-start.10 = (bf16[768,768]{1,0:T(8,128)(2,1)}, bf16[768,768]{1,0:T(8,128)(2,1)S(1)}, u32[]{:S(2)}, u32[]{:S(2)}) collective-permute-start(bf16[768,768]{1,0:T(8,128)(2,1)} %get-tuple-element.86.refs_8_.refs_4_), channel_id=1, source_target_pairs={{0,16},{16,0},{1,17},{17,1},{2,18},{18,2},{3,19},{19,3},{4,20},{20... | collective-permute-start | bytes 3538952 | tf_op jit(solution)/shard_map/ppermute | solution.py:164
  34.1 28.2 %collective-permute-start.11 = (bf16[768,768]{1,0:T(8,128)(2,1)}, bf16[768,768]{1,0:T(8,128)(2,1)S(1)}, u32[]{:S(2)}, u32[]{:S(2)}) collective-permute-start(bf16[768,768]{1,0:T(8,128)(2,1)} %get-tuple-element.87.refs_6_.refs_2_), channel_id=1, source_target_pairs={{0,2},{1,3},{2,0},{3,1},{4,6},{5,7},{6,4},{7,5},{8,10},{9,11},{10,... | collective-permute-start | bytes 3538952 | tf_op jit(solution)/shard_map/ppermute | solution.py:161
  53.1 2.4 %collective-permute-start.6 = (bf16[272,1536]{1,0:T(8,128)(2,1)S(1)}, bf16[272,1536]{1,0:T(8,128)(2,1)S(1)}, u32[]{:S(2)}, u32[]{:S(2)}) collective-permute-start(bf16[272,1536]{1,0:T(8,128)(2,1)S(1)} %collective-permute-done.refs_4_.refs_0_), channel_id=1, source_target_pairs={{0,1},{1,0},{2,3},{3,2},{4,5},{5,4},{6,7},{7,6},{8,9},{9,8},{10,11... | collective-permute-start | bytes 2506760 | tf_op jit(solution)/shard_map/ppermute | solution.py:161
  53.1 3.5 %collective-permute-start.5 = (bf16[272,1536]{1,0:T(8,128)(2,1)S(1)}, bf16[272,1536]{1,0:T(8,128)(2,1)S(1)}, u32[]{:S(2)}, u32[]{:S(2)}) collective-permute-start(bf16[272,1536]{1,0:T(8,128)(2,1)S(1)} %collective-permute-done.1.refs_2_), channel_id=1, source_target_pairs={{0,1},{1,0},{2,3},{3,2},{4,5},{5,4},{6,7},{7,6},{8,9},{9,8},{10,11... | collective-permute-start | bytes 2506760 | tf_op jit(solution)/shard_map/ppermute | solution.py:161
  53.6 22.6 %collective-permute-start.9 = (bf16[272,1536]{1,0:T(8,128)(2,1)S(1)}, bf16[272,1536]{1,0:T(8,128)(2,1)S(1)}, u32[]{:S(2)}, u32[]{:S(2)}) collective-permute-start(bf16[272,1536]{1,0:T(8,128)(2,1)S(1)} %collective-permute-done.refs_4_.refs_0_), channel_id=1, source_target_pairs={{0,4},{1,5},{2,6},{3,7},{4,0},{5,1},{6,2},{7,3},{8,12},{9,13},{10,... | collective-permute-start | bytes 2506760 | tf_op jit(solution)/shard_map/ppermute | solution.py:161
  56.7 29.5 %collective-permute-start.7 = (bf16[768,768]{1,0:T(8,128)(2,1)S(1)}, bf16[768,768]{1,0:T(8,128)(2,1)S(1)}, u32[]{:S(2)}, u32[]{:S(2)}) collective-permute-start(bf16[768,768]{1,0:T(8,128)(2,1)S(1)} %collective-permute-done.3.refs_7_.refs_3_), channel_id=1, source_target_pairs={{0,2},{1,3},{2,0},{3,1},{4,6},{5,7},{6,4},{7,5},{8,10},{9,11},{10,... | collective-permute-start | bytes 3538952 | tf_op jit(solution)/shard_map/ppermute | solution.py:161
  57.2 29.0 %collective-permute-start.8 = (bf16[768,768]{1,0:T(8,128)(2,1)S(1)}, bf16[768,768]{1,0:T(8,128)(2,1)S(1)}, u32[]{:S(2)}, u32[]{:S(2)}) collective-permute-start(bf16[768,768]{1,0:T(8,128)(2,1)S(1)} %collective-permute-done.4.refs_6_.refs_14_), channel_id=1, source_target_pairs={{0,16},{16,0},{1,17},{17,1},{2,18},{18,2},{3,19},{19,3},{4,20},{20... | collective-permute-start | bytes 3538952 | tf_op jit(solution)/shard_map/ppermute | solution.py:164
  62.3 1.3 copy-start
  63.6 1.3 copy-start.2
  64.8 1.1 copy-start.5
  66.0 0.7 copy-start.7
  66.7 12.0 %copy-start.1 = (bf16[768,768]{1,0:T(8,128)(2,1)S(1)}, bf16[768,768]{1,0:T(8,128)(2,1)}, u32[]{:S(2)}) copy-start(bf16[768,768]{1,0:T(8,128)(2,1)} %get-tuple-element.87.refs_6_.refs_2_) | copy-start | bytes 3538948
  66.7 12.0 %copy-start.3 = (bf16[768,768]{1,0:T(8,128)(2,1)S(1)}, bf16[768,768]{1,0:T(8,128)(2,1)}, u32[]{:S(2)}) copy-start(bf16[768,768]{1,0:T(8,128)(2,1)} %get-tuple-element.86.refs_8_.refs_4_) | copy-start | bytes 3538948
  66.7 12.0 %copy-start.8 = (f32[8,128]{1,0:T(8,128)S(1)}, f32[8,128]{1,0:T(8,128)}, u32[]{:S(2)}) copy-start(f32[8,128]{1,0:T(8,128)} %get-tuple-element.116._) | copy-start | bytes 12292
  76.2 2.4 %collective-permute-start.12 = (bf16[272,1536]{1,0:T(8,128)(2,1)S(1)}, bf16[272,1536]{1,0:T(8,128)(2,1)S(1)}, u32[]{:S(2)}, u32[]{:S(2)}) collective-permute-start(bf16[272,1536]{1,0:T(8,128)(2,1)S(1)} %collective-permute-done.9.refs_0_), channel_id=1, source_target_pairs={{0,1},{1,0},{2,3},{3,2},{4,5},{5,4},{6,7},{7,6},{8,9},{9,8},{10,11... | collective-permute-start | bytes 2506760 | tf_op jit(solution)/shard_map/ppermute | solution.py:161
  86.2 4.2 %copy-start.4 = (bf16[768,768]{1,0:T(8,128)(2,1)}, bf16[768,768]{1,0:T(8,128)(2,1)S(1)}, u32[]{:S(2)}) copy-start(bf16[768,768]{1,0:T(8,128)(2,1)S(1)} %collective-permute-done.8.refs_7_.refs_15_) | copy-start | bytes 3538948
  90.4 2.4 %collective-permute-start.13 = (bf16[256,1536]{1,0:T(8,128)(2,1)S(1)}, bf16[256,1536]{1,0:T(8,128)(2,1)S(1)}, u32[]{:S(2)}, u32[]{:S(2)}) collective-permute-start(bf16[256,1536]{1,0:T(8,128)(2,1)S(1)} %get-tuple-element.112), channel_id=1, source_target_pairs={{0,1},{1,0},{2,3},{3,2},{4,5},{5,4},{6,7},{7,6},{8,9},{9,8},{10,11... | collective-permute-start | bytes 2359304 | tf_op jit(solution)/shard_map/ppermute | solution.py:161
  92.8 1.8 %copy-start.6 = (bf16[272,1536]{1,0:T(8,128)(2,1)S(1)}, bf16[272,1536]{1,0:T(8,128)(2,1)}, u32[]{:S(2)}) copy-start(bf16[272,1536]{1,0:T(8,128)(2,1)} %get-tuple-element.72.refs_0_.refs_4_) | copy-start | bytes 2506756
  93.0 19.6 %collective-permute-start.14 = (bf16[256,1536]{1,0:T(8,128)(2,1)S(1)}, bf16[256,1536]{1,0:T(8,128)(2,1)S(1)}, u32[]{:S(2)}, u32[]{:S(2)}) collective-permute-start(bf16[256,1536]{1,0:T(8,128)(2,1)S(1)} %add_convert_fusion.3), channel_id=1, source_target_pairs={{0,4},{1,5},{2,6},{3,7},{4,0},{5,1},{6,2},{7,3},{8,12},{9,13},{10,... | collective-permute-start | bytes 2359304 | tf_op jit(solution)/shard_map/ppermute | solution.py:161
  103.9 8.7 %collective-permute-start.15 = (bf16[256,1536]{1,0:T(8,128)(2,1)S(1)}, bf16[256,1536]{1,0:T(8,128)(2,1)S(1)}, u32[]{:S(2)}, u32[]{:S(2)}) collective-permute-start(bf16[256,1536]{1,0:T(8,128)(2,1)S(1)} %get-tuple-element.125), channel_id=1, source_target_pairs={{0,1},{1,0},{2,3},{3,2},{4,5},{5,4},{6,7},{7,6},{8,9},{9,8},{10,11... | collective-permute-start | bytes 2359304 | tf_op jit(solution)/shard_map/ppermute | solution.py:161
  104.0 8.6 %collective-permute-start.16 = (bf16[256,1536]{1,0:T(8,128)(2,1)S(1)}, bf16[256,1536]{1,0:T(8,128)(2,1)S(1)}, u32[]{:S(2)}, u32[]{:S(2)}) collective-permute-start(bf16[256,1536]{1,0:T(8,128)(2,1)S(1)} %get-tuple-element.126), channel_id=1, source_target_pairs={{0,1},{1,0},{2,3},{3,2},{4,5},{5,4},{6,7},{7,6},{8,9},{9,8},{10,11... | collective-permute-start | bytes 2359304 | tf_op jit(solution)/shard_map/ppermute | solution.py:161
  112.9 37.1 %copy-start.9 = (bf16[256,1536]{1,0:T(8,128)(2,1)S(1)}, bf16[256,1536]{1,0:T(8,128)(2,1)}, u32[]{:S(2)}) copy-start(bf16[256,1536]{1,0:T(8,128)(2,1)} %tokens.1) | copy-start | bytes 2359300
  112.9 36.7 %collective-permute-start.18 = (bf16[256,1536]{1,0:T(8,128)(2,1)S(1)}, bf16[256,1536]{1,0:T(8,128)(2,1)S(1)}, u32[]{:S(2)}, u32[]{:S(2)}) collective-permute-start(bf16[256,1536]{1,0:T(8,128)(2,1)S(1)} %add_convert_fusion.1), channel_id=1, source_target_pairs={{0,8},{1,9},{2,10},{3,11},{4,12},{5,13},{6,14},{7,15},{8,0},{9,1},... | collective-permute-start | bytes 2359304 | tf_op jit(solution)/shard_map/ppermute | solution.py:161
  115.7 34.4 %collective-permute-start.17 = (bf16[256,1536]{1,0:T(8,128)(2,1)S(1)}, bf16[256,1536]{1,0:T(8,128)(2,1)S(1)}, u32[]{:S(2)}, u32[]{:S(2)}) collective-permute-start(bf16[256,1536]{1,0:T(8,128)(2,1)S(1)} %add_convert_fusion.2), channel_id=1, source_target_pairs={{0,4},{1,5},{2,6},{3,7},{4,0},{5,1},{6,2},{7,3},{8,12},{9,13},{10,... | collective-permute-start | bytes 2359304 | tf_op jit(solution)/shard_map/ppermute | solution.py:161
  117.3 32.7 %collective-permute-start.19 = (bf16[256,1536]{1,0:T(8,128)(2,1)S(1)}, bf16[256,1536]{1,0:T(8,128)(2,1)S(1)}, u32[]{:S(2)}, u32[]{:S(2)}) collective-permute-start(bf16[256,1536]{1,0:T(8,128)(2,1)S(1)} %get-tuple-element.136), channel_id=1, source_target_pairs={{0,1},{1,0},{2,3},{3,2},{4,5},{5,4},{6,7},{7,6},{8,9},{9,8},{10,11... | collective-permute-start | bytes 2359304 | tf_op jit(solution)/shard_map/ppermute | solution.py:161

commit v8 on v7

--- a/solution.py
+++ b/solution.py
@@ -78,20 +78,25 @@
 
 
 def pack_kernel(gate, up, down, *refs):
-    packed, sems = refs[:-1], refs[-1]
+    chunks = len(refs) - 3
+    packed, (held, arrived, left) = refs[:chunks], refs[chunks:]
     half = gate.shape[0]
-    copies = []
-    for h, chunk in enumerate(packed):
-        units = pl.ds(CHUNK * h, CHUNK)
-        copies.append((gate.at[:, units], chunk.at[:, pl.ds(0, CHUNK)]))
-        copies.append((up.at[:, units], chunk.at[:, pl.ds(CHUNK, CHUNK)]))
+    reads = []
+    for h in range(chunks):
+        units, chunk = pl.ds(CHUNK * h, CHUNK), held.at[h]
+        pairs = [(gate.at[:, units], chunk.at[:, pl.ds(0, CHUNK)]), (up.at[:, units], chunk.at[:, pl.ds(CHUNK, CHUNK)])]
         for i in range(half // CHUNK):
             columns = pl.ds(CHUNK * i, CHUNK)
-            copies.append((down.at[units, columns], chunk.at[columns, pl.ds(2 * CHUNK, CHUNK)]))
-    copies = [pltpu.make_async_copy(source, target, sems.at[i]) for i, (source, target) in enumerate(copies)]
-    for copy in copies:
-        copy.start()
-    for copy in copies:
+            pairs.append((down.at[units, columns], chunk.at[columns, pl.ds(2 * CHUNK, CHUNK)]))
+        reads.append([pltpu.make_async_copy(source, target, arrived.at[h, i]) for i, (source, target) in enumerate(pairs)])
+        for copy in reads[-1]:
+            copy.start()
+    writes = [pltpu.make_async_copy(held.at[h], packed[h], left.at[h]) for h in range(chunks)]
+    for h in range(chunks):
+        for copy in reads[h]:
+            copy.wait()
+        writes[h].start()
+    for copy in writes:
         copy.wait()
 
 
@@ -172,8 +177,12 @@
         pack_kernel,
         out_shape=(jax.ShapeDtypeStruct((half, half), BF16),) * (hid // CHUNK),
         in_specs=[anywhere] * 3,
-        out_specs=(vmem,) * (hid // CHUNK),
-        scratch_shapes=[pltpu.SemaphoreType.DMA((hid // CHUNK * (2 + half // CHUNK),))],
+        out_specs=(anywhere,) * (hid // CHUNK),
+        scratch_shapes=[
+            pltpu.VMEM((hid // CHUNK, half, half), BF16),
+            pltpu.SemaphoreType.DMA((hid // CHUNK, 2 + half // CHUNK)),
+            pltpu.SemaphoreType.DMA((hid // CHUNK,)),
+        ],
         name="pack",
     )(w_gate[0], w_up[0], w_down[0])
     x_0 = across(own[0])

time: 152 us -> 151 us (level)
  no operation moved by 1% of the time
where the time goes in v8:
time: 151 us
  waiting for transfers between devices  92 us (61%)
  Pallas kernels  32.5 us (22%)
  starting transfers between devices  18.8 us (12%)
  local copies, waits for them, and re-layouts  5 us (3%)
  other arithmetic  2.04 us (1%)
    ppermute x17, waiting for transfers between devices, send(): return lax.ppermute(v, 'tensor', pairs)  71.8 us
    pallas_call x4, Pallas kernels, run(): pl.pallas_call(functools.partial(expert_kernel, tuple(((e, first, last) f...  27.1 us
    ppermute x3, waiting for transfers between devices, across(): return lax.ppermute(v, 'dp', [(0, 1), (1, 0)])  20.2 us
    ppermute x17, starting transfers between devices, send(): return lax.ppermute(v, 'tensor', pairs)  14.9 us
    unnamed x22, local copies, waits for them, and re-layouts  4.4 us
    ppermute x3, starting transfers between devices, across(): return lax.ppermute(v, 'dp', [(0, 1), (1, 0)])  3.89 us
  transfers between devices with their start and end apart: 20, of which 14 were waited for; matrix products, arithmetic and copies ran while one was open for 1% of the time, Pallas kernels for 17%

profile of v8, /device:TPU:0, one launch (start us, length us, event | category | flops | bytes accessed | tf_op | source)
XLA Modules:
  0.0 151.1 jit_solution(10388111446682773413)
XLA Ops:
  0.0 2.8 %pack.1 = (bf16[768,768]{1,0:T(8,128)(2,1)}, bf16[768,768]{1,0:T(8,128)(2,1)}) custom-call(bf16[768,512]{1,0:T(8,128)(2,1)} %bitcast.5, bf16[768,512]{1,0:T(8,128)(2,1)} %bitcast.6, bf16[512,768]{1,0:T(8,128)(2,1)} %bitcast.7), custom_call_target="tpu_custom_call" | custom-call | tf_op jit(solution)/shard_map/pack/pallas_call | solution.py:176
  2.8 3.0 %collective-permute-start.3 = (bf16[768,768]{1,0:T(8,128)(2,1)}, bf16[768,768]{1,0:T(8,128)(2,1)S(1)}, u32[]{:S(2)}, u32[]{:S(2)}) collective-permute-start(bf16[768,768]{1,0:T(8,128)(2,1)} %get-tuple-element.87.refs_6_.refs_2_), channel_id=1, source_target_pairs={{0,16},{16,0},{1,17},{17,1},{2,18},{18,2},{3,19},{19,3},{4,20},{20... | collective-permute-start | bytes 3538952 | tf_op jit(solution)/shard_map/ppermute | solution.py:169
  5.8 1.5 %collective-permute-start.4 = (bf16[768,768]{1,0:T(8,128)(2,1)}, bf16[768,768]{1,0:T(8,128)(2,1)S(1)}, u32[]{:S(2)}, u32[]{:S(2)}) collective-permute-start(bf16[768,768]{1,0:T(8,128)(2,1)} %get-tuple-element.86.refs_8_.refs_4_), channel_id=1, source_target_pairs={{0,2},{1,3},{2,0},{3,1},{4,6},{5,7},{6,4},{7,5},{8,10},{9,11},{10,... | collective-permute-start | bytes 3538952 | tf_op jit(solution)/shard_map/ppermute | solution.py:166
  7.3 0.6 reshape.3.gain
  8.5 2.6 %prologue.1 = (bf16[272,1536]{1,0:T(8,128)(2,1)}, f32[8,128]{1,0:T(8,128)}) custom-call(s32[1]{0:T(128)S(6)} %copy.9.lengths, bf16[256,1536]{1,0:T(8,128)(2,1)} %tokens.1, f32[1,1536]{1,0:T(1,128)} %reshape.3.gain, bf16[16,1536]{1,0:T(8,128)(2,1)} %bitcast.8, s32[8,256]{1,0:T(8,128)} %bitcast.9), custom_call_target="tpu_custom_call" | custom-call | tf_op jit(solution)/shard_map/prologue/pallas_call | solution.py:190
  11.1 1.6 %collective-permute-start.1 = (bf16[272,1536]{1,0:T(8,128)(2,1)}, bf16[272,1536]{1,0:T(8,128)(2,1)S(1)}, u32[]{:S(2)}, u32[]{:S(2)}) collective-permute-start(bf16[272,1536]{1,0:T(8,128)(2,1)} %get-tuple-element.72.refs_0_.refs_4_), channel_id=1, source_target_pairs={{0,4},{1,5},{2,6},{3,7},{4,0},{5,1},{6,2},{7,3},{8,12},{9,13},{10,... | collective-permute-start | bytes 2506760 | tf_op jit(solution)/shard_map/ppermute | solution.py:166
  12.7 0.0 collective-permute-start.2
  12.7 2.6 %collective-permute-start = (bf16[272,1536]{1,0:T(8,128)(2,1)}, bf16[272,1536]{1,0:T(8,128)(2,1)S(1)}, u32[]{:S(2)}, u32[]{:S(2)}) collective-permute-start(bf16[272,1536]{1,0:T(8,128)(2,1)} %get-tuple-element.72.refs_0_.refs_4_), channel_id=1, source_target_pairs={{0,8},{1,9},{2,10},{3,11},{4,12},{5,13},{6,14},{7,15},{8,0},{9,1},... | collective-permute-start | bytes 2506760 | tf_op jit(solution)/shard_map/ppermute | solution.py:166
  15.3 16.7 %collective-permute-done.3.refs_7_.refs_3_ = bf16[768,768]{1,0:T(8,128)(2,1)S(1)} collective-permute-done((bf16[768,768]{1,0:T(8,128)(2,1)}, bf16[768,768]{1,0:T(8,128)(2,1)S(1)}, u32[]{:S(2)}, u32[]{:S(2)}) %collective-permute-start.3) | collective-permute-done | bytes 1179680 | tf_op jit(solution)/shard_map/ppermute | solution.py:169
  31.9 1.5 collective-permute-done.4.refs_6_.refs_14_
  33.4 0.4 collective-permute-start.10
  33.8 1.7 %collective-permute-start.11 = (bf16[768,768]{1,0:T(8,128)(2,1)}, bf16[768,768]{1,0:T(8,128)(2,1)S(1)}, u32[]{:S(2)}, u32[]{:S(2)}) collective-permute-start(bf16[768,768]{1,0:T(8,128)(2,1)} %get-tuple-element.87.refs_6_.refs_2_), channel_id=1, source_target_pairs={{0,2},{1,3},{2,0},{3,1},{4,6},{5,7},{6,4},{7,5},{8,10},{9,11},{10,... | collective-permute-start | bytes 3538952 | tf_op jit(solution)/shard_map/ppermute | solution.py:166
  35.5 11.9 %collective-permute-done.1.refs_2_ = bf16[272,1536]{1,0:T(8,128)(2,1)S(1)} collective-permute-done((bf16[272,1536]{1,0:T(8,128)(2,1)}, bf16[272,1536]{1,0:T(8,128)(2,1)S(1)}, u32[]{:S(2)}, u32[]{:S(2)}) %collective-permute-start.1) | collective-permute-done | bytes 835616 | tf_op jit(solution)/shard_map/ppermute | solution.py:166
  47.4 5.4 %collective-permute-done.refs_4_.refs_0_ = bf16[272,1536]{1,0:T(8,128)(2,1)S(1)} collective-permute-done((bf16[272,1536]{1,0:T(8,128)(2,1)}, bf16[272,1536]{1,0:T(8,128)(2,1)S(1)}, u32[]{:S(2)}, u32[]{:S(2)}) %collective-permute-start) | collective-permute-done | bytes 835616 | tf_op jit(solution)/shard_map/ppermute | solution.py:166
  52.8 0.0 collective-permute-start.6
  52.8 0.5 collective-permute-start.5
  53.3 1.8 %collective-permute-done.6.refs_5_.refs_1_ = bf16[272,1536]{1,0:T(8,128)(2,1)S(1)} collective-permute-done((bf16[272,1536]{1,0:T(8,128)(2,1)S(1)}, bf16[272,1536]{1,0:T(8,128)(2,1)S(1)}, u32[]{:S(2)}, u32[]{:S(2)}) %collective-permute-start.6) | collective-permute-done | bytes 835616 | tf_op jit(solution)/shard_map/ppermute | solution.py:166
  55.1 1.2 collective-permute-done.5.refs_3_
  56.3 0.5 collective-permute-start.7
  56.8 0.5 collective-permute-start.8
  57.4 3.6 %collective-permute-done.10.refs_9_.refs_5_ = bf16[768,768]{1,0:T(8,128)(2,1)S(1)} collective-permute-done((bf16[768,768]{1,0:T(8,128)(2,1)}, bf16[768,768]{1,0:T(8,128)(2,1)S(1)}, u32[]{:S(2)}, u32[]{:S(2)}) %collective-permute-start.10) | collective-permute-done | bytes 1179680 | tf_op jit(solution)/shard_map/ppermute | solution.py:169
  60.9 1.0 collective-permute-done.11.refs_4_.refs_12_
  62.0 1.3 copy-done
  63.2 1.3 copy-done.2
  64.5 1.1 copy-done.5
  65.6 0.7 copy-done.7
  66.3 9.5 %experts.4 = (bf16[256,1536]{1,0:T(8,128)(2,1)S(1)}, bf16[256,1536]{1,0:T(8,128)(2,1)S(1)}, bf16[256,1536]{1,0:T(8,128)(2,1)S(1)}, bf16[256,1536]{1,0:T(8,128)(2...) custom-call(f32[8,128]{1,0:T(8,128)S(1)} %copy-done.7, bf16[272,1536]{1,0:T(8,128)(2,1)S(1)} %copy-done.5, ...), custom_call_target="tpu_custom_call" | custom-call | flops 1 | bytes 1 | tf_op jit(solution)/shard_map/experts/pallas_call | solution.py:208
  75.9 0.1 collective-permute-start.12
  76.0 2.3 %collective-permute-done.12.refs_1_ = bf16[272,1536]{1,0:T(8,128)(2,1)S(1)} collective-permute-done((bf16[272,1536]{1,0:T(8,128)(2,1)S(1)}, bf16[272,1536]{1,0:T(8,128)(2,1)S(1)}, u32[]{:S(2)}, u32[]{:S(2)}) %collective-permute-start.12) | collective-permute-done | bytes 835616 | tf_op jit(solution)/shard_map/ppermute | solution.py:166
  78.3 4.0 %experts.5 = (bf16[256,1536]{1,0:T(8,128)(2,1)S(1)}, bf16[256,1536]{1,0:T(8,128)(2,1)S(1)}) custom-call(f32[8,128]{1,0:T(8,128)S(1)} %copy-done.8, bf16[272,1536]{1,0:T(8,128)(2,1)S(1)} %collective-permute-done.9.refs_0_, bf16[272,1536]{1,0:T(8,128)(2,1)S(1)} %collective-permute-done.12.refs_1_, bf16[768,768]{1,0:T(8,128)(2,1)S(1)} %copy-done.1, ...), custom_call_target="tpu_custom_call" | custom-call | flops 1 | bytes 1 | tf_op jit(solution)/shard_map/experts/pallas_call | solution.py:208
  82.3 3.5 %collective-permute-done.7.refs_5_.refs_13_ = bf16[768,768]{1,0:T(8,128)(2,1)S(1)} collective-permute-done((bf16[768,768]{1,0:T(8,128)(2,1)S(1)}, bf16[768,768]{1,0:T(8,128)(2,1)S(1)}, u32[]{:S(2)}, u32[]{:S(2)}) %collective-permute-start.7) | collective-permute-done | bytes 1179680 | tf_op jit(solution)/shard_map/ppermute | solution.py:166
  85.8 4.2 %experts.6 = (bf16[256,1536]{1,0:T(8,128)(2,1)S(1)}, bf16[256,1536]{1,0:T(8,128)(2,1)S(1)}) custom-call(f32[8,128]{1,0:T(8,128)S(1)} %copy-done.8, bf16[272,1536]{1,0:T(8,128)(2,1)S(1)} %collective-permute-done.9.refs_0_, bf16[272,1536]{1,0:T(8,128)(2,1)S(1)} %collective-permute-done.12.refs_1_, bf16[256,1536]{1,0:T(8,128)(2,1)S(1)} %get-tuple-element.107.refs_2_, ...), custom_call_target="tpu_custom_call" | custom-call | flops 1 | bytes 1 | tf_op jit(solution)/shard_map/experts/pallas_call | solution.py:208
  90.1 0.1 collective-permute-start.13
  90.1 2.3 %collective-permute-done.13 = bf16[256,1536]{1,0:T(8,128)(2,1)S(1)} collective-permute-done((bf16[256,1536]{1,0:T(8,128)(2,1)S(1)}, bf16[256,1536]{1,0:T(8,128)(2,1)S(1)}, u32[]{:S(2)}, u32[]{:S(2)}) %collective-permute-start.13) | collective-permute-done | bytes 786464 | tf_op jit(solution)/shard_map/ppermute | solution.py:166
  92.4 0.2 add_convert_fusion.3
  92.6 1.6 %collective-permute-start.14 = (bf16[256,1536]{1,0:T(8,128)(2,1)S(1)}, bf16[256,1536]{1,0:T(8,128)(2,1)S(1)}, u32[]{:S(2)}, u32[]{:S(2)}) collective-permute-start(bf16[256,1536]{1,0:T(8,128)(2,1)S(1)} %add_convert_fusion.3), channel_id=1, source_target_pairs={{0,4},{1,5},{2,6},{3,7},{4,0},{5,1},{6,2},{7,3},{8,12},{9,13},{10,... | collective-permute-start | bytes 2359304 | tf_op jit(solution)/shard_map/ppermute | solution.py:166
  94.2 9.4 %experts.7 = (bf16[256,1536]{1,0:T(8,128)(2,1)S(1)}, bf16[256,1536]{1,0:T(8,128)(2,1)S(1)}, bf16[256,1536]{1,0:T(8,128)(2,1)S(1)}, bf16[256,1536]{1,0:T(8,128)(2...) custom-call(f32[8,128]{1,0:T(8,128)S(1)} %copy-done.8, ...), custom_call_target="tpu_custom_call" | custom-call | flops 1 | bytes 1 | tf_op jit(solution)/shard_map/experts/pallas_call | solution.py:208
  103.5 0.1 collective-permute-start.15
  103.6 0.5 collective-permute-start.16
  104.1 8.1 %collective-permute-done.14 = bf16[256,1536]{1,0:T(8,128)(2,1)S(1)} collective-permute-done((bf16[256,1536]{1,0:T(8,128)(2,1)S(1)}, bf16[256,1536]{1,0:T(8,128)(2,1)S(1)}, u32[]{:S(2)}, u32[]{:S(2)}) %collective-permute-start.14) | collective-permute-done | bytes 786464 | tf_op jit(solution)/shard_map/ppermute | solution.py:166
  112.3 0.3 add_convert_fusion.1
  112.6 0.0 copy-start.9
  112.6 2.6 %collective-permute-start.18 = (bf16[256,1536]{1,0:T(8,128)(2,1)S(1)}, bf16[256,1536]{1,0:T(8,128)(2,1)S(1)}, u32[]{:S(2)}, u32[]{:S(2)}) collective-permute-start(bf16[256,1536]{1,0:T(8,128)(2,1)S(1)} %add_convert_fusion.1), channel_id=1, source_target_pairs={{0,8},{1,9},{2,10},{3,11},{4,12},{5,13},{6,14},{7,15},{8,0},{9,1},... | collective-permute-start | bytes 2359304 | tf_op jit(solution)/shard_map/ppermute | solution.py:166
  115.2 0.2 add_convert_fusion.2
  115.4 1.6 %collective-permute-start.17 = (bf16[256,1536]{1,0:T(8,128)(2,1)S(1)}, bf16[256,1536]{1,0:T(8,128)(2,1)S(1)}, u32[]{:S(2)}, u32[]{:S(2)}) collective-permute-start(bf16[256,1536]{1,0:T(8,128)(2,1)S(1)} %add_convert_fusion.2), channel_id=1, source_target_pairs={{0,4},{1,5},{2,6},{3,7},{4,0},{5,1},{6,2},{7,3},{8,12},{9,13},{10,... | collective-permute-start | bytes 2359304 | tf_op jit(solution)/shard_map/ppermute | solution.py:166
  117.0 32.3 %collective-permute-done.18 = bf16[256,1536]{1,0:T(8,128)(2,1)S(1)} collective-permute-done((bf16[256,1536]{1,0:T(8,128)(2,1)S(1)}, bf16[256,1536]{1,0:T(8,128)(2,1)S(1)}, u32[]{:S(2)}, u32[]{:S(2)}) %collective-permute-start.18) | collective-permute-done | bytes 786464 | tf_op jit(solution)/shard_map/ppermute | solution.py:166
  149.3 0.4 collective-permute-done.17
  149.7 1.4 add_convert_fusion
  (25 shorter events, 0.1 us)
Async XLA Ops:
  0.0 7.3 %copy-start.10 = (f32[1536]{0:T(1024)S(1)}, f32[1536]{0:T(1024)}, u32[]{:S(2)}) copy-start(f32[1536]{0:T(1024)} %param.11) | copy-start | bytes 18436
  2.8 29.2 %collective-permute-start.3 = (bf16[768,768]{1,0:T(8,128)(2,1)}, bf16[768,768]{1,0:T(8,128)(2,1)S(1)}, u32[]{:S(2)}, u32[]{:S(2)}) collective-permute-start(bf16[768,768]{1,0:T(8,128)(2,1)} %get-tuple-element.87.refs_6_.refs_2_), channel_id=1, source_target_pairs={{0,16},{16,0},{1,17},{17,1},{2,18},{18,2},{3,19},{19,3},{4,20},{20... | collective-permute-start | bytes 3538952 | tf_op jit(solution)/shard_map/ppermute | solution.py:169
  5.8 27.6 %collective-permute-start.4 = (bf16[768,768]{1,0:T(8,128)(2,1)}, bf16[768,768]{1,0:T(8,128)(2,1)S(1)}, u32[]{:S(2)}, u32[]{:S(2)}) collective-permute-start(bf16[768,768]{1,0:T(8,128)(2,1)} %get-tuple-element.86.refs_8_.refs_4_), channel_id=1, source_target_pairs={{0,2},{1,3},{2,0},{3,1},{4,6},{5,7},{6,4},{7,5},{8,10},{9,11},{10,... | collective-permute-start | bytes 3538952 | tf_op jit(solution)/shard_map/ppermute | solution.py:166
  11.1 36.3 %collective-permute-start.1 = (bf16[272,1536]{1,0:T(8,128)(2,1)}, bf16[272,1536]{1,0:T(8,128)(2,1)S(1)}, u32[]{:S(2)}, u32[]{:S(2)}) collective-permute-start(bf16[272,1536]{1,0:T(8,128)(2,1)} %get-tuple-element.72.refs_0_.refs_4_), channel_id=1, source_target_pairs={{0,4},{1,5},{2,6},{3,7},{4,0},{5,1},{6,2},{7,3},{8,12},{9,13},{10,... | collective-permute-start | bytes 2506760 | tf_op jit(solution)/shard_map/ppermute | solution.py:166
  12.7 34.7 %collective-permute-start.2 = (bf16[272,1536]{1,0:T(8,128)(2,1)}, bf16[272,1536]{1,0:T(8,128)(2,1)S(1)}, u32[]{:S(2)}, u32[]{:S(2)}) collective-permute-start(bf16[272,1536]{1,0:T(8,128)(2,1)} %get-tuple-element.72.refs_0_.refs_4_), channel_id=1, source_target_pairs={{0,1},{1,0},{2,3},{3,2},{4,5},{5,4},{6,7},{7,6},{8,9},{9,8},{10,11... | collective-permute-start | bytes 2506760 | tf_op jit(solution)/shard_map/ppermute | solution.py:166
  12.7 40.1 %collective-permute-start = (bf16[272,1536]{1,0:T(8,128)(2,1)}, bf16[272,1536]{1,0:T(8,128)(2,1)S(1)}, u32[]{:S(2)}, u32[]{:S(2)}) collective-permute-start(bf16[272,1536]{1,0:T(8,128)(2,1)} %get-tuple-element.72.refs_0_.refs_4_), channel_id=1, source_target_pairs={{0,8},{1,9},{2,10},{3,11},{4,12},{5,13},{6,14},{7,15},{8,0},{9,1},... | collective-permute-start | bytes 2506760 | tf_op jit(solution)/shard_map/ppermute | solution.py:166
  33.4 27.5 %collective-permute-start.10 = (bf16[768,768]{1,0:T(8,128)(2,1)}, bf16[768,768]{1,0:T(8,128)(2,1)S(1)}, u32[]{:S(2)}, u32[]{:S(2)}) collective-permute-start(bf16[768,768]{1,0:T(8,128)(2,1)} %get-tuple-element.86.refs_8_.refs_4_), channel_id=1, source_target_pairs={{0,16},{16,0},{1,17},{17,1},{2,18},{18,2},{3,19},{19,3},{4,20},{20... | collective-permute-start | bytes 3538952 | tf_op jit(solution)/shard_map/ppermute | solution.py:169
  33.8 28.2 %collective-permute-start.11 = (bf16[768,768]{1,0:T(8,128)(2,1)}, bf16[768,768]{1,0:T(8,128)(2,1)S(1)}, u32[]{:S(2)}, u32[]{:S(2)}) collective-permute-start(bf16[768,768]{1,0:T(8,128)(2,1)} %get-tuple-element.87.refs_6_.refs_2_), channel_id=1, source_target_pairs={{0,2},{1,3},{2,0},{3,1},{4,6},{5,7},{6,4},{7,5},{8,10},{9,11},{10,... | collective-permute-start | bytes 3538952 | tf_op jit(solution)/shard_map/ppermute | solution.py:166
  52.8 2.4 %collective-permute-start.6 = (bf16[272,1536]{1,0:T(8,128)(2,1)S(1)}, bf16[272,1536]{1,0:T(8,128)(2,1)S(1)}, u32[]{:S(2)}, u32[]{:S(2)}) collective-permute-start(bf16[272,1536]{1,0:T(8,128)(2,1)S(1)} %collective-permute-done.refs_4_.refs_0_), channel_id=1, source_target_pairs={{0,1},{1,0},{2,3},{3,2},{4,5},{5,4},{6,7},{7,6},{8,9},{9,8},{10,11... | collective-permute-start | bytes 2506760 | tf_op jit(solution)/shard_map/ppermute | solution.py:166
  52.8 3.5 %collective-permute-start.5 = (bf16[272,1536]{1,0:T(8,128)(2,1)S(1)}, bf16[272,1536]{1,0:T(8,128)(2,1)S(1)}, u32[]{:S(2)}, u32[]{:S(2)}) collective-permute-start(bf16[272,1536]{1,0:T(8,128)(2,1)S(1)} %collective-permute-done.1.refs_2_), channel_id=1, source_target_pairs={{0,1},{1,0},{2,3},{3,2},{4,5},{5,4},{6,7},{7,6},{8,9},{9,8},{10,11... | collective-permute-start | bytes 2506760 | tf_op jit(solution)/shard_map/ppermute | solution.py:166
  53.3 22.6 %collective-permute-start.9 = (bf16[272,1536]{1,0:T(8,128)(2,1)S(1)}, bf16[272,1536]{1,0:T(8,128)(2,1)S(1)}, u32[]{:S(2)}, u32[]{:S(2)}) collective-permute-start(bf16[272,1536]{1,0:T(8,128)(2,1)S(1)} %collective-permute-done.refs_4_.refs_0_), channel_id=1, source_target_pairs={{0,4},{1,5},{2,6},{3,7},{4,0},{5,1},{6,2},{7,3},{8,12},{9,13},{10,... | collective-permute-start | bytes 2506760 | tf_op jit(solution)/shard_map/ppermute | solution.py:166
  56.3 29.5 %collective-permute-start.7 = (bf16[768,768]{1,0:T(8,128)(2,1)S(1)}, bf16[768,768]{1,0:T(8,128)(2,1)S(1)}, u32[]{:S(2)}, u32[]{:S(2)}) collective-permute-start(bf16[768,768]{1,0:T(8,128)(2,1)S(1)} %collective-permute-done.3.refs_7_.refs_3_), channel_id=1, source_target_pairs={{0,2},{1,3},{2,0},{3,1},{4,6},{5,7},{6,4},{7,5},{8,10},{9,11},{10,... | collective-permute-start | bytes 3538952 | tf_op jit(solution)/shard_map/ppermute | solution.py:166
  56.8 29.0 %collective-permute-start.8 = (bf16[768,768]{1,0:T(8,128)(2,1)S(1)}, bf16[768,768]{1,0:T(8,128)(2,1)S(1)}, u32[]{:S(2)}, u32[]{:S(2)}) collective-permute-start(bf16[768,768]{1,0:T(8,128)(2,1)S(1)} %collective-permute-done.4.refs_6_.refs_14_), channel_id=1, source_target_pairs={{0,16},{16,0},{1,17},{17,1},{2,18},{18,2},{3,19},{19,3},{4,20},{20... | collective-permute-start | bytes 3538952 | tf_op jit(solution)/shard_map/ppermute | solution.py:169
  62.0 1.3 copy-start
  63.2 1.3 copy-start.2
  64.5 1.1 copy-start.5
  65.6 0.7 copy-start.7
  66.3 12.0 %copy-start.1 = (bf16[768,768]{1,0:T(8,128)(2,1)S(1)}, bf16[768,768]{1,0:T(8,128)(2,1)}, u32[]{:S(2)}) copy-start(bf16[768,768]{1,0:T(8,128)(2,1)} %get-tuple-element.87.refs_6_.refs_2_) | copy-start | bytes 3538948
  66.3 12.0 %copy-start.3 = (bf16[768,768]{1,0:T(8,128)(2,1)S(1)}, bf16[768,768]{1,0:T(8,128)(2,1)}, u32[]{:S(2)}) copy-start(bf16[768,768]{1,0:T(8,128)(2,1)} %get-tuple-element.86.refs_8_.refs_4_) | copy-start | bytes 3538948
  66.3 12.0 %copy-start.8 = (f32[8,128]{1,0:T(8,128)S(1)}, f32[8,128]{1,0:T(8,128)}, u32[]{:S(2)}) copy-start(f32[8,128]{1,0:T(8,128)} %get-tuple-element.116._) | copy-start | bytes 12292
  75.9 2.4 %collective-permute-start.12 = (bf16[272,1536]{1,0:T(8,128)(2,1)S(1)}, bf16[272,1536]{1,0:T(8,128)(2,1)S(1)}, u32[]{:S(2)}, u32[]{:S(2)}) collective-permute-start(bf16[272,1536]{1,0:T(8,128)(2,1)S(1)} %collective-permute-done.9.refs_0_), channel_id=1, source_target_pairs={{0,1},{1,0},{2,3},{3,2},{4,5},{5,4},{6,7},{7,6},{8,9},{9,8},{10,11... | collective-permute-start | bytes 2506760 | tf_op jit(solution)/shard_map/ppermute | solution.py:166
  85.8 4.2 %copy-start.4 = (bf16[768,768]{1,0:T(8,128)(2,1)}, bf16[768,768]{1,0:T(8,128)(2,1)S(1)}, u32[]{:S(2)}) copy-start(bf16[768,768]{1,0:T(8,128)(2,1)S(1)} %collective-permute-done.8.refs_7_.refs_15_) | copy-start | bytes 3538948
  90.1 2.4 %collective-permute-start.13 = (bf16[256,1536]{1,0:T(8,128)(2,1)S(1)}, bf16[256,1536]{1,0:T(8,128)(2,1)S(1)}, u32[]{:S(2)}, u32[]{:S(2)}) collective-permute-start(bf16[256,1536]{1,0:T(8,128)(2,1)S(1)} %get-tuple-element.112), channel_id=1, source_target_pairs={{0,1},{1,0},{2,3},{3,2},{4,5},{5,4},{6,7},{7,6},{8,9},{9,8},{10,11... | collective-permute-start | bytes 2359304 | tf_op jit(solution)/shard_map/ppermute | solution.py:166
  92.4 1.8 %copy-start.6 = (bf16[272,1536]{1,0:T(8,128)(2,1)S(1)}, bf16[272,1536]{1,0:T(8,128)(2,1)}, u32[]{:S(2)}) copy-start(bf16[272,1536]{1,0:T(8,128)(2,1)} %get-tuple-element.72.refs_0_.refs_4_) | copy-start | bytes 2506756
  92.6 19.6 %collective-permute-start.14 = (bf16[256,1536]{1,0:T(8,128)(2,1)S(1)}, bf16[256,1536]{1,0:T(8,128)(2,1)S(1)}, u32[]{:S(2)}, u32[]{:S(2)}) collective-permute-start(bf16[256,1536]{1,0:T(8,128)(2,1)S(1)} %add_convert_fusion.3), channel_id=1, source_target_pairs={{0,4},{1,5},{2,6},{3,7},{4,0},{5,1},{6,2},{7,3},{8,12},{9,13},{10,... | collective-permute-start | bytes 2359304 | tf_op jit(solution)/shard_map/ppermute | solution.py:166
  103.5 8.7 %collective-permute-start.15 = (bf16[256,1536]{1,0:T(8,128)(2,1)S(1)}, bf16[256,1536]{1,0:T(8,128)(2,1)S(1)}, u32[]{:S(2)}, u32[]{:S(2)}) collective-permute-start(bf16[256,1536]{1,0:T(8,128)(2,1)S(1)} %get-tuple-element.125), channel_id=1, source_target_pairs={{0,1},{1,0},{2,3},{3,2},{4,5},{5,4},{6,7},{7,6},{8,9},{9,8},{10,11... | collective-permute-start | bytes 2359304 | tf_op jit(solution)/shard_map/ppermute | solution.py:166
  103.6 8.6 %collective-permute-start.16 = (bf16[256,1536]{1,0:T(8,128)(2,1)S(1)}, bf16[256,1536]{1,0:T(8,128)(2,1)S(1)}, u32[]{:S(2)}, u32[]{:S(2)}) collective-permute-start(bf16[256,1536]{1,0:T(8,128)(2,1)S(1)} %get-tuple-element.126), channel_id=1, source_target_pairs={{0,1},{1,0},{2,3},{3,2},{4,5},{5,4},{6,7},{7,6},{8,9},{9,8},{10,11... | collective-permute-start | bytes 2359304 | tf_op jit(solution)/shard_map/ppermute | solution.py:166
  112.6 37.1 %copy-start.9 = (bf16[256,1536]{1,0:T(8,128)(2,1)S(1)}, bf16[256,1536]{1,0:T(8,128)(2,1)}, u32[]{:S(2)}) copy-start(bf16[256,1536]{1,0:T(8,128)(2,1)} %tokens.1) | copy-start | bytes 2359300
  112.6 36.7 %collective-permute-start.18 = (bf16[256,1536]{1,0:T(8,128)(2,1)S(1)}, bf16[256,1536]{1,0:T(8,128)(2,1)S(1)}, u32[]{:S(2)}, u32[]{:S(2)}) collective-permute-start(bf16[256,1536]{1,0:T(8,128)(2,1)S(1)} %add_convert_fusion.1), channel_id=1, source_target_pairs={{0,8},{1,9},{2,10},{3,11},{4,12},{5,13},{6,14},{7,15},{8,0},{9,1},... | collective-permute-start | bytes 2359304 | tf_op jit(solution)/shard_map/ppermute | solution.py:166
  115.4 34.4 %collective-permute-start.17 = (bf16[256,1536]{1,0:T(8,128)(2,1)S(1)}, bf16[256,1536]{1,0:T(8,128)(2,1)S(1)}, u32[]{:S(2)}, u32[]{:S(2)}) collective-permute-start(bf16[256,1536]{1,0:T(8,128)(2,1)S(1)} %add_convert_fusion.2), channel_id=1, source_target_pairs={{0,4},{1,5},{2,6},{3,7},{4,0},{5,1},{6,2},{7,3},{8,12},{9,13},{10,... | collective-permute-start | bytes 2359304 | tf_op jit(solution)/shard_map/ppermute | solution.py:166
  117.0 32.7 %collective-permute-start.19 = (bf16[256,1536]{1,0:T(8,128)(2,1)S(1)}, bf16[256,1536]{1,0:T(8,128)(2,1)S(1)}, u32[]{:S(2)}, u32[]{:S(2)}) collective-permute-start(bf16[256,1536]{1,0:T(8,128)(2,1)S(1)} %get-tuple-element.136), channel_id=1, source_target_pairs={{0,1},{1,0},{2,3},{3,2},{4,5},{5,4},{6,7},{7,6},{8,9},{9,8},{10,11... | collective-permute-start | bytes 2359304 | tf_op jit(solution)/shard_map/ppermute | solution.py:166
